TPU v7x, 32 devices: a whole 2x2x4 slice. The times are simulated.
32 devices in a mesh: seg: 8 (over z, y), rep: 4 (over x, core).
Axes of the slice: x: 2, y: 2, z: 4, core: 2. Of those that a mesh axis runs over, the one named last changes fastest.
Arguments:
- frames: bfloat16 [2, 4, 1024, 512], P(None, 'rep', 'seg'), may hold values from -6 to 6
- utt_segments: int32 [2, 4, 4], P(None, 'rep'), may hold values from 1 to 60, as said below
- out_grad: bfloat16 [2, 4, 1024, 512], P(None, 'rep', 'seg'), may hold values from -6 to 6
- qkv_weight: bfloat16 [2, 512, 1536], P(None, 'rep', 'seg'), may hold values from -0.25 to 0.25
- out_weight: bfloat16 [2, 512, 512], P(None, 'rep', 'seg'), may hold values from -0.75 to 0.75
- ffn_in_weight: bfloat16 [2, 512, 2048], P(None, 'rep', 'seg'), may hold values from -0.25 to 0.25
- ffn_out_weight: bfloat16 [2, 2048, 512], P(None, 'rep', 'seg'), may hold values from -0.125 to 0.125
- norm_gains: float32 [2, 2, 512], replicated, may hold values from 0.5 to 1.5
- biases: float32 [2, 6, 512], replicated, may hold values from -1 to 1
- ffn_bias: float32 [2, 2048], replicated, may hold values from -1 to 1
Outputs:
- encoded: float32 [2, 4, 1024, 512], P(None, 'rep', 'seg')
- frames_grad: float32 [2, 4, 1024, 512], P(None, 'rep', 'seg')
- grad_qkv: float32 [2, 512, 1536], P(None, 'rep', 'seg')
- grad_out_weight: float32 [2, 512, 512], P(None, 'rep', 'seg')
- grad_ffn_in: float32 [2, 512, 2048], P(None, 'rep', 'seg')
- grad_ffn_out: float32 [2, 2048, 512], P(None, 'rep', 'seg')
- grad_norm_gains: float32 [2, 2, 512], replicated
- grad_biases: float32 [2, 6, 512], replicated
- grad_ffn_bias: float32 [2, 2048], replicated
Inputs may be any that keep to these rules, and one draw needn't show every extreme that they name: `utt_segments`: A group's 4 entries are the segment counts of its utterances in time order and sum to 64; in every group one utterance holds the most.
All inputs are finite; a program needn't handle non-finite values.
Results may differ from a plain program's by a relative error of at most 0.019.
Values may be sent and summed in bfloat16 or wider, within the bound.
No kernel may reach another device: no remote copies, remote signals or barrier semaphores. Data moves between devices by JAX's collectives and lax.ppermute only.
A program may use at most 192 MiB of HBM per device.

v0:
```python
import jax
import jax.numpy as jnp
from jax import lax
from jax.experimental import pallas as pl
from jax.experimental.pallas import tpu as pltpu
from jax.sharding import PartitionSpec as P

HEADS = 8
SEG_LEN = 16
LEFT_LEN = 30
RIGHT_LEN = 4
MEM_LEN = 4
LAYERS = 2

EPS = 1e-05
ROOT_HALF = 0.7071067811865476
INV_ROOT_TWO_PI = 0.3989422804014327

LANES = 128
TILE = 16
RIGHT_ROWS = 16
LEFT_ROWS = 32
MEM_ROWS = 16
BACK_ROWS = LEFT_ROWS + MEM_ROWS
CHIPS_Z = 4
CHIPS_Y = 2
BLOCKS = CHIPS_Z * CHIPS_Y
SMALL_ROWS = 128
MIB = 1024 * 1024

BF16 = jnp.bfloat16
F32 = jnp.float32


def nn(a, b):
    return lax.dot_general(a, b, (((1,), (0,)), ((), ())), preferred_element_type=F32)


def nt(a, b):
    return lax.dot_general(a, b, (((1,), (1,)), ((), ())), preferred_element_type=F32)


def tn(a, b):
    return lax.dot_general(a, b, (((0,), (0,)), ((), ())), preferred_element_type=F32)


def col_sum(value):
    return jnp.sum(value, axis=0, keepdims=True)


def norm_forward(inputs, gain, bias):
    center = inputs - jnp.mean(inputs, axis=1, keepdims=True)
    inverse = lax.rsqrt(jnp.mean(center * center, axis=1, keepdims=True) + EPS)
    scaled = center * inverse
    return scaled * gain + bias, scaled, inverse


def norm_backward(grad_in, scaled, inverse, gain):
    grad_scaled = grad_in * gain
    return inverse * (
        grad_scaled
        - jnp.mean(grad_scaled, axis=1, keepdims=True)
        - scaled * jnp.mean(grad_scaled * scaled, axis=1, keepdims=True)
    )


def segment_mean(inputs):
    rows, width = inputs.shape
    return jnp.mean(inputs.reshape(rows // SEG_LEN, SEG_LEN, width), axis=1)


def segment_spread(rows, width, per_segment):
    segs = rows // SEG_LEN
    return jnp.broadcast_to(per_segment[:, None, :], (segs, SEG_LEN, width)).reshape(rows, width)


def identity(size):
    row = lax.broadcasted_iota(jnp.int32, (size, size), 0)
    col = lax.broadcasted_iota(jnp.int32, (size, size), 1)
    return (row == col).astype(F32).astype(BF16)


class Sizes:
    def __init__(self, rows, width, ff, with_summary):
        self.rows = rows
        self.width = width
        self.ff = ff
        self.segs = rows // SEG_LEN
        self.top = TILE if with_summary else 0
        self.keys = rows + RIGHT_ROWS + LEFT_ROWS + MEM_ROWS
        self.ext = self.top + self.keys
        self.queries = self.top + rows
        self.right_at = self.top + rows
        self.left_at = self.right_at + RIGHT_ROWS
        self.mem_at = self.left_at + LEFT_ROWS
        self.pairs = width // LANES


class Matrices:
    def __init__(self, width, ff):
        self.qkv = (CHIPS_Z, CHIPS_Y, 3 * width // BLOCKS, width)
        self.out = (CHIPS_Z, CHIPS_Y, width // BLOCKS, width)
        self.up = (CHIPS_Z, CHIPS_Y, ff // BLOCKS, width)
        self.down = (CHIPS_Z, CHIPS_Y, width // BLOCKS, ff)
        self.down_parts = ff // width
        self.attn_rows = self.qkv[2] + self.out[2]
        self.ffn_rows = self.up[2] + self.down_parts * self.down[2]


class Spots:
    def __init__(self, mats):
        high, wide, up, low = mats.qkv[2], mats.out[2], mats.up[2], mats.down[2]
        self.qkv = (0, 0)
        self.out = (0, high)
        self.up = (0, high + wide)
        self.down = [(0, high + wide + up + low * part) for part in range(mats.down_parts)]


def attn_pairs(mats, spots, groups, qkv_ref, out_ref, place_ref):
    if spots is None:
        return [(groups[0], qkv_ref), (groups[1], out_ref)]
    pairs = []
    for k in range(len(groups[0])):
        row = place_ref[2 + 2 * k]
        lane = pl.multiple_of(place_ref[3 + 2 * k], LANES)
        for (group, first), ref, shape in (
            (spots.qkv, qkv_ref, mats.qkv),
            (spots.out, out_ref, mats.out),
        ):
            block = groups[group][k]
            pairs.append(
                (
                    block.at[:, pl.ds(first, shape[2]), :],
                    ref.at[:, row, :, pl.ds(lane, LANES)],
                )
            )
    return pairs


def ffn_pairs(mats, spots, groups, up_ref, down_ref, place_ref):
    if spots is None:
        return [(groups[2], up_ref), (groups[3], down_ref)]
    pairs = []
    for k in range(len(groups[0])):
        row = place_ref[2 + 2 * k]
        lane = pl.multiple_of(place_ref[3 + 2 * k], LANES)
        group, first = spots.up
        block = groups[group][k]
        pairs.append(
            (block.at[:, pl.ds(first, mats.up[2]), :], up_ref.at[:, row, :, pl.ds(lane, LANES)])
        )
        for part, (group, first) in enumerate(spots.down):
            there = pl.multiple_of(
                place_ref[3 + 2 * k] * mats.down_parts + part * LANES, LANES
            )
            block = groups[group][k]
            pairs.append(
                (
                    block.at[:, pl.ds(first, mats.down[2]), :],
                    down_ref.at[:, row, :, pl.ds(there, LANES)],
                )
            )
    return pairs


def start_in(pairs, sems, at):
    copies = [pltpu.make_async_copy(s, d, sems.at[at + i]) for i, (s, d) in enumerate(pairs)]
    for copy in copies:
        copy.start()
    return copies


def start_out(pairs, sems, at):
    copies = [pltpu.make_async_copy(d, s, sems.at[at + i]) for i, (s, d) in enumerate(pairs)]
    for copy in copies:
        copy.start()
    return copies


def in_groups(spots, refs):
    return refs if spots is None else [refs]


def wait_all(copies):
    for copy in copies:
        copy.wait()


def fill_mask(sizes, seqs, starts_ref, place_ref, mask_ref):
    shape = (sizes.keys, 2 * sizes.queries)
    key = lax.broadcasted_iota(jnp.int32, shape, 0)
    col = lax.broadcasted_iota(jnp.int32, shape, 1)
    col = jnp.where(col < sizes.queries, col, col - sizes.queries)
    base = place_ref[0]
    total = place_ref[1]
    query = jnp.where(col < sizes.top, col, lax.shift_right_arithmetic(col - sizes.top, 4))
    left_at = sizes.rows + RIGHT_ROWS
    mem_at = left_at + LEFT_ROWS
    spot = jnp.where(key < left_at, key, key - mem_at)
    mem_seg = jnp.where(key < mem_at + sizes.segs, key - mem_at, key - mem_at - 2 * sizes.segs)
    key_seg = jnp.where(key < mem_at, lax.shift_right_arithmetic(spot, 4), mem_seg)
    near = (
        (key_seg == query)
        | ((spot >= query * SEG_LEN - LEFT_LEN) & (spot < query * SEG_LEN))
        | ((key_seg == query + 1) & (spot < query * SEG_LEN + SEG_LEN + RIGHT_LEN))
    )
    recent = (key_seg >= query - MEM_LEN) & (key_seg < query) & (col >= sizes.top)
    allowed = ((key < mem_at) & near) | ((key >= mem_at) & recent)
    key_abs = key_seg + base
    query_abs = query + base
    allowed = allowed & (key_abs >= 0) & (key_abs < total)
    if sizes.top:
        allowed = allowed & ((col < sizes.segs) | (col >= sizes.top))
    for n in range(seqs):
        key_owner = jnp.zeros(shape, jnp.int32)
        query_owner = jnp.zeros(shape, jnp.int32)
        for u in range(starts_ref.shape[1]):
            first = starts_ref[n, u]
            key_owner = key_owner + (key_abs >= first).astype(jnp.int32)
            query_owner = query_owner + (query_abs >= first).astype(jnp.int32)
        mask_ref[n] = jnp.where(allowed & (key_owner == query_owner), 0.0, -1e30)


def half_masks():
    lane = lax.broadcasted_iota(jnp.int32, (1, LANES), 1)
    even = (lane < LANES // 2).astype(F32)
    return even.astype(BF16), (1.0 - even).astype(BF16), lane < LANES // 2


def project(sizes, z_ref, qkv_ref, row_bias_ref, proj_ref):
    step = CHIPS_Z // 2
    for c in range(2):
        block = qkv_ref[pl.ds(c * step, step)].reshape(-1, sizes.width)
        wide = block.shape[0]
        made = nt(z_ref[...], block) + row_bias_ref[:, pl.ds(c * wide, wide)]
        proj_ref[:, pl.ds(c * wide, wide)] = made.astype(BF16)


def attend(sizes, seqs, proj_ref, mask_ref, probs_ref, att_ref):
    even, odd, is_even = half_masks()
    scale = (sizes.width // HEADS) ** (-0.5)
    count = sizes.queries

    def body(p, carry):
        for n in range(seqs):
            lane = pl.multiple_of(p * LANES, LANES)
            query = proj_ref[pl.ds(n * sizes.ext, count), pl.ds(lane, LANES)]
            first = n * sizes.ext + sizes.top
            key = proj_ref[pl.ds(first, sizes.keys), pl.ds(sizes.width + lane, LANES)]
            value = proj_ref[pl.ds(first, sizes.keys), pl.ds(2 * sizes.width + lane, LANES)]
            queries = jnp.concatenate([query * even, query * odd], axis=0)
            scores = nt(key, queries) * scale + mask_ref[n]
            scores = jnp.exp(scores - jnp.max(scores, axis=0, keepdims=True))
            probs = (scores * (1.0 / jnp.sum(scores, axis=0, keepdims=True))).astype(BF16)
            probs_ref[n * sizes.pairs + p] = probs
            out = tn(probs, value)
            att_ref[pl.ds(n * count, count), pl.ds(lane, LANES)] = jnp.where(
                is_even, out[:count], out[count:]
            ).astype(BF16)
        return carry

    lax.fori_loop(0, sizes.pairs, body, 0, unroll=True)


def attend_back(sizes, seqs, proj_ref, probs_ref, go_ref, gproj_ref):
    even, odd, is_even = half_masks()
    scale = (sizes.width // HEADS) ** (-0.5)
    count = sizes.queries
    wide = sizes.width
    for n in range(seqs):
        base = n * sizes.ext
        rest = sizes.ext - count
        gproj_ref[pl.ds(base + count, rest), pl.ds(0, wide)] = jnp.zeros((rest, wide), BF16)
        if sizes.top:
            gproj_ref[pl.ds(base, sizes.top), pl.ds(wide, 2 * wide)] = jnp.zeros(
                (sizes.top, 2 * wide), BF16
            )

    def body(p, carry):
        for n in range(seqs):
            lane = pl.multiple_of(p * LANES, LANES)
            base = n * sizes.ext
            first = base + sizes.top
            query = proj_ref[pl.ds(base, count), pl.ds(lane, LANES)]
            key = proj_ref[pl.ds(first, sizes.keys), pl.ds(wide + lane, LANES)]
            value = proj_ref[pl.ds(first, sizes.keys), pl.ds(2 * wide + lane, LANES)]
            grad = go_ref[pl.ds(n * count, count), pl.ds(lane, LANES)]
            queries = jnp.concatenate([query * even, query * odd], axis=0)
            grads = jnp.concatenate([grad * even, grad * odd], axis=0)
            probs_low = probs_ref[n * sizes.pairs + p]
            grad_values = nn(probs_low, grads)
            probs = probs_low.astype(F32)
            weighted = nt(value, grads) * probs
            grad_scores = (
                (weighted - probs * jnp.sum(weighted, axis=0, keepdims=True)) * scale
            ).astype(BF16)
            grad_keys = nn(grad_scores, queries)
            grad_both = tn(grad_scores, key)
            grad_query = jnp.where(is_even, grad_both[:count], grad_both[count:])
            gproj_ref[pl.ds(base, count), pl.ds(lane, LANES)] = grad_query.astype(BF16)
            gproj_ref[pl.ds(first, sizes.keys), pl.ds(wide + lane, LANES)] = grad_keys.astype(BF16)
            gproj_ref[pl.ds(first, sizes.keys), pl.ds(2 * wide + lane, LANES)] = (
                grad_values.astype(BF16)
            )
        return carry

    lax.fori_loop(0, sizes.pairs, body, 0)


def gelu_both(upward):
    half = 0.5 * (1.0 + lax.erf(upward * ROOT_HALF))
    slope = half + upward * jnp.exp(-0.5 * upward * upward) * INV_ROOT_TWO_PI
    return upward * half, slope


def up_block(up_ref, c, wide):
    step = wide // (up_ref.shape[1] * up_ref.shape[2])
    return up_ref[pl.ds(c * step, step)].reshape(-1, up_ref.shape[3])


def down_block(down_ref, c, wide):
    at = pl.multiple_of(c * wide, wide)
    return down_ref[:, :, :, pl.ds(at, wide)].reshape(-1, wide)


def ffn_back_step(
    sizes, c, wide, grad_low, hidden_low, active, slope, up_ref, down_ref, gup_ref, gdown_ref, vec
):
    at = pl.multiple_of(c * wide, wide)
    up = up_block(up_ref, c, wide)
    down = down_block(down_ref, c, wide)
    grad_active = nn(grad_low, down)
    grad_up_f = grad_active * slope
    grad_up = grad_up_f.astype(BF16)
    gdown_ref[:, :, :, pl.ds(at, wide)] = (
        tn(grad_low, active).astype(BF16).reshape(gdown_ref.shape[:3] + (wide,))
    )
    step = wide // (gup_ref.shape[1] * gup_ref.shape[2])
    gup_ref[pl.ds(c * step, step)] = (
        tn(grad_up, hidden_low).astype(BF16).reshape((step,) + gup_ref.shape[1:])
    )
    vec[pl.ds(8 + c, 1), :] = col_sum(grad_up.astype(F32))
    return nn(grad_up, up)


def attn_back_stage(
    sizes, seqs, gz, grad_mem_ref, att_ref, proj_ref, probs_ref, z_ref, qkv_ref, out_ref,
    gqkv_ref, gout_ref, go_ref, gproj_ref, branch_ref, vec, gh_ref, gmem_ref, back_left_ref,
    back_right_ref, scaled_rows=None,
):
    wide = sizes.width
    count = sizes.queries
    bias_out = col_sum(gz)
    for n in range(seqs):
        if sizes.top:
            mem_grad = grad_mem_ref[pl.ds(n * sizes.segs, sizes.segs), :]
            bias_out = bias_out + col_sum(mem_grad)
            branch_ref[pl.ds(n * count, sizes.top), :] = jnp.concatenate(
                [mem_grad, jnp.zeros((sizes.top - sizes.segs, wide), F32)], axis=0
            ).astype(BF16)
        branch_ref[pl.ds(n * count + sizes.top, sizes.rows), :] = gz[
            n * sizes.rows : (n + 1) * sizes.rows
        ].astype(BF16)
    vec[pl.ds(5, 1), :] = bias_out
    branch = branch_ref[...]
    gout_ref[...] = tn(branch, att_ref[...]).astype(BF16).reshape(gout_ref.shape)
    go_ref[...] = nn(branch, out_ref[...].reshape(-1, wide)).astype(BF16)
    attend_back(sizes, seqs, proj_ref, probs_ref, go_ref, gproj_ref)
    vec[pl.ds(3, 1), :] = col_sum(gproj_ref[:, pl.ds(0, wide)].astype(F32))
    vec[pl.ds(4, 1), :] = col_sum(gproj_ref[:, pl.ds(2 * wide, wide)].astype(F32))
    grad_ext = nn(gproj_ref[...], qkv_ref[...].reshape(-1, wide))
    gain_sum = jnp.zeros((1, wide), F32)
    bias_sum = jnp.zeros((1, wide), F32)
    for n in range(seqs):
        base = n * sizes.ext
        own = grad_ext[base + sizes.top : base + sizes.top + sizes.rows]
        if sizes.top:
            spread = grad_ext[base : base + sizes.segs] * (1.0 / SEG_LEN)
            own = own + segment_spread(sizes.rows, wide, spread)
        gh_ref[pl.ds(n * sizes.rows, sizes.rows), :] = own
        mem = base + sizes.mem_at
        gmem_ref[pl.ds(n * sizes.segs, sizes.segs), :] = grad_ext[mem : mem + sizes.segs]
        left = base + sizes.left_at
        back_left_ref[n] = grad_ext[left : left + BACK_ROWS].astype(BF16)
        right = base + sizes.right_at
        back_right_ref[n] = grad_ext[right : right + RIGHT_ROWS].astype(BF16)
        if scaled_rows is not None:
            grads = (
                own,
                grad_ext[right : right + RIGHT_ROWS],
                grad_ext[left : left + LEFT_ROWS],
            )
            for rows, scaled in zip(grads, scaled_rows(n)):
                gain_sum = gain_sum + col_sum(rows * scaled)
                bias_sum = bias_sum + col_sum(rows)
    if scaled_rows is not None:
        vec[pl.ds(0, 1), :] = gain_sum
        vec[pl.ds(2, 1), :] = bias_sum
    step = CHIPS_Z // 2
    part = gqkv_ref.shape[1] * gqkv_ref.shape[2] * step
    for c in range(2):
        gqkv_ref[pl.ds(c * step, step)] = (
            tn(gproj_ref[:, pl.ds(c * part, part)], z_ref[...])
            .astype(BF16)
            .reshape((step,) + gqkv_ref.shape[1:])
        )


def merge_halo(sizes, n, gh_ref, gmem_ref, from_right_ref, from_left_ref):
    first = n * sizes.rows
    back = from_right_ref[n].astype(F32)
    head = gh_ref[pl.ds(first, RIGHT_ROWS), :] + from_left_ref[n].astype(F32)
    middle = gh_ref[pl.ds(first + RIGHT_ROWS, sizes.rows - RIGHT_ROWS - LEFT_ROWS), :]
    tail = gh_ref[pl.ds(first + sizes.rows - LEFT_ROWS, LEFT_ROWS), :] + back[:LEFT_ROWS]
    mem = gmem_ref[pl.ds(n * sizes.segs, sizes.segs), :] + back[LEFT_ROWS + sizes.segs :]
    return jnp.concatenate([head, middle, tail], axis=0), mem


def pack_kernel(spots, qkv_ref, out_ref, up_ref, down_ref, *packed):
    eye = identity(LANES)
    high, wide, low = qkv_ref.shape[1], out_ref.shape[1], down_ref.shape[1]
    for layer, ref in enumerate(packed):
        up = tn(up_ref[layer], eye).astype(BF16)
        for z in range(ref.shape[0]):
            ref[z, pl.ds(spots.qkv[1], high), :] = qkv_ref[layer]
            ref[z, pl.ds(spots.out[1], wide), :] = out_ref[layer]
            ref[z, pl.ds(spots.up[1], up_ref.shape[2]), :] = up
            for part, (_, first) in enumerate(spots.down):
                ref[z, pl.ds(first, low), :] = down_ref[layer, :, pl.ds(part * LANES, LANES)]


def unpack_layer(spots, sources, refs):
    qkv_ref, out_ref, up_ref, down_ref = refs
    high, wide, low = qkv_ref.shape[0], out_ref.shape[0], down_ref.shape[0]

    def total(first, rows):
        parts = [ref[z, pl.ds(first, rows), :] for ref in sources for z in range(ref.shape[0])]
        value = parts[0].astype(F32)
        for part in parts[1:]:
            value = value + part.astype(F32)
        return value

    qkv_ref[...] = total(spots.qkv[1], high)
    out_ref[...] = total(spots.out[1], wide)
    up_ref[...] = nt(identity(LANES), total(spots.up[1], up_ref.shape[1]).astype(BF16))
    for part, (_, first) in enumerate(spots.down):
        down_ref[:, pl.ds(part * LANES, LANES)] = total(first, low)
    return total


def store_layer(layer, held, outs, sems):
    copies = [
        pltpu.make_async_copy(ref, out.at[layer], sems.at[i])
        for i, (ref, out) in enumerate(zip(held, outs))
    ]
    for copy in copies:
        copy.start()
    return copies


def unpack_last_kernel(spots, layer, lines_ref, first_ref, *refs):
    outs, held, sems = refs[:4], refs[4:8], refs[8]
    unpack_layer(spots, (lines_ref, first_ref), held)
    wait_all(store_layer(layer, held, outs, sems))


def unpack_first_kernel(spots, small_at, parts_ref, *refs):
    outs, (gains_ref, biases_ref, ffn_bias_ref), held, sems = (
        refs[4:8], refs[8:11], refs[11:15], refs[15],
    )
    total = unpack_layer(spots, (parts_ref,), held)
    copies = store_layer(0, held, outs, sems)
    sums = total(small_at, SMALL_ROWS)
    parts = gains_ref.shape[2] // LANES
    for layer in range(gains_ref.shape[0]):
        for part in range(parts):
            lanes = pl.ds(part * LANES, LANES)
            block = sums[(layer * parts + part) * TILE : (layer * parts + part + 1) * TILE]
            gains_ref[layer, :, lanes] = block[0:2]
            for row in range(biases_ref.shape[0]):
                biases_ref[row, pl.ds(layer, 1), lanes] = block[2 + row : 3 + row]
            for row in range(ffn_bias_ref.shape[1] // gains_ref.shape[2]):
                at = row * gains_ref.shape[2] + part * LANES
                ffn_bias_ref[pl.ds(layer, 1), pl.ds(at, LANES)] = block[8 + row : 9 + row]
    wait_all(copies)


def first_layer_kernel(
    sizes, seqs, mats, spots, count_in, place_ref, starts_ref, frames_ref, left_ref, right_ref,
    gains_ref, biases_ref, ffn_bias_ref, row_bias_ref, *refs
):
    groups = in_groups(spots, refs[:count_in])
    (
        z_ref, proj_ref, probs_ref, att_ref, mixed_ref, mem_ref, next_ref, active_ref, slope_ref,
        low_ref, send_right_ref, send_left_ref, qkv_ref, out_ref, up_ref, down_ref, mask_ref,
        hidden_ref, sems,
    ) = refs[count_in:]
    wide = sizes.width
    copies = start_in(attn_pairs(mats, spots, groups, qkv_ref, out_ref, place_ref), sems, 0)
    ffn_copies = start_in(
        ffn_pairs(mats, spots, groups, up_ref, down_ref, place_ref), sems, len(copies)
    )
    gain = gains_ref[0, pl.ds(0, 1), :]
    bias = biases_ref[0, pl.ds(0, 1), :]
    pad = jnp.zeros((TILE - sizes.segs, wide), F32)
    for n in range(seqs):
        own = frames_ref[n].astype(F32)
        before = left_ref[n].astype(F32)
        hidden = norm_forward(own, gain, bias)[0]
        halo = norm_forward(before[before.shape[0] - LEFT_ROWS :], gain, bias)[0]
        after = norm_forward(right_ref[n].astype(F32), gain, bias)[0]
        memory = jnp.concatenate(
            [
                segment_mean(own),
                jnp.zeros((sizes.segs - before.shape[0] // SEG_LEN, wide), F32),
                segment_mean(before),
            ],
            axis=0,
        )
        base = n * sizes.ext
        z_ref[pl.ds(base, sizes.top), :] = jnp.concatenate(
            [segment_mean(hidden), pad], axis=0
        ).astype(BF16)
        z_ref[pl.ds(base + sizes.top, sizes.rows), :] = hidden.astype(BF16)
        z_ref[pl.ds(base + sizes.right_at, RIGHT_ROWS), :] = after.astype(BF16)
        z_ref[pl.ds(base + sizes.left_at, LEFT_ROWS), :] = halo.astype(BF16)
        z_ref[pl.ds(base + sizes.mem_at, MEM_ROWS), :] = memory.astype(BF16)
    fill_mask(sizes, seqs, starts_ref, place_ref, mask_ref)
    wait_all(copies)
    project(sizes, z_ref, qkv_ref, row_bias_ref, proj_ref)
    attend(sizes, seqs, proj_ref, mask_ref, probs_ref, att_ref)
    mixed = nt(att_ref[...], out_ref[...].reshape(-1, wide)) + biases_ref[3, pl.ds(0, 1), :]
    for n in range(seqs):
        base = n * sizes.queries
        mem_ref[pl.ds(n * sizes.segs, sizes.segs), :] = mixed[base : base + sizes.segs]
        mixed_ref[pl.ds(n * sizes.rows, sizes.rows), :] = (
            frames_ref[n].astype(F32) + mixed[base + sizes.top : base + sizes.top + sizes.rows]
        )
    mixed = mixed_ref[...]
    hidden, _, _ = norm_forward(mixed, gains_ref[0, pl.ds(1, 1), :], biases_ref[4, pl.ds(0, 1), :])
    hidden_ref[...] = hidden.astype(BF16)
    next_ref[...] = mixed + biases_ref[5, pl.ds(0, 1), :]
    wait_all(ffn_copies)

    def body(c, carry):
        at_lane = pl.multiple_of(c * wide, wide)
        upward = nt(hidden_ref[...], up_block(up_ref, c, wide))
        upward = upward + ffn_bias_ref[pl.ds(0, 1), pl.ds(at_lane, wide)]
        active, slope = gelu_both(upward)
        active = active.astype(BF16)
        active_ref[:, pl.ds(at_lane, wide)] = active
        slope_ref[:, pl.ds(at_lane, wide)] = slope.astype(BF16)
        next_ref[...] += nt(active, down_block(down_ref, c, wide))
        return carry

    lax.fori_loop(0, sizes.ff // wide, body, 0)
    low, _, _ = norm_forward(
        next_ref[...], gains_ref[1, pl.ds(0, 1), :], biases_ref[0, pl.ds(1, 1), :]
    )
    low = low.astype(BF16)
    low_ref[...] = low
    for n in range(seqs):
        base = n * sizes.rows
        send_right_ref[n, pl.ds(0, LEFT_ROWS), :] = low[
            base + sizes.rows - LEFT_ROWS : base + sizes.rows
        ]
        send_right_ref[n, pl.ds(LEFT_ROWS, MEM_ROWS), :] = jnp.concatenate(
            [
                mem_ref[pl.ds(n * sizes.segs, sizes.segs), :],
                jnp.zeros((MEM_ROWS - sizes.segs, wide), F32),
            ],
            axis=0,
        ).astype(BF16)
        send_left_ref[n] = low[base : base + RIGHT_ROWS]


def last_layer_kernel(
    sizes, seqs, mats, spots, count_in, count_out, place_ref, starts_ref, low_ref, left_ref,
    right_ref, mem_ref, inputs_ref, out_grad_ref, gains_ref, biases_ref, ffn_bias_ref,
    row_bias_ref, *refs
):
    groups = in_groups(spots, refs[:count_in])
    (encoded_ref, gz_ref, gh_ref, gmem_ref, back_left_ref, back_right_ref, vec) = refs[
        count_in : count_in + 7
    ]
    hbm_out = refs[count_in + 7 : count_in + 7 + count_out]
    (
        qkv_ref, out_ref, up_ref, down_ref, gqkv_ref, gout_ref, gup_ref, gdown_ref, mask_ref,
        z_ref, proj_ref, probs_ref, att_ref, hidden_ref, go_ref, gproj_ref, branch_ref,
        grad_low_ref, grad_hidden_ref, sems,
    ) = refs[count_in + 7 + count_out :]
    outs_to = hbm_out
    if spots is not None:
        rows = mats.attn_rows + mats.ffn_rows
        outs_to = [
            [
                ref.at[hop2, :, pl.ds(hop1 * rows, rows), :]
                for ref in hbm_out
                for hop2 in range(2)
                for hop1 in range(2)
            ]
        ]
    wide = sizes.width
    attn_copies = start_in(attn_pairs(mats, spots, groups, qkv_ref, out_ref, place_ref), sems, 0)
    ffn_copies = start_in(
        ffn_pairs(mats, spots, groups, up_ref, down_ref, place_ref), sems, len(attn_copies)
    )
    vec[...] = jnp.zeros_like(vec)
    for n in range(seqs):
        base = n * sizes.ext
        z_ref[pl.ds(base, sizes.rows), :] = low_ref[pl.ds(n * sizes.rows, sizes.rows), :]
        z_ref[pl.ds(base + sizes.right_at, RIGHT_ROWS), :] = right_ref[n]
        z_ref[pl.ds(base + sizes.left_at, LEFT_ROWS), :] = left_ref[n, pl.ds(0, LEFT_ROWS), :]
        memory = jnp.concatenate(
            [
                mem_ref[pl.ds(n * sizes.segs, sizes.segs), :],
                left_ref[n, pl.ds(LEFT_ROWS, MEM_ROWS), :].astype(F32)[: sizes.segs],
            ],
            axis=0,
        )
        z_ref[pl.ds(base + sizes.mem_at, MEM_ROWS), :] = memory.astype(BF16)
        grad_low_ref[pl.ds(n * sizes.rows, sizes.rows), :] = out_grad_ref[n]
    fill_mask(sizes, seqs, starts_ref, place_ref, mask_ref)
    wait_all(attn_copies)
    project(sizes, z_ref, qkv_ref, row_bias_ref, proj_ref)
    attend(sizes, seqs, proj_ref, mask_ref, probs_ref, att_ref)
    mixed = (
        inputs_ref[...]
        + nt(att_ref[...], out_ref[...].reshape(-1, wide))
        + biases_ref[3, pl.ds(1, 1), :]
    )
    gain = gains_ref[1, pl.ds(1, 1), :]
    hidden, scaled, inverse = norm_forward(mixed, gain, biases_ref[4, pl.ds(1, 1), :])
    hidden_ref[...] = hidden.astype(BF16)
    for n in range(seqs):
        encoded_ref[n] = mixed[n * sizes.rows : (n + 1) * sizes.rows] + biases_ref[5, pl.ds(1, 1), :]
    grad_hidden_ref[...] = jnp.zeros_like(grad_hidden_ref)
    wait_all(ffn_copies)

    def body(c, carry):
        at_lane = pl.multiple_of(c * wide, wide)
        upward = nt(hidden_ref[...], up_block(up_ref, c, wide))
        upward = upward + ffn_bias_ref[pl.ds(1, 1), pl.ds(at_lane, wide)]
        active, slope = gelu_both(upward)
        active = active.astype(BF16)
        made = nt(active, down_block(down_ref, c, wide))
        for n in range(seqs):
            encoded_ref[n] += made[n * sizes.rows : (n + 1) * sizes.rows]
        grad_hidden_ref[...] += ffn_back_step(
            sizes, c, wide, grad_low_ref[...], hidden_ref[...], active, slope, up_ref, down_ref,
            gup_ref, gdown_ref, vec,
        )
        return carry

    lax.fori_loop(0, sizes.ff // wide, body, 0)
    out_at = len(attn_copies) + len(ffn_copies)
    outs = start_out(
        ffn_pairs(mats, spots, outs_to, gup_ref, gdown_ref, place_ref), sems, out_at
    )
    grad = grad_low_ref[...].astype(F32)
    grad_hidden = grad_hidden_ref[...]
    vec[pl.ds(1, 1), :] = col_sum(grad_hidden * scaled)
    vec[pl.ds(6, 1), :] = col_sum(grad_hidden)
    vec[pl.ds(7, 1), :] = col_sum(grad)
    gz = grad + norm_backward(grad_hidden, scaled, inverse, gain)
    gz_ref[...] = gz
    attn_back_stage(
        sizes, seqs, gz, None, att_ref, proj_ref, probs_ref, z_ref, qkv_ref, out_ref, gqkv_ref,
        gout_ref, go_ref, gproj_ref, branch_ref, vec, gh_ref, gmem_ref, back_left_ref,
        back_right_ref,
    )
    outs = outs + start_out(
        attn_pairs(mats, spots, outs_to, gqkv_ref, gout_ref, place_ref),
        sems,
        out_at + len(outs),
    )
    wait_all(outs)


def first_back_kernel(
    last, sizes, seqs, mats, spots, count_in, count_out, place_ref, inputs_ref, gz_in_ref,
    gh_in_ref, gmem_in_ref, from_right_ref, from_left_ref, mixed_ref, active_ref, slope_ref,
    att_ref, probs_ref, proj_ref, z_ref, frames_ref, left_ref, right_ref, gains_ref, biases_ref,
    last_vec, *refs
):
    groups = in_groups(spots, refs[:count_in])
    gz_ref, gh_ref, gmem_ref, back_left_ref, back_right_ref, upper_vec, vec = refs[
        count_in : count_in + 7
    ]
    refs = refs[count_in + 7 :]
    hbm_out = refs[:count_out]
    (
        qkv_ref, out_ref, up_ref, down_ref, gqkv_ref, gout_ref, gup_ref, gdown_ref, hidden_ref,
        grad_low_ref, grad_ref, grad_hidden_ref, grad_mem_ref, go_ref, gproj_ref, branch_ref,
        small_ref, sems,
    ) = refs[count_out:]
    wide = sizes.width
    small = []
    outs_to = hbm_out
    if spots is not None:
        rows = mats.attn_rows + mats.ffn_rows
        end = CHIPS_Z * rows
        each = [
            ref.at[hop2, hop1] for ref in hbm_out for hop2 in range(2) for hop1 in range(2)
        ]
        small = [ref.at[pl.ds(end, SMALL_ROWS), :] for ref in each]
        outs_to = [[ref.at[pl.ds(0, end), :].reshape(CHIPS_Z, rows, LANES) for ref in each]]
    ffn_copies = start_in(ffn_pairs(mats, spots, groups, up_ref, down_ref, place_ref), sems, 0)
    attn_copies = start_in(
        attn_pairs(mats, spots, groups, qkv_ref, out_ref, place_ref), sems, len(ffn_copies)
    )
    vec[...] = jnp.zeros_like(vec)
    upper_vec[...] = jnp.zeros_like(upper_vec)
    gain = gains_ref[1, pl.ds(0, 1), :]
    gain_sum = jnp.zeros((1, wide), F32)
    bias_sum = jnp.zeros((1, wide), F32)
    for n in range(seqs):
        rows = pl.ds(n * sizes.rows, sizes.rows)
        _, scaled, inverse = norm_forward(
            inputs_ref[rows, :], gain, biases_ref[0, pl.ds(1, 1), :]
        )
        total, mem = merge_halo(last, n, gh_in_ref, gmem_in_ref, from_right_ref, from_left_ref)
        gain_sum = gain_sum + col_sum(total * scaled)
        bias_sum = bias_sum + col_sum(total)
        grad = gz_in_ref[rows, :] + norm_backward(total, scaled, inverse, gain)
        grad_ref[rows, :] = grad
        grad_low_ref[rows, :] = grad.astype(BF16)
        grad_mem_ref[pl.ds(n * sizes.segs, sizes.segs), :] = mem
    upper_vec[pl.ds(0, 1), :] = gain_sum
    upper_vec[pl.ds(2, 1), :] = bias_sum
    gain = gains_ref[0, pl.ds(1, 1), :]
    hidden, scaled, inverse = norm_forward(
        mixed_ref[...], gain, biases_ref[4, pl.ds(0, 1), :]
    )
    hidden_ref[...] = hidden.astype(BF16)
    grad_hidden_ref[...] = jnp.zeros_like(grad_hidden_ref)
    wait_all(ffn_copies)

    def body(c, carry):
        at_lane = pl.multiple_of(c * wide, wide)
        grad_hidden_ref[...] += ffn_back_step(
            sizes, c, wide, grad_low_ref[...], hidden_ref[...],
            active_ref[:, pl.ds(at_lane, wide)], slope_ref[:, pl.ds(at_lane, wide)].astype(F32),
            up_ref, down_ref, gup_ref, gdown_ref, vec,
        )
        return carry

    lax.fori_loop(0, sizes.ff // wide, body, 0)
    out_at = len(ffn_copies) + len(attn_copies)
    outs = start_out(
        ffn_pairs(mats, spots, outs_to, gup_ref, gdown_ref, place_ref), sems, out_at
    )
    grad_hidden = grad_hidden_ref[...]
    grad = grad_ref[...]
    vec[pl.ds(1, 1), :] = col_sum(grad_hidden * scaled)
    vec[pl.ds(6, 1), :] = col_sum(grad_hidden)
    vec[pl.ds(7, 1), :] = col_sum(grad)
    gz = grad + norm_backward(grad_hidden, scaled, inverse, gain)
    gz_ref[...] = gz

    def scaled_rows(n):
        before = left_ref[n, pl.ds(left_ref.shape[1] - LEFT_ROWS, LEFT_ROWS), :]
        parts = (frames_ref[n], right_ref[n], before)
        first_gain = gains_ref[0, pl.ds(0, 1), :]
        first_bias = biases_ref[0, pl.ds(0, 1), :]
        return [norm_forward(part.astype(F32), first_gain, first_bias)[1] for part in parts]

    wait_all(attn_copies)
    attn_back_stage(
        sizes, seqs, gz, grad_mem_ref, att_ref, proj_ref, probs_ref, z_ref, qkv_ref, out_ref,
        gqkv_ref, gout_ref, go_ref, gproj_ref, branch_ref, vec, gh_ref, gmem_ref, back_left_ref,
        back_right_ref, scaled_rows,
    )
    outs = outs + start_out(
        attn_pairs(mats, spots, outs_to, gqkv_ref, gout_ref, place_ref),
        sems,
        out_at + len(outs),
    )
    parts = sizes.width // LANES
    for layer, total in enumerate((vec[...], last_vec[...] + upper_vec[...])):
        for part in range(parts):
            small_ref[pl.ds((layer * parts + part) * TILE, TILE), :] = total[
                :, part * LANES : (part + 1) * LANES
            ].astype(BF16)
    outs = outs + start_out([(ref, small_ref) for ref in small], sems, out_at + len(outs))
    wait_all(outs)


def frames_grad_kernel(
    sizes, seqs, frames_ref, gz_ref, gh_ref, gmem_ref, from_right_ref, from_left_ref, gains_ref,
    biases_ref, grad_ref
):
    gain = gains_ref[0, pl.ds(0, 1), :]
    for n in range(seqs):
        _, scaled, inverse = norm_forward(
            frames_ref[n].astype(F32), gain, biases_ref[0, pl.ds(0, 1), :]
        )
        total, mem = merge_halo(sizes, n, gh_ref, gmem_ref, from_right_ref, from_left_ref)
        grad_ref[n] = (
            gz_ref[pl.ds(n * sizes.rows, sizes.rows), :]
            + norm_backward(total, scaled, inverse, gain)
            + segment_spread(sizes.rows, sizes.width, mem * (1.0 / SEG_LEN))
        )


def shifted(value, axis, by):
    size = lax.axis_size(axis)
    return lax.ppermute(value, axis, [(i, (i + by) % size) for i in range(size)])


def permuted(value, move):
    reps = lax.axis_size("rep")
    pairs = []
    for flat in range(lax.axis_size("seg") * reps):
        seg, rep = divmod(flat, reps)
        z, y, x, core = move(seg // CHIPS_Y, seg % CHIPS_Y, rep // 2, rep % 2)
        pairs.append((flat, (z * CHIPS_Y + y) * reps + 2 * x + core))
    return lax.ppermute(value, ("seg", "rep"), pairs)


def across_first(value):
    return permuted(value, lambda z, y, x, c: (z, y, x ^ 1, c) if c == 0 else (z, y ^ 1, x, c))


def across_second(value):
    return permuted(value, lambda z, y, x, c: (z, y ^ 1, x, c) if c == 0 else (z, y, x ^ 1, c))


def other_core(value):
    return permuted(value, lambda z, y, x, c: (z, y, x, c ^ 1))


def after(value, *others):
    return lax.optimization_barrier((value,) + others)[0]


def swap_z(blocks):
    groups = [
        [z * CHIPS_Y + y for z in range(CHIPS_Z)] for y in range(CHIPS_Y)
    ]
    return lax.all_to_all(blocks, "seg", 0, 0, axis_index_groups=groups, tiled=True)


def gather_sides(here):
    return [here, across_first(here), across_second(here)]


def both_cores(blocks):
    return blocks + [other_core(block) for block in blocks]


def summed(*parts):
    total = parts[0].astype(F32)
    for part in parts[1:]:
        total = total + part.astype(F32)
    return total.astype(BF16)


def sum_everywhere(value):
    count = lax.axis_size("seg") * lax.axis_size("rep")
    bit = 1
    while bit < count:
        value = value + lax.ppermute(value, ("seg", "rep"), [(i, i ^ bit) for i in range(count)])
        bit *= 2
    return value


def vmem_spec():
    return pl.BlockSpec(memory_space=pltpu.VMEM)


def smem_spec():
    return pl.BlockSpec(memory_space=pltpu.SMEM)


def hbm_spec():
    return pl.BlockSpec(memory_space=pl.ANY)


def call(body, in_specs, out_shapes, out_specs, scratch, args, flops=0, moved=0, grid=(), aliases={}, vmem=12):
    return pl.pallas_call(
        body,
        grid=grid,
        input_output_aliases=aliases,
        in_specs=in_specs,
        out_shape=tuple(jax.ShapeDtypeStruct(shape, kind) for shape, kind in out_shapes),
        out_specs=tuple(out_specs),
        scratch_shapes=scratch,
        compiler_params=pltpu.CompilerParams(vmem_limit_bytes=vmem * MIB),
        cost_estimate=pl.CostEstimate(flops=flops, bytes_accessed=moved, transcendentals=0),
    )(*args)


def on_device(
    frames,
    utt_segments,
    out_grad,
    qkv_weight,
    out_weight,
    ffn_in_weight,
    ffn_out_weight,
    norm_gains,
    biases,
    ffn_bias,
):
    micros, groups, rows, width = frames.shape
    seqs = micros * groups
    ff = ffn_bias.shape[1]
    reps = lax.axis_size("rep")
    seg_count = lax.axis_size("seg")
    mats = Matrices(width, ff)
    by_blocks = width // reps == LANES and reps == 4 and seg_count == BLOCKS
    first = Sizes(rows, width, ff, True)
    last = Sizes(rows, width, ff, False)
    own = seqs * rows
    mem_own = seqs * first.segs

    seg_at = lax.axis_index("seg")
    seg_base = seg_at * first.segs
    rep_at = lax.axis_index("rep")
    place = [seg_base, jnp.int32(first.segs * seg_count)]
    y_at, x_at, core_at = seg_at % CHIPS_Y, rep_at // 2, rep_at % 2
    for other in range(2):
        core = lax.bitwise_xor(core_at, other)
        for hop2 in range(2):
            for hop1 in range(2):
                x_hop = jnp.where(core == 0, hop1, hop2)
                y_hop = jnp.where(core == 0, hop2, hop1)
                place.append(lax.bitwise_xor(y_at, y_hop))
                place.append((lax.bitwise_xor(x_at, x_hop) * 2 + core) * LANES)
    place = jnp.stack([jnp.asarray(entry, jnp.int32) for entry in place])
    lengths = utt_segments.reshape(seqs, utt_segments.shape[2])
    starts = (jnp.cumsum(lengths, axis=1) - lengths).astype(jnp.int32)
    zero_bias = jnp.zeros((1, width), F32)
    row_biases = [
        jnp.concatenate([biases[l : l + 1, 1], zero_bias, biases[l : l + 1, 2]], axis=1)
        for l in range(LAYERS)
    ]
    biases_by_row = jnp.swapaxes(biases, 0, 1)

    frames_own = frames.reshape(seqs, rows, width)
    grads_own = out_grad.reshape(seqs, rows, width)
    far = MEM_LEN * SEG_LEN
    frames_left = shifted(frames_own[:, rows - far :], "seg", 1)
    frames_right = shifted(frames_own[:, :RIGHT_ROWS], "seg", -1)

    attn_rows, ffn_rows = mats.attn_rows, mats.ffn_rows
    if by_blocks:
        qkv_t, out_t, down_t = (
            jnp.swapaxes(member, 1, 2) for member in (qkv_weight, out_weight, ffn_out_weight)
        )
        all_rows = attn_rows + ffn_rows
        spots = Spots(mats)
        shards = call(
            lambda *refs: pack_kernel(spots, *refs),
            [vmem_spec()] * 4,
            [((CHIPS_Z, all_rows, LANES), BF16)] * LAYERS,
            [vmem_spec()] * LAYERS,
            [],
            (qkv_t, out_t, ffn_in_weight, down_t),
            vmem=56,
        )
        sides0 = gather_sides(after(swap_z(shards[0]), frames_left, frames_right))
        place, starts, row_biases, sent = lax.optimization_barrier(
            (place, starts, row_biases, after(shards[1], sides0[0]))
        )
        sides1 = gather_sides(swap_z(sent))
        first_all = both_cores(sides0 + [across_second(after(sides0[1], sides1[0]))])
        classes = len(first_all) // 2
        grad_outs0 = [((2, 2, CHIPS_Z * all_rows + SMALL_ROWS, LANES), BF16)] * 2
        grad_outs1 = [((2, CHIPS_Z, 2 * all_rows, LANES), BF16)] * 2
        copies_in = len(first_all) * (3 + mats.down_parts)
    else:
        whole = []
        for member, shape in zip(
            (qkv_weight, out_weight, ffn_in_weight, ffn_out_weight),
            (mats.qkv, mats.out, mats.up, mats.down),
        ):
            member = lax.all_gather(member, "rep", axis=1, tiled=True)
            member = lax.all_gather(member, "seg", axis=2, tiled=True)
            whole.append(jnp.swapaxes(member, 1, 2).reshape((LAYERS,) + shape))
        first_all = [member[0] for member in whole]
        last_all = [member[1] for member in whole]
        spots = None
        grad_outs0 = grad_outs1 = [
            (shape, BF16) for shape in (mats.qkv, mats.out, mats.up, mats.down)
        ]
        copies_in = 4
    dma = pltpu.SemaphoreType.DMA

    matrices = [pltpu.VMEM(shape, BF16) for shape in (mats.qkv, mats.out, mats.up, mats.down)]

    (
        z0, proj0, probs0, att0, mixed0, mem1, x1, active0, slope0, low1, send_right, send_left,
    ) = call(
        lambda *refs: first_layer_kernel(
            first, seqs, mats, spots, len(first_all), *refs
        ),
        [smem_spec()] * 2 + [vmem_spec()] * 7 + [hbm_spec()] * len(first_all),
        [
            ((seqs * first.ext, width), BF16),
            ((seqs * first.ext, 3 * width), BF16),
            ((seqs * first.pairs, first.keys, 2 * first.queries), BF16),
            ((seqs * first.queries, width), BF16),
            ((own, width), F32),
            ((mem_own, width), F32),
            ((own, width), F32),
            ((own, ff), BF16),
            ((own, ff), BF16),
            ((own, width), BF16),
            ((seqs, BACK_ROWS, width), BF16),
            ((seqs, RIGHT_ROWS, width), BF16),
        ],
        [vmem_spec()] * 12,
        matrices
        + [
            pltpu.VMEM((seqs, first.keys, 2 * first.queries), F32),
            pltpu.VMEM((own, width), BF16),
            dma((copies_in,)),
        ],
        (place, starts, frames_own, frames_left, frames_right, norm_gains, biases_by_row, ffn_bias,
         row_biases[0]) + tuple(first_all),
        flops=24 * own * (4 * width * width + 2 * width * ff) // 2,
        moved=2 * (4 * width * width + 2 * width * ff),
        vmem=24,
    )
    left1 = shifted(send_right, "seg", 1)
    right1 = shifted(send_left, "seg", -1)
    if by_blocks:
        last_side = across_second(after(sides1[1], sides1[2], left1, right1))
        last_all = both_cores(sides1 + [last_side])

    vec_shape = (TILE, width)
    outs = call(
        lambda *refs: last_layer_kernel(
            last, seqs, mats, spots, len(last_all), len(grad_outs1), *refs
        ),
        [smem_spec()] * 2 + [vmem_spec()] * 10 + [hbm_spec()] * len(last_all),
        [
            ((seqs, rows, width), F32),
            ((own, width), F32),
            ((own, width), F32),
            ((mem_own, width), F32),
            ((seqs, BACK_ROWS, width), BF16),
            ((seqs, RIGHT_ROWS, width), BF16),
            (vec_shape, F32),
        ]
        + grad_outs1,
        [vmem_spec()] * 7 + [hbm_spec()] * len(grad_outs1),
        matrices
        + matrices
        + [
            pltpu.VMEM((seqs, last.keys, 2 * last.queries), F32),
            pltpu.VMEM((seqs * last.ext, width), BF16),
            pltpu.VMEM((seqs * last.ext, 3 * width), BF16),
            pltpu.VMEM((seqs * last.pairs, last.keys, 2 * last.queries), BF16),
            pltpu.VMEM((seqs * last.queries, width), BF16),
            pltpu.VMEM((own, width), BF16),
            pltpu.VMEM((seqs * last.queries, width), BF16),
            pltpu.VMEM((seqs * last.ext, 3 * width), BF16),
            pltpu.VMEM((seqs * last.queries, width), BF16),
            pltpu.VMEM((own, width), BF16),
            pltpu.VMEM((own, width), F32),
            dma((2 * copies_in,)),
        ],
        (place, starts, low1, left1, right1, mem1, x1, grads_own, norm_gains, biases_by_row, ffn_bias,
         row_biases[1]) + tuple(last_all),
        flops=30 * own * (4 * width * width + 2 * width * ff),
        moved=4 * (4 * width * width + 2 * width * ff),
        vmem=34,
    )
    encoded, gz1, gh1, gmem1, back_left1, back_right1, vec1 = outs[:7]
    grad_blocks1 = outs[7:]
    from_right1 = shifted(back_left1, "seg", -1)
    from_left1 = shifted(back_right1, "seg", 1)

    gh1_tied = gh1
    if by_blocks:
        mine1, theirs1 = grad_blocks1[0], other_core(grad_blocks1[1])
        far1 = summed(mine1[1], theirs1[1])
        gh1_tied = after(gh1, far1)
    gz0, gh0, gmem0, back_left0, back_right0, upper_vec, vec0, *grad_blocks0 = call(
        lambda *refs: first_back_kernel(
            last, first, seqs, mats, spots, len(first_all), len(grad_outs0), *refs
        ),
        [smem_spec()] + [vmem_spec()] * 19 + [hbm_spec()] * len(first_all),
        [
            ((own, width), F32),
            ((own, width), F32),
            ((mem_own, width), F32),
            ((seqs, BACK_ROWS, width), BF16),
            ((seqs, RIGHT_ROWS, width), BF16),
            (vec_shape, F32),
            (vec_shape, F32),
        ]
        + grad_outs0,
        [vmem_spec()] * 7 + [hbm_spec()] * len(grad_outs0),
        matrices
        + matrices
        + [
            pltpu.VMEM((own, width), BF16),
            pltpu.VMEM((own, width), BF16),
            pltpu.VMEM((own, width), F32),
            pltpu.VMEM((own, width), F32),
            pltpu.VMEM((mem_own, width), F32),
            pltpu.VMEM((seqs * first.queries, width), BF16),
            pltpu.VMEM((seqs * first.ext, 3 * width), BF16),
            pltpu.VMEM((seqs * first.queries, width), BF16),
            pltpu.VMEM((SMALL_ROWS, LANES), BF16),
            dma((2 * copies_in + 8,)),
        ],
        (place, x1, gz1, gh1_tied, gmem1, from_right1, from_left1, mixed0, active0, slope0, att0,
         probs0, proj0, z0, frames_own, frames_left, frames_right, norm_gains, biases_by_row, vec1)
        + tuple(first_all),
        flops=28 * own * (4 * width * width + 2 * width * ff),
        moved=4 * (4 * width * width + 2 * width * ff),
        vmem=34,
    )
    from_right0 = shifted(back_left0, "seg", -1)
    from_left0 = shifted(back_right0, "seg", 1)
    gz0_last = gz0
    if by_blocks:
        second1 = across_second(far1)
        mine0, theirs0 = grad_blocks0[0], other_core(after(grad_blocks0[1], second1))
        both1 = summed(mine1[0], theirs1[0], second1)
        lines1 = swap_z(both1)
        far0 = summed(mine0[1], after(theirs0, both1, from_right0, from_left0)[1])
        second0 = across_second(far0)
        mid0 = summed(mine0[0, 1], theirs0[0, 1], second0[1])
        first0 = across_first(mid0)
        held0 = summed(mine0[0, 0], theirs0[0, 0], after(second0, mid0)[0])
        near0 = summed(held0, first0)
        blocks = CHIPS_Z * all_rows
        near0 = jnp.concatenate(
            [
                near0[:blocks].reshape(CHIPS_Z, all_rows, LANES),
                jnp.broadcast_to(near0[None, blocks:], (CHIPS_Z, SMALL_ROWS, LANES)),
            ],
            axis=1,
        )
        first_parts = swap_z(near0)
        gz0_last, lines1 = lax.optimization_barrier((after(gz0, near0), lines1))
        cross1 = jnp.sum(lines1[:, all_rows:].astype(F32), axis=0, keepdims=True).astype(BF16)
        first1 = across_first(cross1)
    frames_grad = call(
        lambda *refs: frames_grad_kernel(first, seqs, *refs),
        [vmem_spec()] * 8,
        [((seqs, rows, width), F32)],
        [vmem_spec()],
        [],
        (frames_own, gz0_last, gh0, gmem0, from_right0, from_left0, norm_gains, biases_by_row),
    )[0]

    if by_blocks:
        shapes = [member.shape for member in (qkv_t, out_t, ffn_in_weight, down_t)]
        held = [pltpu.VMEM(shape[1:], F32) for shape in shapes]
        whole = [(shape, F32) for shape in shapes]
        written = call(
            lambda *refs: unpack_last_kernel(spots, LAYERS - 1, *refs),
            [
                pl.BlockSpec((CHIPS_Z, all_rows, LANES), lambda i: (0, 0, 0)),
                pl.BlockSpec((1, all_rows, LANES), lambda i: (0, 0, 0)),
            ],
            whole,
            [hbm_spec()] * 4,
            held + [dma((4,))],
            [lines1, first1],
            grid=(1,),
        )
        small_shapes = [norm_gains.shape, (biases.shape[1], LAYERS, width), ffn_bias.shape]
        reduced = call(
            lambda *refs: unpack_first_kernel(spots, all_rows, *refs),
            [vmem_spec()] + [hbm_spec()] * 4,
            whole + [(shape, F32) for shape in small_shapes],
            [hbm_spec()] * 4 + [vmem_spec()] * 3,
            held + [dma((4,))],
            [after(first_parts, frames_grad)] + list(written),
            aliases={1 + i: i for i in range(4)},
        )
        small = reduced[4], jnp.swapaxes(reduced[5], 0, 1), reduced[6]
        reduced = [
            jnp.swapaxes(reduced[0], 1, 2),
            jnp.swapaxes(reduced[1], 1, 2),
            reduced[2],
            jnp.swapaxes(reduced[3], 1, 2),
        ]
    else:
        reduced = []
        for member0, member1 in zip(grad_blocks0, grad_blocks1):
            both = jnp.stack([member0, member1]).reshape(LAYERS, -1, member0.shape[3])
            both = jnp.swapaxes(both, 1, 2)
            both = lax.psum_scatter(both, "seg", scatter_dimension=2, tiled=True)
            both = lax.psum_scatter(both, "rep", scatter_dimension=1, tiled=True)
            reduced.append(both.astype(F32))
        small = sum_everywhere(jnp.stack([vec0, vec1 + upper_vec]))
        small = small[:, 0:2], small[:, 2:8], small[:, 8:12].reshape(ffn_bias.shape)

    return (
        encoded.reshape(frames.shape),
        frames_grad.reshape(frames.shape),
        reduced[0],
        reduced[1],
        reduced[2],
        reduced[3],
        small[0],
        small[1],
        small[2],
    )


def solution(mesh):
    in_specs = (
        P(None, "rep", "seg", None),
        P(None, "rep", None),
        P(None, "rep", "seg", None),
        P(None, "rep", "seg"),
        P(None, "rep", "seg"),
        P(None, "rep", "seg"),
        P(None, "rep", "seg"),
        P(),
        P(),
        P(),
    )
    out_specs = (
        P(None, "rep", "seg", None),
        P(None, "rep", "seg", None),
        P(None, "rep", "seg"),
        P(None, "rep", "seg"),
        P(None, "rep", "seg"),
        P(None, "rep", "seg"),
        P(),
        P(),
        P(),
    )
    return jax.shard_map(
        on_device, mesh=mesh, in_specs=in_specs, out_specs=out_specs, check_vma=False
    )
```

profile of v0, /device:TPU:0, one launch (start us, length us, event | category | flops | bytes accessed | tf_op | source)
XLA Modules:
  0.0 233.5 jit_solution(5926600522134668194)
XLA Ops:
  0.7 2.5 %shard_map.169 = (bf16[4,768,128]{2,1,0:T(8,128)(2,1)}, bf16[4,768,128]{2,1,0:T(8,128)(2,1)}) custom-call(bf16[2,192,128]{2,1,0:T(8,128)(2,1)} %bitcast.80, bf16[2,64,128]{2,1,0:T(8,128)(2,1)} %bitcast.82, bf16[2,128,256]{2,1,0:T(8,128)(2,1)} %refs_2_.1, bf16[2,64,512]{2,1,0:T(8,128)(2,1)} %bitcast.79), custom_call_target="tpu_custom_call" | custom-call | tf_op jit(solution)/shard_map/pallas_call | solution.py:881
  3.2 6.5 %all-to-all-start = ((bf16[4,768,128]{2,1,0:T(8,128)(2,1)}), bf16[4,768,128]{2,1,0:T(8,128)(2,1)S(1)}, u32[]{:S(2)}, u32[]{:S(2)}) async-start(bf16[4,768,128]{2,1,0:T(8,128)(2,1)} %get-tuple-element.68), calls=%async_computation | async-start | bytes 1572864 | tf_op jit(solution)/shard_map/all_to_all | solution.py:841
  9.6 1.6 collective-permute-start
  11.2 3.3 %collective-permute-start.1 = (bf16[2,16,512]{2,1,0:T(8,128)(2,1)S(1)}, bf16[2,16,512]{2,1,0:T(8,128)(2,1)S(1)}, u32[]{:S(2)}, u32[]{:S(2)}) collective-permute-start(bf16[2,16,512]{2,1,0:T(8,128)(2,1)S(1)} %slice.85), channel_id=1, source_target_pairs={{0,28},{4,0},{8,4},{12,8},{16,12},{20,16},{24,20},{28,24},{1,29},{... | collective-permute-start | bytes 98312 | tf_op jit(solution)/shard_map/ppermute | solution.py:808
  14.9 8.2 %collective-permute-done.1.refs_4_.refs_16_ = bf16[2,16,512]{2,1,0:T(8,128)(2,1)S(1)} collective-permute-done((bf16[2,16,512]{2,1,0:T(8,128)(2,1)S(1)}, bf16[2,16,512]{2,1,0:T(8,128)(2,1)S(1)}, u32[]{:S(2)}, u32[]{:S(2)}) %collective-permute-start.1) | collective-permute-done | bytes 32800 | tf_op jit(solution)/shard_map/ppermute | solution.py:808
  23.1 7.2 %collective-permute-done.refs_3_.refs_15_ = bf16[2,64,512]{2,1,0:T(8,128)(2,1)S(1)} collective-permute-done((bf16[2,64,512]{2,1,0:T(8,128)(2,1)S(1)}, bf16[2,64,512]{2,1,0:T(8,128)(2,1)S(1)}, u32[]{:S(2)}, u32[]{:S(2)}) %collective-permute-start) | collective-permute-done | bytes 131104 | tf_op jit(solution)/shard_map/ppermute | solution.py:808
  30.3 5.0 %all-to-all-start.1 = ((bf16[4,768,128]{2,1,0:T(8,128)(2,1)}), bf16[4,768,128]{2,1,0:T(8,128)(2,1)S(1)}, u32[]{:S(2)}, u32[]{:S(2)}) async-start(bf16[4,768,128]{2,1,0:T(8,128)(2,1)} %get-tuple-element.74), calls=%async_computation.1 | async-start | bytes 1572864 | tf_op jit(solution)/shard_map/all_to_all | solution.py:841
  35.3 1.5 collective-permute-start.2
  36.8 2.3 collective-permute-start.3
  39.1 16.5 %collective-permute-done.2.refs_10_.refs_21_ = bf16[4,768,128]{2,1,0:T(8,128)(2,1)S(1)} collective-permute-done((bf16[4,768,128]{2,1,0:T(8,128)(2,1)S(1)}, bf16[4,768,128]{2,1,0:T(8,128)(2,1)S(1)}, u32[]{:S(2)}, u32[]{:S(2)}) %collective-permute-start.2) | collective-permute-done | bytes 786464 | tf_op jit(solution)/shard_map/ppermute | solution.py:818
  55.6 1.5 collective-permute-start.4
  57.6 10.0 %collective-permute-done.4.refs_12_.refs_23_ = bf16[4,768,128]{2,1,0:T(8,128)(2,1)S(1)} collective-permute-done((bf16[4,768,128]{2,1,0:T(8,128)(2,1)S(1)}, bf16[4,768,128]{2,1,0:T(8,128)(2,1)S(1)}, u32[]{:S(2)}, u32[]{:S(2)}) %collective-permute-start.4) | collective-permute-done | bytes 786464 | tf_op jit(solution)/shard_map/ppermute | solution.py:818
  67.6 1.5 collective-permute-start.11
  69.1 1.5 collective-permute-start.12
  70.7 9.8 %shard_map.170 = (bf16[416,512]{1,0:T(8,128)(2,1)S(1)}, bf16[416,1536]{1,0:T(8,128)(2,1)S(1)}, bf16[8,192,288]{2,1,0:T(8,128)(2,1)S(1)}, bf16[288,512]{1,0:T(8,1...) custom-call(s32[18]{0:T(128)S(1)} %stack.65.refs_0_, ...), custom_call_target="tpu_custom_call" | custom-call | flops 9663676416 | bytes 6291456 | tf_op jit(solution)/shard_map/pallas_call | solution.py:881
  81.2 4.0 %collective-permute-start.10 = (bf16[2,16,512]{2,1,0:T(8,128)(2,1)S(1)}, bf16[2,16,512]{2,1,0:T(8,128)(2,1)S(1)}, u32[]{:S(2)}, u32[]{:S(2)}) collective-permute-start(bf16[2,16,512]{2,1,0:T(8,128)(2,1)S(1)} %get-tuple-element.78), channel_id=1, source_target_pairs={{0,28},{4,0},{8,4},{12,8},{16,12},{20,16},{24,20},{28,24},{1,29},{... | collective-permute-start | bytes 98312 | tf_op jit(solution)/shard_map/ppermute | solution.py:808
  85.2 2.1 collective-permute-done.11.refs_13_
  87.3 2.7 %collective-permute-done.12.refs_14_ = bf16[4,768,128]{2,1,0:T(8,128)(2,1)S(1)} collective-permute-done((bf16[4,768,128]{2,1,0:T(8,128)(2,1)S(1)}, bf16[4,768,128]{2,1,0:T(8,128)(2,1)S(1)}, u32[]{:S(2)}, u32[]{:S(2)}) %collective-permute-start.12) | collective-permute-done | bytes 786464 | tf_op jit(solution)/shard_map/ppermute | solution.py:818
  90.4 1.5 collective-permute-start.13
  92.4 10.0 %collective-permute-done.13.refs_15_ = bf16[4,768,128]{2,1,0:T(8,128)(2,1)S(1)} collective-permute-done((bf16[4,768,128]{2,1,0:T(8,128)(2,1)S(1)}, bf16[4,768,128]{2,1,0:T(8,128)(2,1)S(1)}, u32[]{:S(2)}, u32[]{:S(2)}) %collective-permute-start.13) | collective-permute-done | bytes 786464 | tf_op jit(solution)/shard_map/ppermute | solution.py:818
  102.4 2.3 collective-permute-done.17.refs_19_
  104.7 18.5 %shard_map.171 = (f32[2,128,512]{2,1,0:T(8,128)}, f32[256,512]{1,0:T(8,128)S(1)}, f32[256,512]{1,0:T(8,128)S(1)}, f32[16,512]{1,0:T(8,128)S(1)}, bf16[2,48,512]{...) custom-call(s32[18]{0:T(128)S(1)} %stack.65.refs_0_, ...), custom_call_target="tpu_custom_call" | custom-call | flops 24159191040 | bytes 12582912 | tf_op jit(solution)/shard_map/pallas_call | solution.py:881
  123.3 3.7 %collective-permute-start.19 = (bf16[2,48,512]{2,1,0:T(8,128)(2,1)S(1)}, bf16[2,48,512]{2,1,0:T(8,128)(2,1)S(1)}, u32[]{:S(2)}, u32[]{:S(2)}) collective-permute-start(bf16[2,48,512]{2,1,0:T(8,128)(2,1)S(1)} %get-tuple-element.90), channel_id=1, source_target_pairs={{0,28},{4,0},{8,4},{12,8},{16,12},{20,16},{24,20},{28,24},{1,29},{... | collective-permute-start | bytes 294920 | tf_op jit(solution)/shard_map/ppermute | solution.py:808
  127.0 1.9 collective-permute-done.18
  128.9 1.9 fusion.4
  131.0 1.5 collective-permute-start.21
  132.5 1.1 collective-permute-done.20.refs_6_
  133.6 15.2 %shard_map.172 = (f32[256,512]{1,0:T(8,128)S(1)}, f32[256,512]{1,0:T(8,128)S(1)}, f32[16,512]{1,0:T(8,128)S(1)}, bf16[2,48,512]{2,1,0:T(8,128)(2,1)S(1)}, bf16[2...) custom-call(s32[18]{0:T(128)S(1)} %stack.65.refs_0_, ...), custom_call_target="tpu_custom_call" | custom-call | flops 22548578304 | bytes 12582912 | tf_op jit(solution)/shard_map/pallas_call | solution.py:881
  148.8 2.9 %collective-permute-done.21 = bf16[4,1536,128]{2,1,0:T(8,128)(2,1)S(1)} collective-permute-done((bf16[4,1536,128]{2,1,0:T(8,128)(2,1)}, bf16[4,1536,128]{2,1,0:T(8,128)(2,1)S(1)}, u32[]{:S(2)}, u32[]{:S(2)}) %collective-permute-start.21) | collective-permute-done | bytes 1572896 | tf_op jit(solution)/shard_map/ppermute | solution.py:818
  151.7 3.7 %collective-permute-start.23 = (bf16[2,48,512]{2,1,0:T(8,128)(2,1)S(1)}, bf16[2,48,512]{2,1,0:T(8,128)(2,1)S(1)}, u32[]{:S(2)}, u32[]{:S(2)}) collective-permute-start(bf16[2,48,512]{2,1,0:T(8,128)(2,1)S(1)} %get-tuple-element.104), channel_id=1, source_target_pairs={{0,28},{4,0},{8,4},{12,8},{16,12},{20,16},{24,20},{28,24},{1,29},{... | collective-permute-start | bytes 294920 | tf_op jit(solution)/shard_map/ppermute | solution.py:808
  155.3 1.8 fusion
  157.1 4.8 %collective-permute-done.24.refs_5_ = bf16[2,16,512]{2,1,0:T(8,128)(2,1)S(1)} collective-permute-done((bf16[2,16,512]{2,1,0:T(8,128)(2,1)S(1)}, bf16[2,16,512]{2,1,0:T(8,128)(2,1)S(1)}, u32[]{:S(2)}, u32[]{:S(2)}) %collective-permute-start.24) | collective-permute-done | bytes 32800 | tf_op jit(solution)/shard_map/ppermute | solution.py:808
  161.9 2.0 fusion.1
  164.2 3.6 %all-to-all-start.2 = ((bf16[4,1536,128]{2,1,0:T(8,128)(2,1)}), bf16[4,1536,128]{2,1,0:T(8,128)(2,1)S(1)}, u32[]{:S(2)}, u32[]{:S(2)}) async-start(bf16[4,1536,128]{2,1,0:T(8,128)(2,1)} %fusion), calls=%async_computation.2 | async-start | bytes 3145728 | tf_op jit(solution)/shard_map/all_to_all | solution.py:841
  167.8 17.9 %collective-permute-done.25 = bf16[2,3200,128]{2,1,0:T(8,128)(2,1)} collective-permute-done((bf16[2,3200,128]{2,1,0:T(8,128)(2,1)}, bf16[2,3200,128]{2,1,0:T(8,128)(2,1)}, u32[]{:S(2)}, u32[]{:S(2)}) %collective-permute-start.25) | collective-permute-done | bytes 1638432 | tf_op jit(solution)/shard_map/ppermute | solution.py:818
  185.6 2.0 fusion.3
  187.6 1.5 collective-permute-start.26
  189.2 10.9 %collective-permute-done.26 = bf16[3200,128]{1,0:T(8,128)(2,1)S(1)} collective-permute-done((bf16[3200,128]{1,0:T(8,128)(2,1)S(1)}, bf16[3200,128]{1,0:T(8,128)(2,1)S(1)}, u32[]{:S(2)}, u32[]{:S(2)}) %collective-permute-start.26) | collective-permute-done | bytes 819232 | tf_op jit(solution)/shard_map/ppermute | solution.py:818
  200.0 2.1 add_convert_fusion.2
  202.2 1.0 pad_maximum_fusion
  203.2 2.2 all-to-all-done.2.refs_0_
  205.4 3.5 %all-to-all-start.3 = ((bf16[4,896,128]{2,1,0:T(8,128)(2,1)}), bf16[4,896,128]{2,1,0:T(8,128)(2,1)S(1)}, u32[]{:S(2)}, u32[]{:S(2)}) async-start(bf16[4,896,128]{2,1,0:T(8,128)(2,1)} %pad_maximum_fusion), calls=%async_computation.3 | async-start | bytes 1835008 | tf_op jit(solution)/shard_map/all_to_all | solution.py:841
  209.7 1.0 copy-done.3
  210.7 1.2 shard_map.173
  211.9 2.9 %collective-permute-done.27.refs_1_ = bf16[1,768,128]{2,1,0:T(8,128)(2,1)S(1)} collective-permute-done((bf16[1,768,128]{2,1,0:T(8,128)(2,1)S(1)}, bf16[1,768,128]{2,1,0:T(8,128)(2,1)S(1)}, u32[]{:S(2)}, u32[]{:S(2)}) %collective-permute-start.27) | collective-permute-done | bytes 196640 | tf_op jit(solution)/shard_map/ppermute | solution.py:818
  214.8 0.9 shard_map.174
  215.7 16.0 %all-to-all-done.3.refs_0_ = bf16[4,896,128]{2,1,0:T(8,128)(2,1)S(1)} async-done(((bf16[4,896,128]{2,1,0:T(8,128)(2,1)}), bf16[4,896,128]{2,1,0:T(8,128)(2,1)S(1)}, u32[]{:S(2)}, u32[]{:S(2)}) %all-to-all-start.3) | async-done | bytes 917536 | tf_op jit(solution)/shard_map/all_to_all | solution.py:841
  231.7 1.5 shard_map.175
  (66 shorter events, 4.2 us)
Async XLA Ops:
  0.6 9.0 %copy-start.1 = (bf16[2,1,128,512]{3,2,1,0:T(8,128)(2,1)S(1)}, bf16[2,1,128,512]{3,2,1,0:T(8,128)(2,1)}, u32[]{:S(2)}) copy-start(bf16[2,1,128,512]{3,2,1,0:T(8,128)(2,1)} %param.10) | copy-start | bytes 786436
  0.7 13.9 %copy-start.4 = (f32[2,6,512]{2,0,1:T(2,128)S(1)}, f32[2,6,512]{2,0,1:T(2,128)}, u32[]{:S(2)}) copy-start(f32[2,6,512]{2,0,1:T(2,128)} %param.18) | copy-start | bytes 73732
  0.7 14.0 %copy-start.11 = (s32[2,1,4]{2,1,0:T(1,128)S(1)}, s32[2,1,4]{2,1,0:T(1,128)}, u32[]{:S(2)}) copy-start(s32[2,1,4]{2,1,0:T(1,128)} %param.11) | copy-start | bytes 100
  3.1 67.5 %copy-start.5 = (f32[2,2,512]{2,1,0:T(2,128)S(1)}, f32[2,2,512]{2,1,0:T(2,128)}, u32[]{:S(2)}) copy-start(f32[2,2,512]{2,1,0:T(2,128)} %refs_6_.1) | copy-start | bytes 24580
  3.1 67.5 %copy-start.7 = (f32[2,2048]{1,0:T(2,128)S(1)}, f32[2,2048]{1,0:T(2,128)}, u32[]{:S(2)}) copy-start(f32[2,2048]{1,0:T(2,128)} %refs_10_.1) | copy-start | bytes 49156
  3.2 27.2 %all-to-all-start = ((bf16[4,768,128]{2,1,0:T(8,128)(2,1)}), bf16[4,768,128]{2,1,0:T(8,128)(2,1)S(1)}, u32[]{:S(2)}, u32[]{:S(2)}) async-start(bf16[4,768,128]{2,1,0:T(8,128)(2,1)} %get-tuple-element.68), calls=%async_computation | async-start | bytes 1572864 | tf_op jit(solution)/shard_map/all_to_all | solution.py:841
  9.6 20.7 %collective-permute-start = (bf16[2,64,512]{2,1,0:T(8,128)(2,1)S(1)}, bf16[2,64,512]{2,1,0:T(8,128)(2,1)S(1)}, u32[]{:S(2)}, u32[]{:S(2)}) collective-permute-start(bf16[2,64,512]{2,1,0:T(8,128)(2,1)S(1)} %slice.84), channel_id=1, source_target_pairs={{0,4},{4,8},{8,12},{12,16},{16,20},{20,24},{24,28},{28,0},{1,5},{5... | collective-permute-start | bytes 393224 | tf_op jit(solution)/shard_map/ppermute | solution.py:808
  11.2 11.9 %collective-permute-start.1 = (bf16[2,16,512]{2,1,0:T(8,128)(2,1)S(1)}, bf16[2,16,512]{2,1,0:T(8,128)(2,1)S(1)}, u32[]{:S(2)}, u32[]{:S(2)}) collective-permute-start(bf16[2,16,512]{2,1,0:T(8,128)(2,1)S(1)} %slice.85), channel_id=1, source_target_pairs={{0,28},{4,0},{8,4},{12,8},{16,12},{20,16},{24,20},{28,24},{1,29},{... | collective-permute-start | bytes 98312 | tf_op jit(solution)/shard_map/ppermute | solution.py:808
  30.3 25.3 %all-to-all-start.1 = ((bf16[4,768,128]{2,1,0:T(8,128)(2,1)}), bf16[4,768,128]{2,1,0:T(8,128)(2,1)S(1)}, u32[]{:S(2)}, u32[]{:S(2)}) async-start(bf16[4,768,128]{2,1,0:T(8,128)(2,1)} %get-tuple-element.74), calls=%async_computation.1 | async-start | bytes 1572864 | tf_op jit(solution)/shard_map/all_to_all | solution.py:841
  35.3 20.3 %collective-permute-start.2 = (bf16[4,768,128]{2,1,0:T(8,128)(2,1)S(1)}, bf16[4,768,128]{2,1,0:T(8,128)(2,1)S(1)}, u32[]{:S(2)}, u32[]{:S(2)}) collective-permute-start(bf16[4,768,128]{2,1,0:T(8,128)(2,1)S(1)} %all-to-all-done.refs_9_.refs_20_), channel_id=1, source_target_pairs={{0,2},{1,5},{2,0},{3,7},{4,6},{5,1},{6,4},{7,3},{8,10},{9,13},{10,... | collective-permute-start | bytes 2359304 | tf_op jit(solution)/shard_map/ppermute | solution.py:818
  36.8 20.8 %collective-permute-start.3 = (bf16[4,768,128]{2,1,0:T(8,128)(2,1)S(1)}, bf16[4,768,128]{2,1,0:T(8,128)(2,1)}, u32[]{:S(2)}, u32[]{:S(2)}) collective-permute-start(bf16[4,768,128]{2,1,0:T(8,128)(2,1)S(1)} %all-to-all-done.refs_9_.refs_20_), channel_id=1, source_target_pairs={{0,4},{1,3},{2,6},{3,1},{4,0},{5,7},{6,2},{7,5},{8,12},{9,11},{10,... | collective-permute-start | bytes 2359304 | tf_op jit(solution)/shard_map/ppermute | solution.py:818
  55.6 12.0 %collective-permute-start.4 = (bf16[4,768,128]{2,1,0:T(8,128)(2,1)S(1)}, bf16[4,768,128]{2,1,0:T(8,128)(2,1)S(1)}, u32[]{:S(2)}, u32[]{:S(2)}) collective-permute-start(bf16[4,768,128]{2,1,0:T(8,128)(2,1)S(1)} %collective-permute-done.2.refs_10_.refs_21_), channel_id=1, source_target_pairs={{0,4},{1,3},{2,6},{3,1},{4,0},{5,7},{6,2},{7,5},{8,12},{9,11},{10,... | collective-permute-start | bytes 2359304 | tf_op jit(solution)/shard_map/ppermute | solution.py:818
  57.1 12.0 %collective-permute-start.5 = (bf16[4,768,128]{2,1,0:T(8,128)(2,1)S(1)}, bf16[4,768,128]{2,1,0:T(8,128)(2,1)S(1)}, u32[]{:S(2)}, u32[]{:S(2)}) collective-permute-start(bf16[4,768,128]{2,1,0:T(8,128)(2,1)S(1)} %all-to-all-done.refs_9_.refs_20_), channel_id=1, source_target_pairs={{0,1},{1,0},{2,3},{3,2},{4,5},{5,4},{6,7},{7,6},{8,9},{9,8},{10,11... | collective-permute-start | bytes 2359304 | tf_op jit(solution)/shard_map/ppermute | solution.py:818
  57.1 13.5 %collective-permute-start.6 = (bf16[4,768,128]{2,1,0:T(8,128)(2,1)S(1)}, bf16[4,768,128]{2,1,0:T(8,128)(2,1)S(1)}, u32[]{:S(2)}, u32[]{:S(2)}) collective-permute-start(bf16[4,768,128]{2,1,0:T(8,128)(2,1)S(1)} %collective-permute-done.2.refs_10_.refs_21_), channel_id=1, source_target_pairs={{0,1},{1,0},{2,3},{3,2},{4,5},{5,4},{6,7},{7,6},{8,9},{9,8},{10,11... | collective-permute-start | bytes 2359304 | tf_op jit(solution)/shard_map/ppermute | solution.py:818
  57.6 13.0 %collective-permute-start.7 = (bf16[4,768,128]{2,1,0:T(8,128)(2,1)}, bf16[4,768,128]{2,1,0:T(8,128)(2,1)S(1)}, u32[]{:S(2)}, u32[]{:S(2)}) collective-permute-start(bf16[4,768,128]{2,1,0:T(8,128)(2,1)} %collective-permute-done.3.refs_11_.refs_22_), channel_id=1, source_target_pairs={{0,1},{1,0},{2,3},{3,2},{4,5},{5,4},{6,7},{7,6},{8,9},{9,8},{10,11... | collective-permute-start | bytes 2359304 | tf_op jit(solution)/shard_map/ppermute | solution.py:818
  67.6 3.0 %collective-permute-start.8 = (bf16[4,768,128]{2,1,0:T(8,128)(2,1)S(1)}, bf16[4,768,128]{2,1,0:T(8,128)(2,1)S(1)}, u32[]{:S(2)}, u32[]{:S(2)}) collective-permute-start(bf16[4,768,128]{2,1,0:T(8,128)(2,1)S(1)} %collective-permute-done.4.refs_12_.refs_23_), channel_id=1, source_target_pairs={{0,1},{1,0},{2,3},{3,2},{4,5},{5,4},{6,7},{7,6},{8,9},{9,8},{10,11... | collective-permute-start | bytes 2359304 | tf_op jit(solution)/shard_map/ppermute | solution.py:818
  67.6 19.7 %collective-permute-start.11 = (bf16[4,768,128]{2,1,0:T(8,128)(2,1)S(1)}, bf16[4,768,128]{2,1,0:T(8,128)(2,1)S(1)}, u32[]{:S(2)}, u32[]{:S(2)}) collective-permute-start(bf16[4,768,128]{2,1,0:T(8,128)(2,1)S(1)} %all-to-all-done.1.refs_12_), channel_id=1, source_target_pairs={{0,2},{1,5},{2,0},{3,7},{4,6},{5,1},{6,4},{7,3},{8,10},{9,13},{10,... | collective-permute-start | bytes 2359304 | tf_op jit(solution)/shard_map/ppermute | solution.py:818
  69.1 20.9 %collective-permute-start.12 = (bf16[4,768,128]{2,1,0:T(8,128)(2,1)S(1)}, bf16[4,768,128]{2,1,0:T(8,128)(2,1)S(1)}, u32[]{:S(2)}, u32[]{:S(2)}) collective-permute-start(bf16[4,768,128]{2,1,0:T(8,128)(2,1)S(1)} %all-to-all-done.1.refs_12_), channel_id=1, source_target_pairs={{0,4},{1,3},{2,6},{3,1},{4,0},{5,7},{6,2},{7,5},{8,12},{9,11},{10,... | collective-permute-start | bytes 2359304 | tf_op jit(solution)/shard_map/ppermute | solution.py:818
  70.6 34.0 %copy-start.6 = (bf16[2,1,128,512]{3,2,1,0:T(8,128)(2,1)S(1)}, bf16[2,1,128,512]{3,2,1,0:T(8,128)(2,1)}, u32[]{:S(2)}) copy-start(bf16[2,1,128,512]{3,2,1,0:T(8,128)(2,1)} %param.12) | copy-start | bytes 786436
  80.4 9.9 %collective-permute-start.9 = (bf16[2,48,512]{2,1,0:T(8,128)(2,1)S(1)}, bf16[2,48,512]{2,1,0:T(8,128)(2,1)S(1)}, u32[]{:S(2)}, u32[]{:S(2)}) collective-permute-start(bf16[2,48,512]{2,1,0:T(8,128)(2,1)S(1)} %get-tuple-element.77), channel_id=1, source_target_pairs={{0,4},{4,8},{8,12},{12,16},{16,20},{20,24},{24,28},{28,0},{1,5},{5... | collective-permute-start | bytes 294920 | tf_op jit(solution)/shard_map/ppermute | solution.py:808
  81.2 9.1 %collective-permute-start.10 = (bf16[2,16,512]{2,1,0:T(8,128)(2,1)S(1)}, bf16[2,16,512]{2,1,0:T(8,128)(2,1)S(1)}, u32[]{:S(2)}, u32[]{:S(2)}) collective-permute-start(bf16[2,16,512]{2,1,0:T(8,128)(2,1)S(1)} %get-tuple-element.78), channel_id=1, source_target_pairs={{0,28},{4,0},{8,4},{12,8},{16,12},{20,16},{24,20},{28,24},{1,29},{... | collective-permute-start | bytes 98312 | tf_op jit(solution)/shard_map/ppermute | solution.py:808
  90.4 12.0 %collective-permute-start.13 = (bf16[4,768,128]{2,1,0:T(8,128)(2,1)S(1)}, bf16[4,768,128]{2,1,0:T(8,128)(2,1)S(1)}, u32[]{:S(2)}, u32[]{:S(2)}) collective-permute-start(bf16[4,768,128]{2,1,0:T(8,128)(2,1)S(1)} %collective-permute-done.11.refs_13_), channel_id=1, source_target_pairs={{0,4},{1,3},{2,6},{3,1},{4,0},{5,7},{6,2},{7,5},{8,12},{9,11},{10,... | collective-permute-start | bytes 2359304 | tf_op jit(solution)/shard_map/ppermute | solution.py:818
  91.9 10.5 %collective-permute-start.14 = (bf16[4,768,128]{2,1,0:T(8,128)(2,1)S(1)}, bf16[4,768,128]{2,1,0:T(8,128)(2,1)S(1)}, u32[]{:S(2)}, u32[]{:S(2)}) collective-permute-start(bf16[4,768,128]{2,1,0:T(8,128)(2,1)S(1)} %all-to-all-done.1.refs_12_), channel_id=1, source_target_pairs={{0,1},{1,0},{2,3},{3,2},{4,5},{5,4},{6,7},{7,6},{8,9},{9,8},{10,11... | collective-permute-start | bytes 2359304 | tf_op jit(solution)/shard_map/ppermute | solution.py:818
  91.9 10.5 %collective-permute-start.15 = (bf16[4,768,128]{2,1,0:T(8,128)(2,1)S(1)}, bf16[4,768,128]{2,1,0:T(8,128)(2,1)S(1)}, u32[]{:S(2)}, u32[]{:S(2)}) collective-permute-start(bf16[4,768,128]{2,1,0:T(8,128)(2,1)S(1)} %collective-permute-done.11.refs_13_), channel_id=1, source_target_pairs={{0,1},{1,0},{2,3},{3,2},{4,5},{5,4},{6,7},{7,6},{8,9},{9,8},{10,11... | collective-permute-start | bytes 2359304 | tf_op jit(solution)/shard_map/ppermute | solution.py:818
  92.4 10.0 %collective-permute-start.16 = (bf16[4,768,128]{2,1,0:T(8,128)(2,1)S(1)}, bf16[4,768,128]{2,1,0:T(8,128)(2,1)S(1)}, u32[]{:S(2)}, u32[]{:S(2)}) collective-permute-start(bf16[4,768,128]{2,1,0:T(8,128)(2,1)S(1)} %collective-permute-done.12.refs_14_), channel_id=1, source_target_pairs={{0,1},{1,0},{2,3},{3,2},{4,5},{5,4},{6,7},{7,6},{8,9},{9,8},{10,11... | collective-permute-start | bytes 2359304 | tf_op jit(solution)/shard_map/ppermute | solution.py:818
  102.4 2.3 collective-permute-start.17
  123.1 5.7 %collective-permute-start.18 = (bf16[2,4,1536,128]{3,2,1,0:T(8,128)(2,1)S(1)}, bf16[2,4,1536,128]{3,2,1,0:T(8,128)(2,1)S(1)}, u32[]{:S(2)}, u32[]{:S(2)}) collective-permute-start(bf16[2,4,1536,128]{3,2,1,0:T(8,128)(2,1)S(1)} %get-tuple-element.87), channel_id=1, source_target_pairs={{0,1},{1,0},{2,3},{3,2},{4,5},{5,4},{6,7},{7,6},{8,9},{9,8},{10,11... | collective-permute-start | bytes 9437192 | tf_op jit(solution)/shard_map/ppermute | solution.py:818
  123.3 10.3 %collective-permute-start.19 = (bf16[2,48,512]{2,1,0:T(8,128)(2,1)S(1)}, bf16[2,48,512]{2,1,0:T(8,128)(2,1)S(1)}, u32[]{:S(2)}, u32[]{:S(2)}) collective-permute-start(bf16[2,48,512]{2,1,0:T(8,128)(2,1)S(1)} %get-tuple-element.90), channel_id=1, source_target_pairs={{0,28},{4,0},{8,4},{12,8},{16,12},{20,16},{24,20},{28,24},{1,29},{... | collective-permute-start | bytes 294920 | tf_op jit(solution)/shard_map/ppermute | solution.py:808
  127.0 6.6 %collective-permute-start.20 = (bf16[2,16,512]{2,1,0:T(8,128)(2,1)S(1)}, bf16[2,16,512]{2,1,0:T(8,128)(2,1)S(1)}, u32[]{:S(2)}, u32[]{:S(2)}) collective-permute-start(bf16[2,16,512]{2,1,0:T(8,128)(2,1)S(1)} %get-tuple-element.91), channel_id=1, source_target_pairs={{0,4},{4,8},{8,12},{12,16},{16,20},{20,24},{24,28},{28,0},{1,5},{5... | collective-permute-start | bytes 98312 | tf_op jit(solution)/shard_map/ppermute | solution.py:808
  128.9 2.2 copy-start.9
  131.0 20.6 %collective-permute-start.21 = (bf16[4,1536,128]{2,1,0:T(8,128)(2,1)}, bf16[4,1536,128]{2,1,0:T(8,128)(2,1)S(1)}, u32[]{:S(2)}, u32[]{:S(2)}) collective-permute-start(bf16[4,1536,128]{2,1,0:T(8,128)(2,1)} %fusion.4), channel_id=1, source_target_pairs={{0,4},{1,3},{2,6},{3,1},{4,0},{5,7},{6,2},{7,5},{8,12},{9,11},{10,... | collective-permute-start | bytes 4718600 | tf_op jit(solution)/shard_map/ppermute | solution.py:818
  133.6 21.7 %copy-start.10 = (bf16[2,4,1536,128]{3,2,1,0:T(8,128)(2,1)S(1)}, bf16[2,4,1536,128]{3,2,1,0:T(8,128)(2,1)}, u32[]{:S(2)}) copy-start(bf16[2,4,1536,128]{3,2,1,0:T(8,128)(2,1)} %copy-done.9) | copy-start | bytes 9437188
  148.8 8.3 %copy-start.2 = (f32[256,512]{1,0:T(8,128)}, f32[256,512]{1,0:T(8,128)S(1)}, u32[]{:S(2)}) copy-start(f32[256,512]{1,0:T(8,128)S(1)} %get-tuple-element.110.refs_2_) | copy-start | bytes 1572868
  148.8 13.2 %copy-start = (bf16[2,2,3200,128]{3,2,1,0:T(8,128)(2,1)}, bf16[2,2,3200,128]{3,2,1,0:T(8,128)(2,1)S(1)}, u32[]{:S(2)}) copy-start(bf16[2,2,3200,128]{3,2,1,0:T(8,128)(2,1)S(1)} %get-tuple-element.101) | copy-start | bytes 9830404
  151.7 10.3 %collective-permute-start.22 = (bf16[2,2,3200,128]{3,2,1,0:T(8,128)(2,1)}, bf16[2,2,3200,128]{3,2,1,0:T(8,128)(2,1)S(1)}, u32[]{:S(2)}, u32[]{:S(2)}) collective-permute-start(bf16[2,2,3200,128]{3,2,1,0:T(8,128)(2,1)} %get-tuple-element.103), channel_id=1, source_target_pairs={{0,1},{1,0},{2,3},{3,2},{4,5},{5,4},{6,7},{7,6},{8,9},{9,8},{10,11... | collective-permute-start | bytes 9830408 | tf_op jit(solution)/shard_map/ppermute | solution.py:818
  151.7 10.3 %collective-permute-start.23 = (bf16[2,48,512]{2,1,0:T(8,128)(2,1)S(1)}, bf16[2,48,512]{2,1,0:T(8,128)(2,1)S(1)}, u32[]{:S(2)}, u32[]{:S(2)}) collective-permute-start(bf16[2,48,512]{2,1,0:T(8,128)(2,1)S(1)} %get-tuple-element.104), channel_id=1, source_target_pairs={{0,28},{4,0},{8,4},{12,8},{16,12},{20,16},{24,20},{28,24},{1,29},{... | collective-permute-start | bytes 294920 | tf_op jit(solution)/shard_map/ppermute | solution.py:808
  155.3 6.6 %collective-permute-start.24 = (bf16[2,16,512]{2,1,0:T(8,128)(2,1)S(1)}, bf16[2,16,512]{2,1,0:T(8,128)(2,1)S(1)}, u32[]{:S(2)}, u32[]{:S(2)}) collective-permute-start(bf16[2,16,512]{2,1,0:T(8,128)(2,1)S(1)} %get-tuple-element.105), channel_id=1, source_target_pairs={{0,4},{4,8},{8,12},{12,16},{16,20},{20,24},{24,28},{28,0},{1,5},{5... | collective-permute-start | bytes 98312 | tf_op jit(solution)/shard_map/ppermute | solution.py:808
  161.9 2.3 copy-start.8
  164.2 21.4 %collective-permute-start.25 = (bf16[2,3200,128]{2,1,0:T(8,128)(2,1)}, bf16[2,3200,128]{2,1,0:T(8,128)(2,1)}, u32[]{:S(2)}, u32[]{:S(2)}) collective-permute-start(bf16[2,3200,128]{2,1,0:T(8,128)(2,1)} %fusion.1), channel_id=1, source_target_pairs={{0,4},{1,3},{2,6},{3,1},{4,0},{5,7},{6,2},{7,5},{8,12},{9,11},{10,... | collective-permute-start | bytes 4915208 | tf_op jit(solution)/shard_map/ppermute | solution.py:818
  164.2 41.2 %all-to-all-start.2 = ((bf16[4,1536,128]{2,1,0:T(8,128)(2,1)}), bf16[4,1536,128]{2,1,0:T(8,128)(2,1)S(1)}, u32[]{:S(2)}, u32[]{:S(2)}) async-start(bf16[4,1536,128]{2,1,0:T(8,128)(2,1)} %fusion), calls=%async_computation.2 | async-start | bytes 3145728 | tf_op jit(solution)/shard_map/all_to_all | solution.py:841
  187.6 12.4 %collective-permute-start.26 = (bf16[3200,128]{1,0:T(8,128)(2,1)S(1)}, bf16[3200,128]{1,0:T(8,128)(2,1)S(1)}, u32[]{:S(2)}, u32[]{:S(2)}) collective-permute-start(bf16[3200,128]{1,0:T(8,128)(2,1)S(1)} %fusion.3), channel_id=1, source_target_pairs={{0,2},{1,5},{2,0},{3,7},{4,6},{5,1},{6,4},{7,3},{8,10},{9,13},{10,... | collective-permute-start | bytes 2457608 | tf_op jit(solution)/shard_map/ppermute | solution.py:818
  205.4 26.3 %all-to-all-start.3 = ((bf16[4,896,128]{2,1,0:T(8,128)(2,1)}), bf16[4,896,128]{2,1,0:T(8,128)(2,1)S(1)}, u32[]{:S(2)}, u32[]{:S(2)}) async-start(bf16[4,896,128]{2,1,0:T(8,128)(2,1)} %pad_maximum_fusion), calls=%async_computation.3 | async-start | bytes 1835008 | tf_op jit(solution)/shard_map/all_to_all | solution.py:841
  209.1 5.7 %collective-permute-start.27 = (bf16[1,768,128]{2,1,0:T(8,128)(2,1)S(1)}, bf16[1,768,128]{2,1,0:T(8,128)(2,1)S(1)}, u32[]{:S(2)}, u32[]{:S(2)}) collective-permute-start(bf16[1,768,128]{2,1,0:T(8,128)(2,1)S(1)} %bitcast.78), channel_id=1, source_target_pairs={{0,2},{1,5},{2,0},{3,7},{4,6},{5,1},{6,4},{7,3},{8,10},{9,13},{10,... | collective-permute-start | bytes 589832 | tf_op jit(solution)/shard_map/ppermute | solution.py:818
  209.7 1.0 copy-start.3
where the time goes:
time: 234 us; the launch traced here: 233 us
  waiting for transfers between devices  120 us (51%)
  starting transfers between devices  50.2 us (21%)
  Pallas kernels  49.5 us (21%)
  other arithmetic  11 us (5%)
    ppermute x20, waiting for transfers between devices, permuted(): return lax.ppermute(value, ('seg', 'rep'), pairs)  79.9 us
    pallas_call x7, Pallas kernels, call(): pl.pallas_call(body, grid=grid, input_output_aliases=aliases, in_specs=in...  49.5 us
    ppermute x8, waiting for transfers between devices, shifted(): lax.ppermute(value, axis, [(i, (i + by) % size) for i in range(size)])  21.6 us
    all_to_all x4, starting transfers between devices, swap_z(): lax.all_to_all(blocks, 'seg', 0, 0, axis_index_groups=groups, tiled=True)  18.5 us
    all_to_all x4, waiting for transfers between devices, swap_z(): lax.all_to_all(blocks, 'seg', 0, 0, axis_index_groups=groups, tiled=True)  18.2 us
    ppermute x8, starting transfers between devices, shifted(): lax.ppermute(value, axis, [(i, (i + by) % size) for i in range(size)])  17 us
    ppermute x20, starting transfers between devices, permuted(): return lax.ppermute(value, ('seg', 'rep'), pairs)  14.6 us
    convert_element_type x5, other arithmetic, summed(): return total.astype(BF16)  9.64 us
  transfers between devices with their start and end apart: 32, of which 18 were waited for; matrix products, arithmetic and copies ran while one was open for 4% of the time, Pallas kernels for 12%

commit v1 on v0

--- a/solution.py
+++ b/solution.py
@@ -25,7 +25,8 @@
 CHIPS_Z = 4
 CHIPS_Y = 2
 BLOCKS = CHIPS_Z * CHIPS_Y
-SMALL_ROWS = 128
+VEC_ROWS = 12
+SMALL_ROWS = 96
 MIB = 1024 * 1024
 
 BF16 = jnp.bfloat16
@@ -475,7 +476,8 @@
     for layer in range(gains_ref.shape[0]):
         for part in range(parts):
             lanes = pl.ds(part * LANES, LANES)
-            block = sums[(layer * parts + part) * TILE : (layer * parts + part + 1) * TILE]
+            at = (part * gains_ref.shape[0] + layer) * VEC_ROWS
+            block = sums[at : at + VEC_ROWS]
             gains_ref[layer, :, lanes] = block[0:2]
             for row in range(biases_ref.shape[0]):
                 biases_ref[row, pl.ds(layer, 1), lanes] = block[2 + row : 3 + row]
@@ -776,12 +778,15 @@
         sems,
         out_at + len(outs),
     )
-    parts = sizes.width // LANES
-    for layer, total in enumerate((vec[...], last_vec[...] + upper_vec[...])):
-        for part in range(parts):
-            small_ref[pl.ds((layer * parts + part) * TILE, TILE), :] = total[
-                :, part * LANES : (part + 1) * LANES
-            ].astype(BF16)
+    totals = vec[...], last_vec[...] + upper_vec[...]
+    small_ref[...] = jnp.concatenate(
+        [
+            total[:VEC_ROWS, part * LANES : (part + 1) * LANES]
+            for part in range(sizes.pairs)
+            for total in totals
+        ],
+        axis=0,
+    ).astype(BF16)
     outs = outs + start_out([(ref, small_ref) for ref in small], sems, out_at + len(outs))
     wait_all(outs)
 
@@ -1124,7 +1129,8 @@
         mine0, theirs0 = grad_blocks0[0], other_core(after(grad_blocks0[1], second1))
         both1 = summed(mine1[0], theirs1[0], second1)
         lines1 = swap_z(both1)
-        far0 = summed(mine0[1], after(theirs0, both1, from_right0, from_left0)[1])
+        far0 = summed(mine0[1], after(theirs0, both1)[1])
+        far0 = after(far0, from_right0, from_left0)
         second0 = across_second(far0)
         mid0 = summed(mine0[0, 1], theirs0[0, 1], second0[1])
         first0 = across_first(mid0)

time: 234 us -> 230 us (0.983)
  waiting for transfers between devices: 120 us -> 114 us
    ppermute x8, waiting for transfers between devices: 21.6 us -> 18.7 us  [shifted(): lax.ppermute(value, axis, [(i, (i + by) % size) for i in range(size)])]
    ppermute x20, waiting for transfers between devices: 79.9 us -> 77.2 us  [permuted(): return lax.ppermute(value, ('seg', 'rep'), pairs)]
  transfers between devices with their start and end apart: 32 -> 32, of which waited for: 18 -> 18; matrix products, arithmetic and copies ran while one was open for 4% -> 5% of each run, Pallas kernels for 12% -> 12%
where the time goes in v1:
time: 230 us
  waiting for transfers between devices  114 us (50%)
  starting transfers between devices  51.9 us (23%)
  Pallas kernels  49.5 us (22%)
  other arithmetic  10.9 us (5%)
  local copies, waits for them, and re-layouts  2.57 us (1%)
    ppermute x20, waiting for transfers between devices, permuted(): return lax.ppermute(value, ('seg', 'rep'), pairs)  77.2 us
    pallas_call x7, Pallas kernels, call(): pl.pallas_call(body, grid=grid, input_output_aliases=aliases, in_specs=in...  49.5 us
    all_to_all x4, starting transfers between devices, swap_z(): lax.all_to_all(blocks, 'seg', 0, 0, axis_index_groups=groups, tiled=True)  20.3 us
    ppermute x8, waiting for transfers between devices, shifted(): lax.ppermute(value, axis, [(i, (i + by) % size) for i in range(size)])  18.7 us
    all_to_all x4, waiting for transfers between devices, swap_z(): lax.all_to_all(blocks, 'seg', 0, 0, axis_index_groups=groups, tiled=True)  17.8 us
    ppermute x8, starting transfers between devices, shifted(): lax.ppermute(value, axis, [(i, (i + by) % size) for i in range(size)])  17 us
    ppermute x20, starting transfers between devices, permuted(): return lax.ppermute(value, ('seg', 'rep'), pairs)  14.6 us
    convert_element_type x5, other arithmetic, summed(): return total.astype(BF16)  9.64 us
  transfers between devices with their start and end apart: 32, of which 18 were waited for; matrix products, arithmetic and copies ran while one was open for 5% of the time, Pallas kernels for 12%

profile of v1, /device:TPU:0, one launch (start us, length us, event | category | flops | bytes accessed | tf_op | source)
XLA Modules:
  0.0 229.9 jit_solution(4606563614627599009)
XLA Ops:
  0.7 2.5 %shard_map.169 = (bf16[4,768,128]{2,1,0:T(8,128)(2,1)}, bf16[4,768,128]{2,1,0:T(8,128)(2,1)}) custom-call(bf16[2,192,128]{2,1,0:T(8,128)(2,1)} %bitcast.80, bf16[2,64,128]{2,1,0:T(8,128)(2,1)} %bitcast.82, bf16[2,128,256]{2,1,0:T(8,128)(2,1)} %refs_2_.1, bf16[2,64,512]{2,1,0:T(8,128)(2,1)} %bitcast.79), custom_call_target="tpu_custom_call" | custom-call | tf_op jit(solution)/shard_map/pallas_call | solution.py:886
  3.1 6.5 %all-to-all-start = ((bf16[4,768,128]{2,1,0:T(8,128)(2,1)}), bf16[4,768,128]{2,1,0:T(8,128)(2,1)S(1)}, u32[]{:S(2)}, u32[]{:S(2)}) async-start(bf16[4,768,128]{2,1,0:T(8,128)(2,1)} %get-tuple-element.69), calls=%async_computation | async-start | bytes 1572864 | tf_op jit(solution)/shard_map/all_to_all | solution.py:846
  9.6 1.6 collective-permute-start
  11.2 3.3 %collective-permute-start.1 = (bf16[2,16,512]{2,1,0:T(8,128)(2,1)S(1)}, bf16[2,16,512]{2,1,0:T(8,128)(2,1)S(1)}, u32[]{:S(2)}, u32[]{:S(2)}) collective-permute-start(bf16[2,16,512]{2,1,0:T(8,128)(2,1)S(1)} %slice.85), channel_id=1, source_target_pairs={{0,28},{4,0},{8,4},{12,8},{16,12},{20,16},{24,20},{28,24},{1,29},{... | collective-permute-start | bytes 98312 | tf_op jit(solution)/shard_map/ppermute | solution.py:813
  14.9 8.2 %collective-permute-done.1.refs_4_.refs_16_ = bf16[2,16,512]{2,1,0:T(8,128)(2,1)S(1)} collective-permute-done((bf16[2,16,512]{2,1,0:T(8,128)(2,1)S(1)}, bf16[2,16,512]{2,1,0:T(8,128)(2,1)S(1)}, u32[]{:S(2)}, u32[]{:S(2)}) %collective-permute-start.1) | collective-permute-done | bytes 32800 | tf_op jit(solution)/shard_map/ppermute | solution.py:813
  23.1 7.2 %collective-permute-done.refs_3_.refs_15_ = bf16[2,64,512]{2,1,0:T(8,128)(2,1)S(1)} collective-permute-done((bf16[2,64,512]{2,1,0:T(8,128)(2,1)S(1)}, bf16[2,64,512]{2,1,0:T(8,128)(2,1)S(1)}, u32[]{:S(2)}, u32[]{:S(2)}) %collective-permute-start) | collective-permute-done | bytes 131104 | tf_op jit(solution)/shard_map/ppermute | solution.py:813
  30.3 5.0 %all-to-all-start.1 = ((bf16[4,768,128]{2,1,0:T(8,128)(2,1)}), bf16[4,768,128]{2,1,0:T(8,128)(2,1)S(1)}, u32[]{:S(2)}, u32[]{:S(2)}) async-start(bf16[4,768,128]{2,1,0:T(8,128)(2,1)} %get-tuple-element.75), calls=%async_computation.1 | async-start | bytes 1572864 | tf_op jit(solution)/shard_map/all_to_all | solution.py:846
  35.3 1.5 collective-permute-start.2
  36.8 2.3 collective-permute-start.3
  39.1 16.5 %collective-permute-done.2.refs_10_.refs_21_ = bf16[4,768,128]{2,1,0:T(8,128)(2,1)S(1)} collective-permute-done((bf16[4,768,128]{2,1,0:T(8,128)(2,1)S(1)}, bf16[4,768,128]{2,1,0:T(8,128)(2,1)S(1)}, u32[]{:S(2)}, u32[]{:S(2)}) %collective-permute-start.2) | collective-permute-done | bytes 786464 | tf_op jit(solution)/shard_map/ppermute | solution.py:823
  55.6 1.5 collective-permute-start.4
  57.6 10.0 %collective-permute-done.4.refs_12_.refs_23_ = bf16[4,768,128]{2,1,0:T(8,128)(2,1)S(1)} collective-permute-done((bf16[4,768,128]{2,1,0:T(8,128)(2,1)S(1)}, bf16[4,768,128]{2,1,0:T(8,128)(2,1)S(1)}, u32[]{:S(2)}, u32[]{:S(2)}) %collective-permute-start.4) | collective-permute-done | bytes 786464 | tf_op jit(solution)/shard_map/ppermute | solution.py:823
  67.6 1.5 collective-permute-start.11
  69.1 1.5 collective-permute-start.12
  70.6 9.8 %shard_map.170 = (bf16[416,512]{1,0:T(8,128)(2,1)S(1)}, bf16[416,1536]{1,0:T(8,128)(2,1)S(1)}, bf16[8,192,288]{2,1,0:T(8,128)(2,1)S(1)}, bf16[288,512]{1,0:T(8,1...) custom-call(s32[18]{0:T(128)S(1)} %stack.65.refs_0_, ...), custom_call_target="tpu_custom_call" | custom-call | flops 9663676416 | bytes 6291456 | tf_op jit(solution)/shard_map/pallas_call | solution.py:886
  81.3 4.0 %collective-permute-start.10 = (bf16[2,16,512]{2,1,0:T(8,128)(2,1)S(1)}, bf16[2,16,512]{2,1,0:T(8,128)(2,1)S(1)}, u32[]{:S(2)}, u32[]{:S(2)}) collective-permute-start(bf16[2,16,512]{2,1,0:T(8,128)(2,1)S(1)} %get-tuple-element.79), channel_id=1, source_target_pairs={{0,28},{4,0},{8,4},{12,8},{16,12},{20,16},{24,20},{28,24},{1,29},{... | collective-permute-start | bytes 98312 | tf_op jit(solution)/shard_map/ppermute | solution.py:813
  85.2 2.1 collective-permute-done.11.refs_13_
  87.3 2.7 %collective-permute-done.12.refs_14_ = bf16[4,768,128]{2,1,0:T(8,128)(2,1)S(1)} collective-permute-done((bf16[4,768,128]{2,1,0:T(8,128)(2,1)S(1)}, bf16[4,768,128]{2,1,0:T(8,128)(2,1)S(1)}, u32[]{:S(2)}, u32[]{:S(2)}) %collective-permute-start.12) | collective-permute-done | bytes 786464 | tf_op jit(solution)/shard_map/ppermute | solution.py:823
  90.4 1.5 collective-permute-start.13
  92.4 10.0 %collective-permute-done.13.refs_15_ = bf16[4,768,128]{2,1,0:T(8,128)(2,1)S(1)} collective-permute-done((bf16[4,768,128]{2,1,0:T(8,128)(2,1)S(1)}, bf16[4,768,128]{2,1,0:T(8,128)(2,1)S(1)}, u32[]{:S(2)}, u32[]{:S(2)}) %collective-permute-start.13) | collective-permute-done | bytes 786464 | tf_op jit(solution)/shard_map/ppermute | solution.py:823
  102.4 2.3 collective-permute-done.17.refs_19_
  104.7 18.5 %shard_map.171 = (f32[2,128,512]{2,1,0:T(8,128)}, f32[256,512]{1,0:T(8,128)S(1)}, f32[256,512]{1,0:T(8,128)S(1)}, f32[16,512]{1,0:T(8,128)S(1)}, bf16[2,48,512]{...) custom-call(s32[18]{0:T(128)S(1)} %stack.65.refs_0_, ...), custom_call_target="tpu_custom_call" | custom-call | flops 24159191040 | bytes 12582912 | tf_op jit(solution)/shard_map/pallas_call | solution.py:886
  123.3 3.7 %collective-permute-start.19 = (bf16[2,48,512]{2,1,0:T(8,128)(2,1)S(1)}, bf16[2,48,512]{2,1,0:T(8,128)(2,1)S(1)}, u32[]{:S(2)}, u32[]{:S(2)}) collective-permute-start(bf16[2,48,512]{2,1,0:T(8,128)(2,1)S(1)} %get-tuple-element.91), channel_id=1, source_target_pairs={{0,28},{4,0},{8,4},{12,8},{16,12},{20,16},{24,20},{28,24},{1,29},{... | collective-permute-start | bytes 294920 | tf_op jit(solution)/shard_map/ppermute | solution.py:813
  127.0 1.9 collective-permute-done.18
  129.3 1.3 copy-done.11
  130.6 1.5 collective-permute-start.21
  132.1 1.5 collective-permute-done.20.refs_6_
  133.6 15.1 %shard_map.172 = (f32[256,512]{1,0:T(8,128)S(1)}, f32[256,512]{1,0:T(8,128)S(1)}, f32[16,512]{1,0:T(8,128)S(1)}, bf16[2,48,512]{2,1,0:T(8,128)(2,1)S(1)}, bf16[2...) custom-call(s32[18]{0:T(128)S(1)} %stack.65.refs_0_, ...), custom_call_target="tpu_custom_call" | custom-call | flops 22548578304 | bytes 12582912 | tf_op jit(solution)/shard_map/pallas_call | solution.py:886
  148.8 2.2 collective-permute-done.21
  151.0 3.6 %collective-permute-start.23 = (bf16[2,48,512]{2,1,0:T(8,128)(2,1)S(1)}, bf16[2,48,512]{2,1,0:T(8,128)(2,1)S(1)}, u32[]{:S(2)}, u32[]{:S(2)}) collective-permute-start(bf16[2,48,512]{2,1,0:T(8,128)(2,1)S(1)} %get-tuple-element.106), channel_id=1, source_target_pairs={{0,28},{4,0},{8,4},{12,8},{16,12},{20,16},{24,20},{28,24},{1,29},{... | collective-permute-start | bytes 294920 | tf_op jit(solution)/shard_map/ppermute | solution.py:813
  154.6 3.2 %fusion = bf16[4,1536,128]{2,1,0:T(8,128)(2,1)} fusion(bf16[4,1536,128]{2,1,0:T(8,128)(2,1)S(1)} %collective-permute-done.21, bf16[2,4,1536,128]{3,2,1,0:T(8,128)(2,1)} %copy-done.11, bf16[2,4,1536,128]{3,2,1,0:T(8,128)(2,1)S(1)} %get-tuple-element.87), kind=kLoop, calls=%fused_computation.2 | loop fusion | flops 4718592 | bytes 6291456 | tf_op jit(solution)/shard_map/convert_element_type | solution.py:861
  157.8 2.0 fusion.1
  159.8 1.5 collective-permute-done.24.refs_5_
  161.3 5.4 %all-to-all-start.2 = ((bf16[4,1536,128]{2,1,0:T(8,128)(2,1)}), bf16[4,1536,128]{2,1,0:T(8,128)(2,1)S(1)}, u32[]{:S(2)}, u32[]{:S(2)}) async-start(bf16[4,1536,128]{2,1,0:T(8,128)(2,1)} %fusion), calls=%async_computation.2 | async-start | bytes 3145728 | tf_op jit(solution)/shard_map/all_to_all | solution.py:846
  166.6 15.9 %collective-permute-done.25 = bf16[2,3168,128]{2,1,0:T(8,128)(2,1)} collective-permute-done((bf16[2,3168,128]{2,1,0:T(8,128)(2,1)}, bf16[2,3168,128]{2,1,0:T(8,128)(2,1)}, u32[]{:S(2)}, u32[]{:S(2)}) %collective-permute-start.25) | collective-permute-done | bytes 1622048 | tf_op jit(solution)/shard_map/ppermute | solution.py:823
  182.5 1.9 fusion.3
  184.5 1.6 collective-permute-start.26
  186.0 10.8 %collective-permute-done.26 = bf16[3168,128]{1,0:T(8,128)(2,1)S(1)} collective-permute-done((bf16[3168,128]{1,0:T(8,128)(2,1)S(1)}, bf16[3168,128]{1,0:T(8,128)(2,1)S(1)}, u32[]{:S(2)}, u32[]{:S(2)}) %collective-permute-start.26) | collective-permute-done | bytes 811040 | tf_op jit(solution)/shard_map/ppermute | solution.py:823
  196.8 2.1 add_convert_fusion.2
  199.0 1.0 pad_maximum_fusion
  200.0 2.9 %all-to-all-done.2.refs_0_ = bf16[4,1536,128]{2,1,0:T(8,128)(2,1)S(1)} async-done(((bf16[4,1536,128]{2,1,0:T(8,128)(2,1)}), bf16[4,1536,128]{2,1,0:T(8,128)(2,1)S(1)}, u32[]{:S(2)}, u32[]{:S(2)}) %all-to-all-start.2) | async-done | bytes 1572896 | tf_op jit(solution)/shard_map/all_to_all | solution.py:846
  202.9 3.5 %all-to-all-start.3 = ((bf16[4,864,128]{2,1,0:T(8,128)(2,1)}), bf16[4,864,128]{2,1,0:T(8,128)(2,1)S(1)}, u32[]{:S(2)}, u32[]{:S(2)}) async-start(bf16[4,864,128]{2,1,0:T(8,128)(2,1)} %pad_maximum_fusion), calls=%async_computation.3 | async-start | bytes 1769472 | tf_op jit(solution)/shard_map/all_to_all | solution.py:846
  207.2 1.0 copy-done.3
  208.2 1.2 shard_map.173
  209.4 2.9 %collective-permute-done.27.refs_1_ = bf16[1,768,128]{2,1,0:T(8,128)(2,1)S(1)} collective-permute-done((bf16[1,768,128]{2,1,0:T(8,128)(2,1)S(1)}, bf16[1,768,128]{2,1,0:T(8,128)(2,1)S(1)}, u32[]{:S(2)}, u32[]{:S(2)}) %collective-permute-start.27) | collective-permute-done | bytes 196640 | tf_op jit(solution)/shard_map/ppermute | solution.py:823
  212.3 0.9 shard_map.174
  213.2 14.9 %all-to-all-done.3.refs_0_ = bf16[4,864,128]{2,1,0:T(8,128)(2,1)S(1)} async-done(((bf16[4,864,128]{2,1,0:T(8,128)(2,1)}), bf16[4,864,128]{2,1,0:T(8,128)(2,1)S(1)}, u32[]{:S(2)}, u32[]{:S(2)}) %all-to-all-start.3) | async-done | bytes 884768 | tf_op jit(solution)/shard_map/all_to_all | solution.py:846
  228.1 1.5 shard_map.175
  (68 shorter events, 4.0 us)
Async XLA Ops:
  0.6 9.0 %copy-start.1 = (bf16[2,1,128,512]{3,2,1,0:T(8,128)(2,1)S(1)}, bf16[2,1,128,512]{3,2,1,0:T(8,128)(2,1)}, u32[]{:S(2)}) copy-start(bf16[2,1,128,512]{3,2,1,0:T(8,128)(2,1)} %param.10) | copy-start | bytes 786436
  0.7 13.9 %copy-start.4 = (f32[2,6,512]{2,0,1:T(2,128)S(1)}, f32[2,6,512]{2,0,1:T(2,128)}, u32[]{:S(2)}) copy-start(f32[2,6,512]{2,0,1:T(2,128)} %param.18) | copy-start | bytes 73732
  0.7 14.0 %copy-start.12 = (s32[2,1,4]{2,1,0:T(1,128)S(1)}, s32[2,1,4]{2,1,0:T(1,128)}, u32[]{:S(2)}) copy-start(s32[2,1,4]{2,1,0:T(1,128)} %param.11) | copy-start | bytes 100
  3.1 67.5 %copy-start.5 = (f32[2,2,512]{2,1,0:T(2,128)S(1)}, f32[2,2,512]{2,1,0:T(2,128)}, u32[]{:S(2)}) copy-start(f32[2,2,512]{2,1,0:T(2,128)} %refs_6_.1) | copy-start | bytes 24580
  3.1 67.5 %copy-start.9 = (f32[2,2048]{1,0:T(2,128)S(1)}, f32[2,2048]{1,0:T(2,128)}, u32[]{:S(2)}) copy-start(f32[2,2048]{1,0:T(2,128)} %refs_10_.1) | copy-start | bytes 49156
  3.1 27.2 %all-to-all-start = ((bf16[4,768,128]{2,1,0:T(8,128)(2,1)}), bf16[4,768,128]{2,1,0:T(8,128)(2,1)S(1)}, u32[]{:S(2)}, u32[]{:S(2)}) async-start(bf16[4,768,128]{2,1,0:T(8,128)(2,1)} %get-tuple-element.69), calls=%async_computation | async-start | bytes 1572864 | tf_op jit(solution)/shard_map/all_to_all | solution.py:846
  9.6 20.7 %collective-permute-start = (bf16[2,64,512]{2,1,0:T(8,128)(2,1)S(1)}, bf16[2,64,512]{2,1,0:T(8,128)(2,1)S(1)}, u32[]{:S(2)}, u32[]{:S(2)}) collective-permute-start(bf16[2,64,512]{2,1,0:T(8,128)(2,1)S(1)} %slice.84), channel_id=1, source_target_pairs={{0,4},{4,8},{8,12},{12,16},{16,20},{20,24},{24,28},{28,0},{1,5},{5... | collective-permute-start | bytes 393224 | tf_op jit(solution)/shard_map/ppermute | solution.py:813
  11.2 11.9 %collective-permute-start.1 = (bf16[2,16,512]{2,1,0:T(8,128)(2,1)S(1)}, bf16[2,16,512]{2,1,0:T(8,128)(2,1)S(1)}, u32[]{:S(2)}, u32[]{:S(2)}) collective-permute-start(bf16[2,16,512]{2,1,0:T(8,128)(2,1)S(1)} %slice.85), channel_id=1, source_target_pairs={{0,28},{4,0},{8,4},{12,8},{16,12},{20,16},{24,20},{28,24},{1,29},{... | collective-permute-start | bytes 98312 | tf_op jit(solution)/shard_map/ppermute | solution.py:813
  30.3 50.1 %copy-start.7 = (bf16[2,64,512]{2,1,0:T(8,128)(2,1)}, bf16[2,64,512]{2,1,0:T(8,128)(2,1)S(1)}, u32[]{:S(2)}) copy-start(bf16[2,64,512]{2,1,0:T(8,128)(2,1)S(1)} %collective-permute-done.refs_3_.refs_15_) | copy-start | bytes 393220
  30.3 25.3 %all-to-all-start.1 = ((bf16[4,768,128]{2,1,0:T(8,128)(2,1)}), bf16[4,768,128]{2,1,0:T(8,128)(2,1)S(1)}, u32[]{:S(2)}, u32[]{:S(2)}) async-start(bf16[4,768,128]{2,1,0:T(8,128)(2,1)} %get-tuple-element.75), calls=%async_computation.1 | async-start | bytes 1572864 | tf_op jit(solution)/shard_map/all_to_all | solution.py:846
  35.3 20.3 %collective-permute-start.2 = (bf16[4,768,128]{2,1,0:T(8,128)(2,1)S(1)}, bf16[4,768,128]{2,1,0:T(8,128)(2,1)S(1)}, u32[]{:S(2)}, u32[]{:S(2)}) collective-permute-start(bf16[4,768,128]{2,1,0:T(8,128)(2,1)S(1)} %all-to-all-done.refs_9_.refs_20_), channel_id=1, source_target_pairs={{0,2},{1,5},{2,0},{3,7},{4,6},{5,1},{6,4},{7,3},{8,10},{9,13},{10,... | collective-permute-start | bytes 2359304 | tf_op jit(solution)/shard_map/ppermute | solution.py:823
  36.8 20.8 %collective-permute-start.3 = (bf16[4,768,128]{2,1,0:T(8,128)(2,1)S(1)}, bf16[4,768,128]{2,1,0:T(8,128)(2,1)}, u32[]{:S(2)}, u32[]{:S(2)}) collective-permute-start(bf16[4,768,128]{2,1,0:T(8,128)(2,1)S(1)} %all-to-all-done.refs_9_.refs_20_), channel_id=1, source_target_pairs={{0,4},{1,3},{2,6},{3,1},{4,0},{5,7},{6,2},{7,5},{8,12},{9,11},{10,... | collective-permute-start | bytes 2359304 | tf_op jit(solution)/shard_map/ppermute | solution.py:823
  55.6 12.0 %collective-permute-start.4 = (bf16[4,768,128]{2,1,0:T(8,128)(2,1)S(1)}, bf16[4,768,128]{2,1,0:T(8,128)(2,1)S(1)}, u32[]{:S(2)}, u32[]{:S(2)}) collective-permute-start(bf16[4,768,128]{2,1,0:T(8,128)(2,1)S(1)} %collective-permute-done.2.refs_10_.refs_21_), channel_id=1, source_target_pairs={{0,4},{1,3},{2,6},{3,1},{4,0},{5,7},{6,2},{7,5},{8,12},{9,11},{10,... | collective-permute-start | bytes 2359304 | tf_op jit(solution)/shard_map/ppermute | solution.py:823
  57.1 12.0 %collective-permute-start.5 = (bf16[4,768,128]{2,1,0:T(8,128)(2,1)S(1)}, bf16[4,768,128]{2,1,0:T(8,128)(2,1)S(1)}, u32[]{:S(2)}, u32[]{:S(2)}) collective-permute-start(bf16[4,768,128]{2,1,0:T(8,128)(2,1)S(1)} %all-to-all-done.refs_9_.refs_20_), channel_id=1, source_target_pairs={{0,1},{1,0},{2,3},{3,2},{4,5},{5,4},{6,7},{7,6},{8,9},{9,8},{10,11... | collective-permute-start | bytes 2359304 | tf_op jit(solution)/shard_map/ppermute | solution.py:823
  57.1 13.5 %collective-permute-start.6 = (bf16[4,768,128]{2,1,0:T(8,128)(2,1)S(1)}, bf16[4,768,128]{2,1,0:T(8,128)(2,1)S(1)}, u32[]{:S(2)}, u32[]{:S(2)}) collective-permute-start(bf16[4,768,128]{2,1,0:T(8,128)(2,1)S(1)} %collective-permute-done.2.refs_10_.refs_21_), channel_id=1, source_target_pairs={{0,1},{1,0},{2,3},{3,2},{4,5},{5,4},{6,7},{7,6},{8,9},{9,8},{10,11... | collective-permute-start | bytes 2359304 | tf_op jit(solution)/shard_map/ppermute | solution.py:823
  57.6 13.0 %collective-permute-start.7 = (bf16[4,768,128]{2,1,0:T(8,128)(2,1)}, bf16[4,768,128]{2,1,0:T(8,128)(2,1)S(1)}, u32[]{:S(2)}, u32[]{:S(2)}) collective-permute-start(bf16[4,768,128]{2,1,0:T(8,128)(2,1)} %collective-permute-done.3.refs_11_.refs_22_), channel_id=1, source_target_pairs={{0,1},{1,0},{2,3},{3,2},{4,5},{5,4},{6,7},{7,6},{8,9},{9,8},{10,11... | collective-permute-start | bytes 2359304 | tf_op jit(solution)/shard_map/ppermute | solution.py:823
  67.6 3.0 %collective-permute-start.8 = (bf16[4,768,128]{2,1,0:T(8,128)(2,1)S(1)}, bf16[4,768,128]{2,1,0:T(8,128)(2,1)S(1)}, u32[]{:S(2)}, u32[]{:S(2)}) collective-permute-start(bf16[4,768,128]{2,1,0:T(8,128)(2,1)S(1)} %collective-permute-done.4.refs_12_.refs_23_), channel_id=1, source_target_pairs={{0,1},{1,0},{2,3},{3,2},{4,5},{5,4},{6,7},{7,6},{8,9},{9,8},{10,11... | collective-permute-start | bytes 2359304 | tf_op jit(solution)/shard_map/ppermute | solution.py:823
  67.6 19.7 %collective-permute-start.11 = (bf16[4,768,128]{2,1,0:T(8,128)(2,1)S(1)}, bf16[4,768,128]{2,1,0:T(8,128)(2,1)S(1)}, u32[]{:S(2)}, u32[]{:S(2)}) collective-permute-start(bf16[4,768,128]{2,1,0:T(8,128)(2,1)S(1)} %all-to-all-done.1.refs_12_), channel_id=1, source_target_pairs={{0,2},{1,5},{2,0},{3,7},{4,6},{5,1},{6,4},{7,3},{8,10},{9,13},{10,... | collective-permute-start | bytes 2359304 | tf_op jit(solution)/shard_map/ppermute | solution.py:823
  69.1 20.9 %collective-permute-start.12 = (bf16[4,768,128]{2,1,0:T(8,128)(2,1)S(1)}, bf16[4,768,128]{2,1,0:T(8,128)(2,1)S(1)}, u32[]{:S(2)}, u32[]{:S(2)}) collective-permute-start(bf16[4,768,128]{2,1,0:T(8,128)(2,1)S(1)} %all-to-all-done.1.refs_12_), channel_id=1, source_target_pairs={{0,4},{1,3},{2,6},{3,1},{4,0},{5,7},{6,2},{7,5},{8,12},{9,11},{10,... | collective-permute-start | bytes 2359304 | tf_op jit(solution)/shard_map/ppermute | solution.py:823
  70.6 34.0 %copy-start.6 = (bf16[2,1,128,512]{3,2,1,0:T(8,128)(2,1)S(1)}, bf16[2,1,128,512]{3,2,1,0:T(8,128)(2,1)}, u32[]{:S(2)}) copy-start(bf16[2,1,128,512]{3,2,1,0:T(8,128)(2,1)} %param.12) | copy-start | bytes 786436
  80.5 9.9 %collective-permute-start.9 = (bf16[2,48,512]{2,1,0:T(8,128)(2,1)S(1)}, bf16[2,48,512]{2,1,0:T(8,128)(2,1)S(1)}, u32[]{:S(2)}, u32[]{:S(2)}) collective-permute-start(bf16[2,48,512]{2,1,0:T(8,128)(2,1)S(1)} %get-tuple-element.78), channel_id=1, source_target_pairs={{0,4},{4,8},{8,12},{12,16},{16,20},{20,24},{24,28},{28,0},{1,5},{5... | collective-permute-start | bytes 294920 | tf_op jit(solution)/shard_map/ppermute | solution.py:813
  81.3 9.1 %collective-permute-start.10 = (bf16[2,16,512]{2,1,0:T(8,128)(2,1)S(1)}, bf16[2,16,512]{2,1,0:T(8,128)(2,1)S(1)}, u32[]{:S(2)}, u32[]{:S(2)}) collective-permute-start(bf16[2,16,512]{2,1,0:T(8,128)(2,1)S(1)} %get-tuple-element.79), channel_id=1, source_target_pairs={{0,28},{4,0},{8,4},{12,8},{16,12},{20,16},{24,20},{28,24},{1,29},{... | collective-permute-start | bytes 98312 | tf_op jit(solution)/shard_map/ppermute | solution.py:813
  90.4 12.0 %collective-permute-start.13 = (bf16[4,768,128]{2,1,0:T(8,128)(2,1)S(1)}, bf16[4,768,128]{2,1,0:T(8,128)(2,1)S(1)}, u32[]{:S(2)}, u32[]{:S(2)}) collective-permute-start(bf16[4,768,128]{2,1,0:T(8,128)(2,1)S(1)} %collective-permute-done.11.refs_13_), channel_id=1, source_target_pairs={{0,4},{1,3},{2,6},{3,1},{4,0},{5,7},{6,2},{7,5},{8,12},{9,11},{10,... | collective-permute-start | bytes 2359304 | tf_op jit(solution)/shard_map/ppermute | solution.py:823
  91.9 10.5 %collective-permute-start.14 = (bf16[4,768,128]{2,1,0:T(8,128)(2,1)S(1)}, bf16[4,768,128]{2,1,0:T(8,128)(2,1)S(1)}, u32[]{:S(2)}, u32[]{:S(2)}) collective-permute-start(bf16[4,768,128]{2,1,0:T(8,128)(2,1)S(1)} %all-to-all-done.1.refs_12_), channel_id=1, source_target_pairs={{0,1},{1,0},{2,3},{3,2},{4,5},{5,4},{6,7},{7,6},{8,9},{9,8},{10,11... | collective-permute-start | bytes 2359304 | tf_op jit(solution)/shard_map/ppermute | solution.py:823
  91.9 10.5 %collective-permute-start.15 = (bf16[4,768,128]{2,1,0:T(8,128)(2,1)S(1)}, bf16[4,768,128]{2,1,0:T(8,128)(2,1)S(1)}, u32[]{:S(2)}, u32[]{:S(2)}) collective-permute-start(bf16[4,768,128]{2,1,0:T(8,128)(2,1)S(1)} %collective-permute-done.11.refs_13_), channel_id=1, source_target_pairs={{0,1},{1,0},{2,3},{3,2},{4,5},{5,4},{6,7},{7,6},{8,9},{9,8},{10,11... | collective-permute-start | bytes 2359304 | tf_op jit(solution)/shard_map/ppermute | solution.py:823
  92.4 10.0 %collective-permute-start.16 = (bf16[4,768,128]{2,1,0:T(8,128)(2,1)S(1)}, bf16[4,768,128]{2,1,0:T(8,128)(2,1)S(1)}, u32[]{:S(2)}, u32[]{:S(2)}) collective-permute-start(bf16[4,768,128]{2,1,0:T(8,128)(2,1)S(1)} %collective-permute-done.12.refs_14_), channel_id=1, source_target_pairs={{0,1},{1,0},{2,3},{3,2},{4,5},{5,4},{6,7},{7,6},{8,9},{9,8},{10,11... | collective-permute-start | bytes 2359304 | tf_op jit(solution)/shard_map/ppermute | solution.py:823
  102.4 2.3 collective-permute-start.17
  123.1 5.7 %collective-permute-start.18 = (bf16[2,4,1536,128]{3,2,1,0:T(8,128)(2,1)S(1)}, bf16[2,4,1536,128]{3,2,1,0:T(8,128)(2,1)S(1)}, u32[]{:S(2)}, u32[]{:S(2)}) collective-permute-start(bf16[2,4,1536,128]{3,2,1,0:T(8,128)(2,1)S(1)} %get-tuple-element.88), channel_id=1, source_target_pairs={{0,1},{1,0},{2,3},{3,2},{4,5},{5,4},{6,7},{7,6},{8,9},{9,8},{10,11... | collective-permute-start | bytes 9437192 | tf_op jit(solution)/shard_map/ppermute | solution.py:823
  123.3 10.3 %collective-permute-start.19 = (bf16[2,48,512]{2,1,0:T(8,128)(2,1)S(1)}, bf16[2,48,512]{2,1,0:T(8,128)(2,1)S(1)}, u32[]{:S(2)}, u32[]{:S(2)}) collective-permute-start(bf16[2,48,512]{2,1,0:T(8,128)(2,1)S(1)} %get-tuple-element.91), channel_id=1, source_target_pairs={{0,28},{4,0},{8,4},{12,8},{16,12},{20,16},{24,20},{28,24},{1,29},{... | collective-permute-start | bytes 294920 | tf_op jit(solution)/shard_map/ppermute | solution.py:813
  127.0 6.6 %collective-permute-start.20 = (bf16[2,16,512]{2,1,0:T(8,128)(2,1)S(1)}, bf16[2,16,512]{2,1,0:T(8,128)(2,1)S(1)}, u32[]{:S(2)}, u32[]{:S(2)}) collective-permute-start(bf16[2,16,512]{2,1,0:T(8,128)(2,1)S(1)} %get-tuple-element.92), channel_id=1, source_target_pairs={{0,4},{4,8},{8,12},{12,16},{16,20},{20,24},{24,28},{28,0},{1,5},{5... | collective-permute-start | bytes 98312 | tf_op jit(solution)/shard_map/ppermute | solution.py:813
  128.9 1.7 copy-start.11
  128.9 4.7 %copy-start.8 = (bf16[2,64,512]{2,1,0:T(8,128)(2,1)S(1)}, bf16[2,64,512]{2,1,0:T(8,128)(2,1)}, u32[]{:S(2)}) copy-start(bf16[2,64,512]{2,1,0:T(8,128)(2,1)} %copy-done.7) | copy-start | bytes 393220
  130.6 20.4 %collective-permute-start.21 = (bf16[4,1536,128]{2,1,0:T(8,128)(2,1)S(1)}, bf16[4,1536,128]{2,1,0:T(8,128)(2,1)S(1)}, u32[]{:S(2)}, u32[]{:S(2)}) collective-permute-start(bf16[4,1536,128]{2,1,0:T(8,128)(2,1)S(1)} %fusion.4), channel_id=1, source_target_pairs={{0,4},{1,3},{2,6},{3,1},{4,0},{5,7},{6,2},{7,5},{8,12},{9,11},{10,... | collective-permute-start | bytes 4718600 | tf_op jit(solution)/shard_map/ppermute | solution.py:823
  148.7 9.1 %copy-start.2 = (f32[256,512]{1,0:T(8,128)}, f32[256,512]{1,0:T(8,128)S(1)}, u32[]{:S(2)}) copy-start(f32[256,512]{1,0:T(8,128)S(1)} %get-tuple-element.112.refs_2_) | copy-start | bytes 1572868
  148.8 9.1 %copy-start = (bf16[2,2,3168,128]{3,2,1,0:T(8,128)(2,1)}, bf16[2,2,3168,128]{3,2,1,0:T(8,128)(2,1)S(1)}, u32[]{:S(2)}) copy-start(bf16[2,2,3168,128]{3,2,1,0:T(8,128)(2,1)S(1)} %get-tuple-element.102) | copy-start | bytes 9732100
  151.0 6.8 %collective-permute-start.22 = (bf16[2,2,3168,128]{3,2,1,0:T(8,128)(2,1)}, bf16[2,2,3168,128]{3,2,1,0:T(8,128)(2,1)S(1)}, u32[]{:S(2)}, u32[]{:S(2)}) collective-permute-start(bf16[2,2,3168,128]{3,2,1,0:T(8,128)(2,1)} %get-tuple-element.104), channel_id=1, source_target_pairs={{0,1},{1,0},{2,3},{3,2},{4,5},{5,4},{6,7},{7,6},{8,9},{9,8},{10,11... | collective-permute-start | bytes 9732104 | tf_op jit(solution)/shard_map/ppermute | solution.py:823
  151.0 10.2 %collective-permute-start.23 = (bf16[2,48,512]{2,1,0:T(8,128)(2,1)S(1)}, bf16[2,48,512]{2,1,0:T(8,128)(2,1)S(1)}, u32[]{:S(2)}, u32[]{:S(2)}) collective-permute-start(bf16[2,48,512]{2,1,0:T(8,128)(2,1)S(1)} %get-tuple-element.106), channel_id=1, source_target_pairs={{0,28},{4,0},{8,4},{12,8},{16,12},{20,16},{24,20},{28,24},{1,29},{... | collective-permute-start | bytes 294920 | tf_op jit(solution)/shard_map/ppermute | solution.py:813
  154.6 6.6 %collective-permute-start.24 = (bf16[2,16,512]{2,1,0:T(8,128)(2,1)S(1)}, bf16[2,16,512]{2,1,0:T(8,128)(2,1)S(1)}, u32[]{:S(2)}, u32[]{:S(2)}) collective-permute-start(bf16[2,16,512]{2,1,0:T(8,128)(2,1)S(1)} %get-tuple-element.107), channel_id=1, source_target_pairs={{0,4},{4,8},{8,12},{12,16},{16,20},{20,24},{24,28},{28,0},{1,5},{5... | collective-permute-start | bytes 98312 | tf_op jit(solution)/shard_map/ppermute | solution.py:813
  157.8 3.4 %copy-start.10 = (bf16[2,2,3168,128]{3,2,1,0:T(8,128)(2,1)}, bf16[2,2,3168,128]{3,2,1,0:T(8,128)(2,1)S(1)}, u32[]{:S(2)}) copy-start(bf16[2,2,3168,128]{3,2,1,0:T(8,128)(2,1)S(1)} %collective-permute-done.22) | copy-start | bytes 9732100
  161.2 21.3 %collective-permute-start.25 = (bf16[2,3168,128]{2,1,0:T(8,128)(2,1)}, bf16[2,3168,128]{2,1,0:T(8,128)(2,1)}, u32[]{:S(2)}, u32[]{:S(2)}) collective-permute-start(bf16[2,3168,128]{2,1,0:T(8,128)(2,1)} %fusion.1), channel_id=1, source_target_pairs={{0,4},{1,3},{2,6},{3,1},{4,0},{5,7},{6,2},{7,5},{8,12},{9,11},{10,... | collective-permute-start | bytes 4866056 | tf_op jit(solution)/shard_map/ppermute | solution.py:823
  161.3 41.7 %all-to-all-start.2 = ((bf16[4,1536,128]{2,1,0:T(8,128)(2,1)}), bf16[4,1536,128]{2,1,0:T(8,128)(2,1)S(1)}, u32[]{:S(2)}, u32[]{:S(2)}) async-start(bf16[4,1536,128]{2,1,0:T(8,128)(2,1)} %fusion), calls=%async_computation.2 | async-start | bytes 3145728 | tf_op jit(solution)/shard_map/all_to_all | solution.py:846
  184.5 12.3 %collective-permute-start.26 = (bf16[3168,128]{1,0:T(8,128)(2,1)S(1)}, bf16[3168,128]{1,0:T(8,128)(2,1)S(1)}, u32[]{:S(2)}, u32[]{:S(2)}) collective-permute-start(bf16[3168,128]{1,0:T(8,128)(2,1)S(1)} %fusion.3), channel_id=1, source_target_pairs={{0,2},{1,5},{2,0},{3,7},{4,6},{5,1},{6,4},{7,3},{8,10},{9,13},{10,... | collective-permute-start | bytes 2433032 | tf_op jit(solution)/shard_map/ppermute | solution.py:823
  202.9 25.2 %all-to-all-start.3 = ((bf16[4,864,128]{2,1,0:T(8,128)(2,1)}), bf16[4,864,128]{2,1,0:T(8,128)(2,1)S(1)}, u32[]{:S(2)}, u32[]{:S(2)}) async-start(bf16[4,864,128]{2,1,0:T(8,128)(2,1)} %pad_maximum_fusion), calls=%async_computation.3 | async-start | bytes 1769472 | tf_op jit(solution)/shard_map/all_to_all | solution.py:846
  206.6 5.7 %collective-permute-start.27 = (bf16[1,768,128]{2,1,0:T(8,128)(2,1)S(1)}, bf16[1,768,128]{2,1,0:T(8,128)(2,1)S(1)}, u32[]{:S(2)}, u32[]{:S(2)}) collective-permute-start(bf16[1,768,128]{2,1,0:T(8,128)(2,1)S(1)} %bitcast.78), channel_id=1, source_target_pairs={{0,2},{1,5},{2,0},{3,7},{4,6},{5,1},{6,4},{7,3},{8,10},{9,13},{10,... | collective-permute-start | bytes 589832 | tf_op jit(solution)/shard_map/ppermute | solution.py:823
  207.2 1.0 copy-start.3

commit v2 on v1

--- a/solution.py
+++ b/solution.py
@@ -595,12 +595,7 @@
     if spots is not None:
         rows = mats.attn_rows + mats.ffn_rows
         outs_to = [
-            [
-                ref.at[hop2, :, pl.ds(hop1 * rows, rows), :]
-                for ref in hbm_out
-                for hop2 in range(2)
-                for hop1 in range(2)
-            ]
+            [ref.at[:, pl.ds(hop1 * rows, rows), :] for ref in hbm_out for hop1 in range(2)]
         ]
     wide = sizes.width
     attn_copies = start_in(attn_pairs(mats, spots, groups, qkv_ref, out_ref, place_ref), sems, 0)
@@ -973,7 +968,7 @@
         first_all = both_cores(sides0 + [across_second(after(sides0[1], sides1[0]))])
         classes = len(first_all) // 2
         grad_outs0 = [((2, 2, CHIPS_Z * all_rows + SMALL_ROWS, LANES), BF16)] * 2
-        grad_outs1 = [((2, CHIPS_Z, 2 * all_rows, LANES), BF16)] * 2
+        grad_outs1 = [((CHIPS_Z, 2 * all_rows, LANES), BF16)] * 4
         copies_in = len(first_all) * (3 + mats.down_parts)
     else:
         whole = []
@@ -1027,7 +1022,7 @@
          row_biases[0]) + tuple(first_all),
         flops=24 * own * (4 * width * width + 2 * width * ff) // 2,
         moved=2 * (4 * width * width + 2 * width * ff),
-        vmem=24,
+        vmem=20,
     )
     left1 = shifted(send_right, "seg", 1)
     right1 = shifted(send_left, "seg", -1)
@@ -1072,7 +1067,7 @@
          row_biases[1]) + tuple(last_all),
         flops=30 * own * (4 * width * width + 2 * width * ff),
         moved=4 * (4 * width * width + 2 * width * ff),
-        vmem=34,
+        vmem=26,
     )
     encoded, gz1, gh1, gmem1, back_left1, back_right1, vec1 = outs[:7]
     grad_blocks1 = outs[7:]
@@ -1081,9 +1076,10 @@
 
     gh1_tied = gh1
     if by_blocks:
-        mine1, theirs1 = grad_blocks1[0], other_core(grad_blocks1[1])
-        far1 = summed(mine1[1], theirs1[1])
-        gh1_tied = after(gh1, far1)
+        near1, far1, near1_other, far1_other = grad_blocks1
+        far1 = summed(far1, other_core(far1_other))
+        near1_theirs = other_core(near1_other)
+        gh1_tied = after(gh1, far1, near1_theirs)
     gz0, gh0, gmem0, back_left0, back_right0, upper_vec, vec0, *grad_blocks0 = call(
         lambda *refs: first_back_kernel(
             last, first, seqs, mats, spots, len(first_all), len(grad_outs0), *refs
@@ -1119,7 +1115,7 @@
         + tuple(first_all),
         flops=28 * own * (4 * width * width + 2 * width * ff),
         moved=4 * (4 * width * width + 2 * width * ff),
-        vmem=34,
+        vmem=28,
     )
     from_right0 = shifted(back_left0, "seg", -1)
     from_left0 = shifted(back_right0, "seg", 1)
@@ -1127,7 +1123,7 @@
     if by_blocks:
         second1 = across_second(far1)
         mine0, theirs0 = grad_blocks0[0], other_core(after(grad_blocks0[1], second1))
-        both1 = summed(mine1[0], theirs1[0], second1)
+        both1 = summed(near1, near1_theirs, second1)
         lines1 = swap_z(both1)
         far0 = summed(mine0[1], after(theirs0, both1)[1])
         far0 = after(far0, from_right0, from_left0)

time: 230 us -> 228 us (level)
    ppermute x20 -> x21, waiting for transfers between devices: 77.2 us -> 75.5 us  [permuted(): return lax.ppermute(value, ('seg', 'rep'), pairs)]
    ppermute x20 -> x21, starting transfers between devices: 14.6 us -> 14 us  [permuted(): return lax.ppermute(value, ('seg', 'rep'), pairs)]
  transfers between devices with their start and end apart: 32 -> 33, of which waited for: 18 -> 16; matrix products, arithmetic and copies ran while one was open for 5% -> 4% of each run, Pallas kernels for 12% -> 12%
where the time goes in v2:
time: 228 us; the launch traced here: 227 us
  waiting for transfers between devices  112 us (49%)
  starting transfers between devices  53.4 us (23%)
  Pallas kernels  49.4 us (22%)
  other arithmetic  9.51 us (4%)
    ppermute x21, waiting for transfers between devices, permuted(): return lax.ppermute(value, ('seg', 'rep'), pairs)  75.5 us
    pallas_call x7, Pallas kernels, call(): pl.pallas_call(body, grid=grid, input_output_aliases=aliases, in_specs=in...  49.4 us
    all_to_all x4, starting transfers between devices, swap_z(): lax.all_to_all(blocks, 'seg', 0, 0, axis_index_groups=groups, tiled=True)  20.4 us
    ppermute x8, starting transfers between devices, shifted(): lax.ppermute(value, axis, [(i, (i + by) % size) for i in range(size)])  19.1 us
    all_to_all x4, waiting for transfers between devices, swap_z(): lax.all_to_all(blocks, 'seg', 0, 0, axis_index_groups=groups, tiled=True)  18.8 us
    ppermute x8, waiting for transfers between devices, shifted(): lax.ppermute(value, axis, [(i, (i + by) % size) for i in range(size)])  18 us
    ppermute x21, starting transfers between devices, permuted(): return lax.ppermute(value, ('seg', 'rep'), pairs)  14 us
    convert_element_type x5, other arithmetic, summed(): return total.astype(BF16)  8.2 us
  transfers between devices with their start and end apart: 33, of which 16 were waited for; matrix products, arithmetic and copies ran while one was open for 4% of the time, Pallas kernels for 12%

profile of v2, /device:TPU:0, one launch (start us, length us, event | category | flops | bytes accessed | tf_op | source)
XLA Modules:
  0.0 227.4 jit_solution(2340732452958095142)
XLA Ops:
  0.7 2.5 %shard_map.169 = (bf16[4,768,128]{2,1,0:T(8,128)(2,1)}, bf16[4,768,128]{2,1,0:T(8,128)(2,1)}) custom-call(bf16[2,192,128]{2,1,0:T(8,128)(2,1)} %bitcast.74, bf16[2,64,128]{2,1,0:T(8,128)(2,1)} %bitcast.76, bf16[2,128,256]{2,1,0:T(8,128)(2,1)} %refs_2_.1, bf16[2,64,512]{2,1,0:T(8,128)(2,1)} %bitcast.73), custom_call_target="tpu_custom_call" | custom-call | tf_op jit(solution)/shard_map/pallas_call | solution.py:881
  3.1 6.5 %all-to-all-start = ((bf16[4,768,128]{2,1,0:T(8,128)(2,1)}), bf16[4,768,128]{2,1,0:T(8,128)(2,1)S(1)}, u32[]{:S(2)}, u32[]{:S(2)}) async-start(bf16[4,768,128]{2,1,0:T(8,128)(2,1)} %get-tuple-element.71), calls=%async_computation | async-start | bytes 1572864 | tf_op jit(solution)/shard_map/all_to_all | solution.py:841
  9.6 4.8 %collective-permute-start.1 = (bf16[2,16,512]{2,1,0:T(8,128)(2,1)S(1)}, bf16[2,16,512]{2,1,0:T(8,128)(2,1)S(1)}, u32[]{:S(2)}, u32[]{:S(2)}) collective-permute-start(bf16[2,16,512]{2,1,0:T(8,128)(2,1)S(1)} %slice.69), channel_id=1, source_target_pairs={{0,28},{4,0},{8,4},{12,8},{16,12},{20,16},{24,20},{28,24},{1,29},{... | collective-permute-start | bytes 98312 | tf_op jit(solution)/shard_map/ppermute | solution.py:808
  14.9 8.2 %collective-permute-done.1.refs_4_.refs_16_ = bf16[2,16,512]{2,1,0:T(8,128)(2,1)S(1)} collective-permute-done((bf16[2,16,512]{2,1,0:T(8,128)(2,1)S(1)}, bf16[2,16,512]{2,1,0:T(8,128)(2,1)S(1)}, u32[]{:S(2)}, u32[]{:S(2)}) %collective-permute-start.1) | collective-permute-done | bytes 32800 | tf_op jit(solution)/shard_map/ppermute | solution.py:808
  23.1 7.2 %collective-permute-done.refs_3_.refs_15_ = bf16[2,64,512]{2,1,0:T(8,128)(2,1)S(1)} collective-permute-done((bf16[2,64,512]{2,1,0:T(8,128)(2,1)S(1)}, bf16[2,64,512]{2,1,0:T(8,128)(2,1)S(1)}, u32[]{:S(2)}, u32[]{:S(2)}) %collective-permute-start) | collective-permute-done | bytes 131104 | tf_op jit(solution)/shard_map/ppermute | solution.py:808
  30.3 5.0 %all-to-all-start.1 = ((bf16[4,768,128]{2,1,0:T(8,128)(2,1)}), bf16[4,768,128]{2,1,0:T(8,128)(2,1)S(1)}, u32[]{:S(2)}, u32[]{:S(2)}) async-start(bf16[4,768,128]{2,1,0:T(8,128)(2,1)} %get-tuple-element.77), calls=%async_computation.1 | async-start | bytes 1572864 | tf_op jit(solution)/shard_map/all_to_all | solution.py:841
  35.3 1.5 collective-permute-start.2
  36.8 2.3 %collective-permute-start.3 = (bf16[4,768,128]{2,1,0:T(8,128)(2,1)S(1)}, bf16[4,768,128]{2,1,0:T(8,128)(2,1)}, u32[]{:S(2)}, u32[]{:S(2)}) collective-permute-start(bf16[4,768,128]{2,1,0:T(8,128)(2,1)S(1)} %all-to-all-done.refs_9_.refs_20_), channel_id=1, source_target_pairs={{0,4},{1,3},{2,6},{3,1},{4,0},{5,7},{6,2},{7,5},{8,12},{9,11},{10,... | collective-permute-start | bytes 2359304 | tf_op jit(solution)/shard_map/ppermute | solution.py:818
  39.1 16.5 %collective-permute-done.2.refs_10_.refs_21_ = bf16[4,768,128]{2,1,0:T(8,128)(2,1)S(1)} collective-permute-done((bf16[4,768,128]{2,1,0:T(8,128)(2,1)S(1)}, bf16[4,768,128]{2,1,0:T(8,128)(2,1)S(1)}, u32[]{:S(2)}, u32[]{:S(2)}) %collective-permute-start.2) | collective-permute-done | bytes 786464 | tf_op jit(solution)/shard_map/ppermute | solution.py:818
  55.6 1.5 collective-permute-start.4
  57.1 0.5 collective-permute-start.6
  57.6 10.0 %collective-permute-done.4.refs_12_.refs_23_ = bf16[4,768,128]{2,1,0:T(8,128)(2,1)S(1)} collective-permute-done((bf16[4,768,128]{2,1,0:T(8,128)(2,1)S(1)}, bf16[4,768,128]{2,1,0:T(8,128)(2,1)S(1)}, u32[]{:S(2)}, u32[]{:S(2)}) %collective-permute-start.4) | collective-permute-done | bytes 786464 | tf_op jit(solution)/shard_map/ppermute | solution.py:818
  67.6 1.5 collective-permute-start.12
  69.1 1.5 collective-permute-start.11
  70.6 9.8 %shard_map.170 = (bf16[416,512]{1,0:T(8,128)(2,1)S(1)}, bf16[416,1536]{1,0:T(8,128)(2,1)S(1)}, bf16[8,192,288]{2,1,0:T(8,128)(2,1)S(1)}, bf16[288,512]{1,0:T(8,1...) custom-call(s32[18]{0:T(128)S(1)} %stack.65.refs_0_, ...), custom_call_target="tpu_custom_call" | custom-call | flops 9663676416 | bytes 6291456 | tf_op jit(solution)/shard_map/pallas_call | solution.py:881
  80.4 0.8 collective-permute-start.9
  81.2 4.0 %collective-permute-start.10 = (bf16[2,16,512]{2,1,0:T(8,128)(2,1)S(1)}, bf16[2,16,512]{2,1,0:T(8,128)(2,1)S(1)}, u32[]{:S(2)}, u32[]{:S(2)}) collective-permute-start(bf16[2,16,512]{2,1,0:T(8,128)(2,1)S(1)} %get-tuple-element.81), channel_id=1, source_target_pairs={{0,28},{4,0},{8,4},{12,8},{16,12},{20,16},{24,20},{28,24},{1,29},{... | collective-permute-start | bytes 98312 | tf_op jit(solution)/shard_map/ppermute | solution.py:808
  85.2 4.2 %collective-permute-done.12.refs_14_ = bf16[4,768,128]{2,1,0:T(8,128)(2,1)S(1)} collective-permute-done((bf16[4,768,128]{2,1,0:T(8,128)(2,1)S(1)}, bf16[4,768,128]{2,1,0:T(8,128)(2,1)S(1)}, u32[]{:S(2)}, u32[]{:S(2)}) %collective-permute-start.12) | collective-permute-done | bytes 786464 | tf_op jit(solution)/shard_map/ppermute | solution.py:818
  89.4 0.7 collective-permute-done.10.refs_4_
  90.1 1.5 collective-permute-start.13
  92.3 9.8 %collective-permute-done.13.refs_15_ = bf16[4,768,128]{2,1,0:T(8,128)(2,1)S(1)} collective-permute-done((bf16[4,768,128]{2,1,0:T(8,128)(2,1)S(1)}, bf16[4,768,128]{2,1,0:T(8,128)(2,1)S(1)}, u32[]{:S(2)}, u32[]{:S(2)}) %collective-permute-start.13) | collective-permute-done | bytes 786464 | tf_op jit(solution)/shard_map/ppermute | solution.py:818
  102.1 2.3 collective-permute-done.17.refs_19_
  104.4 18.4 %shard_map.171 = (f32[2,128,512]{2,1,0:T(8,128)}, f32[256,512]{1,0:T(8,128)S(1)}, f32[256,512]{1,0:T(8,128)S(1)}, f32[16,512]{1,0:T(8,128)S(1)}, bf16[2,48,512]{...) custom-call(s32[18]{0:T(128)S(1)} %stack.65.refs_0_, ...), custom_call_target="tpu_custom_call" | custom-call | flops 24159191040 | bytes 12582912 | tf_op jit(solution)/shard_map/pallas_call | solution.py:881
  123.4 1.5 collective-permute-start.21
  124.9 3.2 %collective-permute-start.20 = (bf16[2,48,512]{2,1,0:T(8,128)(2,1)S(1)}, bf16[2,48,512]{2,1,0:T(8,128)(2,1)S(1)}, u32[]{:S(2)}, u32[]{:S(2)}) collective-permute-start(bf16[2,48,512]{2,1,0:T(8,128)(2,1)S(1)} %get-tuple-element.94), channel_id=1, source_target_pairs={{0,28},{4,0},{8,4},{12,8},{16,12},{20,16},{24,20},{28,24},{1,29},{... | collective-permute-start | bytes 294920 | tf_op jit(solution)/shard_map/ppermute | solution.py:808
  128.1 0.4 add_convert_fusion.2
  128.6 1.4 collective-permute-done.21.refs_6_
  130.1 0.4 collective-permute-done.20.refs_5_
  130.5 15.1 %shard_map.172 = (f32[256,512]{1,0:T(8,128)S(1)}, f32[256,512]{1,0:T(8,128)S(1)}, f32[16,512]{1,0:T(8,128)S(1)}, bf16[2,48,512]{2,1,0:T(8,128)(2,1)S(1)}, bf16[2...) custom-call(s32[18]{0:T(128)S(1)} %stack.65.refs_0_, ...), custom_call_target="tpu_custom_call" | custom-call | flops 22548578304 | bytes 12582912 | tf_op jit(solution)/shard_map/pallas_call | solution.py:881
  145.6 3.4 %collective-permute-done.22 = bf16[4,1536,128]{2,1,0:T(8,128)(2,1)S(1)} collective-permute-done((bf16[4,1536,128]{2,1,0:T(8,128)(2,1)S(1)}, bf16[4,1536,128]{2,1,0:T(8,128)(2,1)S(1)}, u32[]{:S(2)}, u32[]{:S(2)}) %collective-permute-start.22) | collective-permute-done | bytes 1572896 | tf_op jit(solution)/shard_map/ppermute | solution.py:818
  149.4 4.4 %collective-permute-start.24 = (bf16[2,48,512]{2,1,0:T(8,128)(2,1)S(1)}, bf16[2,48,512]{2,1,0:T(8,128)(2,1)S(1)}, u32[]{:S(2)}, u32[]{:S(2)}) collective-permute-start(bf16[2,48,512]{2,1,0:T(8,128)(2,1)S(1)} %get-tuple-element.110), channel_id=1, source_target_pairs={{0,28},{4,0},{8,4},{12,8},{16,12},{20,16},{24,20},{28,24},{1,29},{... | collective-permute-start | bytes 294920 | tf_op jit(solution)/shard_map/ppermute | solution.py:808
  153.8 1.8 add_convert_fusion.1
  155.5 2.0 fusion
  157.8 5.4 %all-to-all-start.2 = ((bf16[4,1536,128]{2,1,0:T(8,128)(2,1)}), bf16[4,1536,128]{2,1,0:T(8,128)(2,1)S(1)}, u32[]{:S(2)}, u32[]{:S(2)}) async-start(bf16[4,1536,128]{2,1,0:T(8,128)(2,1)} %add_convert_fusion.1), calls=%async_computation.2 | async-start | bytes 3145728 | tf_op jit(solution)/shard_map/all_to_all | solution.py:841
  163.2 15.8 %collective-permute-done.26 = bf16[2,3168,128]{2,1,0:T(8,128)(2,1)} collective-permute-done((bf16[2,3168,128]{2,1,0:T(8,128)(2,1)}, bf16[2,3168,128]{2,1,0:T(8,128)(2,1)}, u32[]{:S(2)}, u32[]{:S(2)}) %collective-permute-start.26) | collective-permute-done | bytes 1622048 | tf_op jit(solution)/shard_map/ppermute | solution.py:818
  179.1 1.9 fusion.2
  181.0 2.1 collective-permute-start.27
  183.1 10.2 %collective-permute-done.27 = bf16[3168,128]{1,0:T(8,128)(2,1)S(1)} collective-permute-done((bf16[3168,128]{1,0:T(8,128)(2,1)S(1)}, bf16[3168,128]{1,0:T(8,128)(2,1)S(1)}, u32[]{:S(2)}, u32[]{:S(2)}) %collective-permute-start.27) | collective-permute-done | bytes 811040 | tf_op jit(solution)/shard_map/ppermute | solution.py:818
  193.3 2.1 add_convert_fusion.3
  195.6 1.0 pad_maximum_fusion
  196.6 3.9 %all-to-all-done.2.refs_0_ = bf16[4,1536,128]{2,1,0:T(8,128)(2,1)S(1)} async-done(((bf16[4,1536,128]{2,1,0:T(8,128)(2,1)}), bf16[4,1536,128]{2,1,0:T(8,128)(2,1)S(1)}, u32[]{:S(2)}, u32[]{:S(2)}) %all-to-all-start.2) | async-done | bytes 1572896 | tf_op jit(solution)/shard_map/all_to_all | solution.py:841
  200.4 3.5 %all-to-all-start.3 = ((bf16[4,864,128]{2,1,0:T(8,128)(2,1)}), bf16[4,864,128]{2,1,0:T(8,128)(2,1)S(1)}, u32[]{:S(2)}, u32[]{:S(2)}) async-start(bf16[4,864,128]{2,1,0:T(8,128)(2,1)} %pad_maximum_fusion), calls=%async_computation.3 | async-start | bytes 1769472 | tf_op jit(solution)/shard_map/all_to_all | solution.py:841
  204.4 1.0 copy-done.3
  205.4 1.2 shard_map.173
  206.6 3.2 %collective-permute-done.28.refs_1_ = bf16[1,768,128]{2,1,0:T(8,128)(2,1)S(1)} collective-permute-done((bf16[1,768,128]{2,1,0:T(8,128)(2,1)S(1)}, bf16[1,768,128]{2,1,0:T(8,128)(2,1)S(1)}, u32[]{:S(2)}, u32[]{:S(2)}) %collective-permute-start.28) | collective-permute-done | bytes 196640 | tf_op jit(solution)/shard_map/ppermute | solution.py:818
  209.8 0.9 shard_map.174
  210.7 14.9 %all-to-all-done.3.refs_0_ = bf16[4,864,128]{2,1,0:T(8,128)(2,1)S(1)} async-done(((bf16[4,864,128]{2,1,0:T(8,128)(2,1)}), bf16[4,864,128]{2,1,0:T(8,128)(2,1)S(1)}, u32[]{:S(2)}, u32[]{:S(2)}) %all-to-all-start.3) | async-done | bytes 884768 | tf_op jit(solution)/shard_map/all_to_all | solution.py:841
  225.6 1.5 shard_map.175
  (68 shorter events, 2.9 us)
Async XLA Ops:
  0.6 9.0 %copy-start.1 = (bf16[2,1,128,512]{3,2,1,0:T(8,128)(2,1)S(1)}, bf16[2,1,128,512]{3,2,1,0:T(8,128)(2,1)}, u32[]{:S(2)}) copy-start(bf16[2,1,128,512]{3,2,1,0:T(8,128)(2,1)} %param.10) | copy-start | bytes 786436
  0.7 13.8 %copy-start.4 = (f32[2,6,512]{2,0,1:T(2,128)S(1)}, f32[2,6,512]{2,0,1:T(2,128)}, u32[]{:S(2)}) copy-start(f32[2,6,512]{2,0,1:T(2,128)} %param.18) | copy-start | bytes 73732
  0.7 13.9 %copy-start.11 = (s32[2,1,4]{2,1,0:T(1,128)S(1)}, s32[2,1,4]{2,1,0:T(1,128)}, u32[]{:S(2)}) copy-start(s32[2,1,4]{2,1,0:T(1,128)} %param.11) | copy-start | bytes 100
  3.1 67.5 %copy-start.5 = (f32[2,2,512]{2,1,0:T(2,128)S(1)}, f32[2,2,512]{2,1,0:T(2,128)}, u32[]{:S(2)}) copy-start(f32[2,2,512]{2,1,0:T(2,128)} %refs_6_.1) | copy-start | bytes 24580
  3.1 67.5 %copy-start.9 = (f32[2,2048]{1,0:T(2,128)S(1)}, f32[2,2048]{1,0:T(2,128)}, u32[]{:S(2)}) copy-start(f32[2,2048]{1,0:T(2,128)} %refs_10_.1) | copy-start | bytes 49156
  3.1 27.2 %all-to-all-start = ((bf16[4,768,128]{2,1,0:T(8,128)(2,1)}), bf16[4,768,128]{2,1,0:T(8,128)(2,1)S(1)}, u32[]{:S(2)}, u32[]{:S(2)}) async-start(bf16[4,768,128]{2,1,0:T(8,128)(2,1)} %get-tuple-element.71), calls=%async_computation | async-start | bytes 1572864 | tf_op jit(solution)/shard_map/all_to_all | solution.py:841
  9.6 13.5 %collective-permute-start.1 = (bf16[2,16,512]{2,1,0:T(8,128)(2,1)S(1)}, bf16[2,16,512]{2,1,0:T(8,128)(2,1)S(1)}, u32[]{:S(2)}, u32[]{:S(2)}) collective-permute-start(bf16[2,16,512]{2,1,0:T(8,128)(2,1)S(1)} %slice.69), channel_id=1, source_target_pairs={{0,28},{4,0},{8,4},{12,8},{16,12},{20,16},{24,20},{28,24},{1,29},{... | collective-permute-start | bytes 98312 | tf_op jit(solution)/shard_map/ppermute | solution.py:808
  14.4 15.9 %collective-permute-start = (bf16[2,64,512]{2,1,0:T(8,128)(2,1)S(1)}, bf16[2,64,512]{2,1,0:T(8,128)(2,1)S(1)}, u32[]{:S(2)}, u32[]{:S(2)}) collective-permute-start(bf16[2,64,512]{2,1,0:T(8,128)(2,1)S(1)} %slice.68), channel_id=1, source_target_pairs={{0,4},{4,8},{8,12},{12,16},{16,20},{20,24},{24,28},{28,0},{1,5},{5... | collective-permute-start | bytes 393224 | tf_op jit(solution)/shard_map/ppermute | solution.py:808
  30.3 50.1 %copy-start.7 = (bf16[2,64,512]{2,1,0:T(8,128)(2,1)}, bf16[2,64,512]{2,1,0:T(8,128)(2,1)S(1)}, u32[]{:S(2)}) copy-start(bf16[2,64,512]{2,1,0:T(8,128)(2,1)S(1)} %collective-permute-done.refs_3_.refs_15_) | copy-start | bytes 393220
  30.3 25.3 %all-to-all-start.1 = ((bf16[4,768,128]{2,1,0:T(8,128)(2,1)}), bf16[4,768,128]{2,1,0:T(8,128)(2,1)S(1)}, u32[]{:S(2)}, u32[]{:S(2)}) async-start(bf16[4,768,128]{2,1,0:T(8,128)(2,1)} %get-tuple-element.77), calls=%async_computation.1 | async-start | bytes 1572864 | tf_op jit(solution)/shard_map/all_to_all | solution.py:841
  35.3 20.3 %collective-permute-start.2 = (bf16[4,768,128]{2,1,0:T(8,128)(2,1)S(1)}, bf16[4,768,128]{2,1,0:T(8,128)(2,1)S(1)}, u32[]{:S(2)}, u32[]{:S(2)}) collective-permute-start(bf16[4,768,128]{2,1,0:T(8,128)(2,1)S(1)} %all-to-all-done.refs_9_.refs_20_), channel_id=1, source_target_pairs={{0,2},{1,5},{2,0},{3,7},{4,6},{5,1},{6,4},{7,3},{8,10},{9,13},{10,... | collective-permute-start | bytes 2359304 | tf_op jit(solution)/shard_map/ppermute | solution.py:818
  36.8 20.8 %collective-permute-start.3 = (bf16[4,768,128]{2,1,0:T(8,128)(2,1)S(1)}, bf16[4,768,128]{2,1,0:T(8,128)(2,1)}, u32[]{:S(2)}, u32[]{:S(2)}) collective-permute-start(bf16[4,768,128]{2,1,0:T(8,128)(2,1)S(1)} %all-to-all-done.refs_9_.refs_20_), channel_id=1, source_target_pairs={{0,4},{1,3},{2,6},{3,1},{4,0},{5,7},{6,2},{7,5},{8,12},{9,11},{10,... | collective-permute-start | bytes 2359304 | tf_op jit(solution)/shard_map/ppermute | solution.py:818
  55.6 12.0 %collective-permute-start.4 = (bf16[4,768,128]{2,1,0:T(8,128)(2,1)S(1)}, bf16[4,768,128]{2,1,0:T(8,128)(2,1)S(1)}, u32[]{:S(2)}, u32[]{:S(2)}) collective-permute-start(bf16[4,768,128]{2,1,0:T(8,128)(2,1)S(1)} %collective-permute-done.2.refs_10_.refs_21_), channel_id=1, source_target_pairs={{0,4},{1,3},{2,6},{3,1},{4,0},{5,7},{6,2},{7,5},{8,12},{9,11},{10,... | collective-permute-start | bytes 2359304 | tf_op jit(solution)/shard_map/ppermute | solution.py:818
  57.1 12.0 %collective-permute-start.5 = (bf16[4,768,128]{2,1,0:T(8,128)(2,1)S(1)}, bf16[4,768,128]{2,1,0:T(8,128)(2,1)S(1)}, u32[]{:S(2)}, u32[]{:S(2)}) collective-permute-start(bf16[4,768,128]{2,1,0:T(8,128)(2,1)S(1)} %all-to-all-done.refs_9_.refs_20_), channel_id=1, source_target_pairs={{0,1},{1,0},{2,3},{3,2},{4,5},{5,4},{6,7},{7,6},{8,9},{9,8},{10,11... | collective-permute-start | bytes 2359304 | tf_op jit(solution)/shard_map/ppermute | solution.py:818
  57.1 13.5 %collective-permute-start.6 = (bf16[4,768,128]{2,1,0:T(8,128)(2,1)S(1)}, bf16[4,768,128]{2,1,0:T(8,128)(2,1)S(1)}, u32[]{:S(2)}, u32[]{:S(2)}) collective-permute-start(bf16[4,768,128]{2,1,0:T(8,128)(2,1)S(1)} %collective-permute-done.2.refs_10_.refs_21_), channel_id=1, source_target_pairs={{0,1},{1,0},{2,3},{3,2},{4,5},{5,4},{6,7},{7,6},{8,9},{9,8},{10,11... | collective-permute-start | bytes 2359304 | tf_op jit(solution)/shard_map/ppermute | solution.py:818
  57.6 13.0 %collective-permute-start.7 = (bf16[4,768,128]{2,1,0:T(8,128)(2,1)}, bf16[4,768,128]{2,1,0:T(8,128)(2,1)S(1)}, u32[]{:S(2)}, u32[]{:S(2)}) collective-permute-start(bf16[4,768,128]{2,1,0:T(8,128)(2,1)} %collective-permute-done.3.refs_11_.refs_22_), channel_id=1, source_target_pairs={{0,1},{1,0},{2,3},{3,2},{4,5},{5,4},{6,7},{7,6},{8,9},{9,8},{10,11... | collective-permute-start | bytes 2359304 | tf_op jit(solution)/shard_map/ppermute | solution.py:818
  67.6 3.0 %collective-permute-start.8 = (bf16[4,768,128]{2,1,0:T(8,128)(2,1)S(1)}, bf16[4,768,128]{2,1,0:T(8,128)(2,1)S(1)}, u32[]{:S(2)}, u32[]{:S(2)}) collective-permute-start(bf16[4,768,128]{2,1,0:T(8,128)(2,1)S(1)} %collective-permute-done.4.refs_12_.refs_23_), channel_id=1, source_target_pairs={{0,1},{1,0},{2,3},{3,2},{4,5},{5,4},{6,7},{7,6},{8,9},{9,8},{10,11... | collective-permute-start | bytes 2359304 | tf_op jit(solution)/shard_map/ppermute | solution.py:818
  67.6 21.8 %collective-permute-start.12 = (bf16[4,768,128]{2,1,0:T(8,128)(2,1)S(1)}, bf16[4,768,128]{2,1,0:T(8,128)(2,1)S(1)}, u32[]{:S(2)}, u32[]{:S(2)}) collective-permute-start(bf16[4,768,128]{2,1,0:T(8,128)(2,1)S(1)} %all-to-all-done.1.refs_12_), channel_id=1, source_target_pairs={{0,4},{1,3},{2,6},{3,1},{4,0},{5,7},{6,2},{7,5},{8,12},{9,11},{10,... | collective-permute-start | bytes 2359304 | tf_op jit(solution)/shard_map/ppermute | solution.py:818
  69.1 20.3 %collective-permute-start.11 = (bf16[4,768,128]{2,1,0:T(8,128)(2,1)S(1)}, bf16[4,768,128]{2,1,0:T(8,128)(2,1)S(1)}, u32[]{:S(2)}, u32[]{:S(2)}) collective-permute-start(bf16[4,768,128]{2,1,0:T(8,128)(2,1)S(1)} %all-to-all-done.1.refs_12_), channel_id=1, source_target_pairs={{0,2},{1,5},{2,0},{3,7},{4,6},{5,1},{6,4},{7,3},{8,10},{9,13},{10,... | collective-permute-start | bytes 2359304 | tf_op jit(solution)/shard_map/ppermute | solution.py:818
  70.6 33.8 %copy-start.6 = (bf16[2,1,128,512]{3,2,1,0:T(8,128)(2,1)S(1)}, bf16[2,1,128,512]{3,2,1,0:T(8,128)(2,1)}, u32[]{:S(2)}) copy-start(bf16[2,1,128,512]{3,2,1,0:T(8,128)(2,1)} %param.12) | copy-start | bytes 786436
  80.4 9.7 %collective-permute-start.9 = (bf16[2,48,512]{2,1,0:T(8,128)(2,1)S(1)}, bf16[2,48,512]{2,1,0:T(8,128)(2,1)S(1)}, u32[]{:S(2)}, u32[]{:S(2)}) collective-permute-start(bf16[2,48,512]{2,1,0:T(8,128)(2,1)S(1)} %get-tuple-element.80), channel_id=1, source_target_pairs={{0,4},{4,8},{8,12},{12,16},{16,20},{20,24},{24,28},{28,0},{1,5},{5... | collective-permute-start | bytes 294920 | tf_op jit(solution)/shard_map/ppermute | solution.py:808
  81.2 8.9 %collective-permute-start.10 = (bf16[2,16,512]{2,1,0:T(8,128)(2,1)S(1)}, bf16[2,16,512]{2,1,0:T(8,128)(2,1)S(1)}, u32[]{:S(2)}, u32[]{:S(2)}) collective-permute-start(bf16[2,16,512]{2,1,0:T(8,128)(2,1)S(1)} %get-tuple-element.81), channel_id=1, source_target_pairs={{0,28},{4,0},{8,4},{12,8},{16,12},{20,16},{24,20},{28,24},{1,29},{... | collective-permute-start | bytes 98312 | tf_op jit(solution)/shard_map/ppermute | solution.py:808
  90.1 12.0 %collective-permute-start.13 = (bf16[4,768,128]{2,1,0:T(8,128)(2,1)S(1)}, bf16[4,768,128]{2,1,0:T(8,128)(2,1)S(1)}, u32[]{:S(2)}, u32[]{:S(2)}) collective-permute-start(bf16[4,768,128]{2,1,0:T(8,128)(2,1)S(1)} %collective-permute-done.11.refs_13_), channel_id=1, source_target_pairs={{0,4},{1,3},{2,6},{3,1},{4,0},{5,7},{6,2},{7,5},{8,12},{9,11},{10,... | collective-permute-start | bytes 2359304 | tf_op jit(solution)/shard_map/ppermute | solution.py:818
  91.6 10.5 %collective-permute-start.14 = (bf16[4,768,128]{2,1,0:T(8,128)(2,1)S(1)}, bf16[4,768,128]{2,1,0:T(8,128)(2,1)S(1)}, u32[]{:S(2)}, u32[]{:S(2)}) collective-permute-start(bf16[4,768,128]{2,1,0:T(8,128)(2,1)S(1)} %all-to-all-done.1.refs_12_), channel_id=1, source_target_pairs={{0,1},{1,0},{2,3},{3,2},{4,5},{5,4},{6,7},{7,6},{8,9},{9,8},{10,11... | collective-permute-start | bytes 2359304 | tf_op jit(solution)/shard_map/ppermute | solution.py:818
  91.8 10.4 %collective-permute-start.16 = (bf16[4,768,128]{2,1,0:T(8,128)(2,1)S(1)}, bf16[4,768,128]{2,1,0:T(8,128)(2,1)S(1)}, u32[]{:S(2)}, u32[]{:S(2)}) collective-permute-start(bf16[4,768,128]{2,1,0:T(8,128)(2,1)S(1)} %collective-permute-done.12.refs_14_), channel_id=1, source_target_pairs={{0,1},{1,0},{2,3},{3,2},{4,5},{5,4},{6,7},{7,6},{8,9},{9,8},{10,11... | collective-permute-start | bytes 2359304 | tf_op jit(solution)/shard_map/ppermute | solution.py:818
  92.1 10.0 %collective-permute-start.15 = (bf16[4,768,128]{2,1,0:T(8,128)(2,1)S(1)}, bf16[4,768,128]{2,1,0:T(8,128)(2,1)S(1)}, u32[]{:S(2)}, u32[]{:S(2)}) collective-permute-start(bf16[4,768,128]{2,1,0:T(8,128)(2,1)S(1)} %collective-permute-done.11.refs_13_), channel_id=1, source_target_pairs={{0,1},{1,0},{2,3},{3,2},{4,5},{5,4},{6,7},{7,6},{8,9},{9,8},{10,11... | collective-permute-start | bytes 2359304 | tf_op jit(solution)/shard_map/ppermute | solution.py:818
  102.1 2.3 %collective-permute-start.17 = (bf16[4,768,128]{2,1,0:T(8,128)(2,1)S(1)}, bf16[4,768,128]{2,1,0:T(8,128)(2,1)S(1)}, u32[]{:S(2)}, u32[]{:S(2)}) collective-permute-start(bf16[4,768,128]{2,1,0:T(8,128)(2,1)S(1)} %collective-permute-done.13.refs_15_), channel_id=1, source_target_pairs={{0,1},{1,0},{2,3},{3,2},{4,5},{5,4},{6,7},{7,6},{8,9},{9,8},{10,11... | collective-permute-start | bytes 2359304 | tf_op jit(solution)/shard_map/ppermute | solution.py:818
  122.8 5.3 %collective-permute-start.18 = (bf16[4,1536,128]{2,1,0:T(8,128)(2,1)S(1)}, bf16[4,1536,128]{2,1,0:T(8,128)(2,1)S(1)}, u32[]{:S(2)}, u32[]{:S(2)}) collective-permute-start(bf16[4,1536,128]{2,1,0:T(8,128)(2,1)S(1)} %get-tuple-element.90), channel_id=1, source_target_pairs={{0,1},{1,0},{2,3},{3,2},{4,5},{5,4},{6,7},{7,6},{8,9},{9,8},{10,11... | collective-permute-start | bytes 4718600 | tf_op jit(solution)/shard_map/ppermute | solution.py:818
  123.0 5.6 %collective-permute-start.19 = (bf16[4,1536,128]{2,1,0:T(8,128)(2,1)S(1)}, bf16[4,1536,128]{2,1,0:T(8,128)(2,1)S(1)}, u32[]{:S(2)}, u32[]{:S(2)}) collective-permute-start(bf16[4,1536,128]{2,1,0:T(8,128)(2,1)S(1)} %get-tuple-element.91), channel_id=1, source_target_pairs={{0,1},{1,0},{2,3},{3,2},{4,5},{5,4},{6,7},{7,6},{8,9},{9,8},{10,11... | collective-permute-start | bytes 4718600 | tf_op jit(solution)/shard_map/ppermute | solution.py:818
  123.4 6.7 %collective-permute-start.21 = (bf16[2,16,512]{2,1,0:T(8,128)(2,1)S(1)}, bf16[2,16,512]{2,1,0:T(8,128)(2,1)S(1)}, u32[]{:S(2)}, u32[]{:S(2)}) collective-permute-start(bf16[2,16,512]{2,1,0:T(8,128)(2,1)S(1)} %get-tuple-element.95), channel_id=1, source_target_pairs={{0,4},{4,8},{8,12},{12,16},{16,20},{20,24},{24,28},{28,0},{1,5},{5... | collective-permute-start | bytes 98312 | tf_op jit(solution)/shard_map/ppermute | solution.py:808
  124.9 5.6 %collective-permute-start.20 = (bf16[2,48,512]{2,1,0:T(8,128)(2,1)S(1)}, bf16[2,48,512]{2,1,0:T(8,128)(2,1)S(1)}, u32[]{:S(2)}, u32[]{:S(2)}) collective-permute-start(bf16[2,48,512]{2,1,0:T(8,128)(2,1)S(1)} %get-tuple-element.94), channel_id=1, source_target_pairs={{0,28},{4,0},{8,4},{12,8},{16,12},{20,16},{24,20},{28,24},{1,29},{... | collective-permute-start | bytes 294920 | tf_op jit(solution)/shard_map/ppermute | solution.py:808
  128.1 2.4 %copy-start.8 = (bf16[2,64,512]{2,1,0:T(8,128)(2,1)S(1)}, bf16[2,64,512]{2,1,0:T(8,128)(2,1)}, u32[]{:S(2)}) copy-start(bf16[2,64,512]{2,1,0:T(8,128)(2,1)} %copy-done.7) | copy-start | bytes 393220
  128.6 20.5 %collective-permute-start.22 = (bf16[4,1536,128]{2,1,0:T(8,128)(2,1)S(1)}, bf16[4,1536,128]{2,1,0:T(8,128)(2,1)S(1)}, u32[]{:S(2)}, u32[]{:S(2)}) collective-permute-start(bf16[4,1536,128]{2,1,0:T(8,128)(2,1)S(1)} %add_convert_fusion.2), channel_id=1, source_target_pairs={{0,4},{1,3},{2,6},{3,1},{4,0},{5,7},{6,2},{7,5},{8,12},{9,11},{10,... | collective-permute-start | bytes 4718600 | tf_op jit(solution)/shard_map/ppermute | solution.py:818
  145.6 9.9 %copy-start.2 = (f32[256,512]{1,0:T(8,128)}, f32[256,512]{1,0:T(8,128)S(1)}, u32[]{:S(2)}) copy-start(f32[256,512]{1,0:T(8,128)S(1)} %get-tuple-element.116.refs_2_) | copy-start | bytes 1572868
  145.6 9.9 %copy-start = (bf16[2,2,3168,128]{3,2,1,0:T(8,128)(2,1)}, bf16[2,2,3168,128]{3,2,1,0:T(8,128)(2,1)S(1)}, u32[]{:S(2)}) copy-start(bf16[2,2,3168,128]{3,2,1,0:T(8,128)(2,1)S(1)} %get-tuple-element.105) | copy-start | bytes 9732100
  149.0 6.5 %collective-permute-start.23 = (bf16[2,2,3168,128]{3,2,1,0:T(8,128)(2,1)S(1)}, bf16[2,2,3168,128]{3,2,1,0:T(8,128)(2,1)S(1)}, u32[]{:S(2)}, u32[]{:S(2)}) collective-permute-start(bf16[2,2,3168,128]{3,2,1,0:T(8,128)(2,1)S(1)} %get-tuple-element.107), channel_id=1, source_target_pairs={{0,1},{1,0},{2,3},{3,2},{4,5},{5,4},{6,7},{7,6},{8,9},{9,8},{10,11... | collective-permute-start | bytes 9732104 | tf_op jit(solution)/shard_map/ppermute | solution.py:818
  149.0 8.5 %collective-permute-start.25 = (bf16[2,16,512]{2,1,0:T(8,128)(2,1)S(1)}, bf16[2,16,512]{2,1,0:T(8,128)(2,1)S(1)}, u32[]{:S(2)}, u32[]{:S(2)}) collective-permute-start(bf16[2,16,512]{2,1,0:T(8,128)(2,1)S(1)} %get-tuple-element.111), channel_id=1, source_target_pairs={{0,4},{4,8},{8,12},{12,16},{16,20},{20,24},{24,28},{28,0},{1,5},{5... | collective-permute-start | bytes 98312 | tf_op jit(solution)/shard_map/ppermute | solution.py:808
  149.4 8.1 %collective-permute-start.24 = (bf16[2,48,512]{2,1,0:T(8,128)(2,1)S(1)}, bf16[2,48,512]{2,1,0:T(8,128)(2,1)S(1)}, u32[]{:S(2)}, u32[]{:S(2)}) collective-permute-start(bf16[2,48,512]{2,1,0:T(8,128)(2,1)S(1)} %get-tuple-element.110), channel_id=1, source_target_pairs={{0,28},{4,0},{8,4},{12,8},{16,12},{20,16},{24,20},{28,24},{1,29},{... | collective-permute-start | bytes 294920 | tf_op jit(solution)/shard_map/ppermute | solution.py:808
  155.5 2.3 %copy-start.10 = (bf16[2,2,3168,128]{3,2,1,0:T(8,128)(2,1)}, bf16[2,2,3168,128]{3,2,1,0:T(8,128)(2,1)S(1)}, u32[]{:S(2)}) copy-start(bf16[2,2,3168,128]{3,2,1,0:T(8,128)(2,1)S(1)} %collective-permute-done.23) | copy-start | bytes 9732100
  157.8 21.3 %collective-permute-start.26 = (bf16[2,3168,128]{2,1,0:T(8,128)(2,1)}, bf16[2,3168,128]{2,1,0:T(8,128)(2,1)}, u32[]{:S(2)}, u32[]{:S(2)}) collective-permute-start(bf16[2,3168,128]{2,1,0:T(8,128)(2,1)} %fusion), channel_id=1, source_target_pairs={{0,4},{1,3},{2,6},{3,1},{4,0},{5,7},{6,2},{7,5},{8,12},{9,11},{10,... | collective-permute-start | bytes 4866056 | tf_op jit(solution)/shard_map/ppermute | solution.py:818
  157.8 42.6 %all-to-all-start.2 = ((bf16[4,1536,128]{2,1,0:T(8,128)(2,1)}), bf16[4,1536,128]{2,1,0:T(8,128)(2,1)S(1)}, u32[]{:S(2)}, u32[]{:S(2)}) async-start(bf16[4,1536,128]{2,1,0:T(8,128)(2,1)} %add_convert_fusion.1), calls=%async_computation.2 | async-start | bytes 3145728 | tf_op jit(solution)/shard_map/all_to_all | solution.py:841
  181.0 12.3 %collective-permute-start.27 = (bf16[3168,128]{1,0:T(8,128)(2,1)S(1)}, bf16[3168,128]{1,0:T(8,128)(2,1)S(1)}, u32[]{:S(2)}, u32[]{:S(2)}) collective-permute-start(bf16[3168,128]{1,0:T(8,128)(2,1)S(1)} %fusion.2), channel_id=1, source_target_pairs={{0,2},{1,5},{2,0},{3,7},{4,6},{5,1},{6,4},{7,3},{8,10},{9,13},{10,... | collective-permute-start | bytes 2433032 | tf_op jit(solution)/shard_map/ppermute | solution.py:818
  200.4 25.2 %all-to-all-start.3 = ((bf16[4,864,128]{2,1,0:T(8,128)(2,1)}), bf16[4,864,128]{2,1,0:T(8,128)(2,1)S(1)}, u32[]{:S(2)}, u32[]{:S(2)}) async-start(bf16[4,864,128]{2,1,0:T(8,128)(2,1)} %pad_maximum_fusion), calls=%async_computation.3 | async-start | bytes 1769472 | tf_op jit(solution)/shard_map/all_to_all | solution.py:841
  204.0 5.7 %collective-permute-start.28 = (bf16[1,768,128]{2,1,0:T(8,128)(2,1)S(1)}, bf16[1,768,128]{2,1,0:T(8,128)(2,1)S(1)}, u32[]{:S(2)}, u32[]{:S(2)}) collective-permute-start(bf16[1,768,128]{2,1,0:T(8,128)(2,1)S(1)} %bitcast.72), channel_id=1, source_target_pairs={{0,2},{1,5},{2,0},{3,7},{4,6},{5,1},{6,4},{7,3},{8,10},{9,13},{10,... | collective-permute-start | bytes 589832 | tf_op jit(solution)/shard_map/ppermute | solution.py:818
  204.4 1.0 copy-start.3

commit v3 on v2

--- a/solution.py
+++ b/solution.py
@@ -305,7 +305,7 @@
             )
         return carry
 
-    lax.fori_loop(0, sizes.pairs, body, 0)
+    lax.fori_loop(0, sizes.pairs, body, 0, unroll=sizes.pairs if sizes.top == 0 else 1)
 
 
 def gelu_both(upward):
@@ -649,7 +649,7 @@
         )
         return carry
 
-    lax.fori_loop(0, sizes.ff // wide, body, 0)
+    lax.fori_loop(0, sizes.ff // wide, body, 0, unroll=True)
     out_at = len(attn_copies) + len(ffn_copies)
     outs = start_out(
         ffn_pairs(mats, spots, outs_to, gup_ref, gdown_ref, place_ref), sems, out_at

time: 228 us -> 227 us (level)
  no operation moved by 1% of the time
where the time goes in v3:
time: 227 us; the launch traced here: 226 us
  waiting for transfers between devices  112 us (49%)
  starting transfers between devices  53.4 us (24%)
  Pallas kernels  48.2 us (21%)
  other arithmetic  9.51 us (4%)
    ppermute x21, waiting for transfers between devices, permuted(): return lax.ppermute(value, ('seg', 'rep'), pairs)  75.5 us
    pallas_call x7, Pallas kernels, call(): pl.pallas_call(body, grid=grid, input_output_aliases=aliases, in_specs=in...  48.2 us
    all_to_all x4, starting transfers between devices, swap_z(): lax.all_to_all(blocks, 'seg', 0, 0, axis_index_groups=groups, tiled=True)  20.4 us
    ppermute x8, starting transfers between devices, shifted(): lax.ppermute(value, axis, [(i, (i + by) % size) for i in range(size)])  19.1 us
    all_to_all x4, waiting for transfers between devices, swap_z(): lax.all_to_all(blocks, 'seg', 0, 0, axis_index_groups=groups, tiled=True)  18.8 us
    ppermute x8, waiting for transfers between devices, shifted(): lax.ppermute(value, axis, [(i, (i + by) % size) for i in range(size)])  18 us
    ppermute x21, starting transfers between devices, permuted(): return lax.ppermute(value, ('seg', 'rep'), pairs)  14 us
    convert_element_type x5, other arithmetic, summed(): return total.astype(BF16)  8.2 us
  transfers between devices with their start and end apart: 33, of which 16 were waited for; matrix products, arithmetic and copies ran while one was open for 4% of the time, Pallas kernels for 12%

profile of v3, /device:TPU:0, one launch (start us, length us, event | category | flops | bytes accessed | tf_op | source)
XLA Modules:
  0.0 226.1 jit_solution(6268409785160457760)
XLA Ops:
  0.7 2.5 %shard_map.169 = (bf16[4,768,128]{2,1,0:T(8,128)(2,1)}, bf16[4,768,128]{2,1,0:T(8,128)(2,1)}) custom-call(bf16[2,192,128]{2,1,0:T(8,128)(2,1)} %bitcast.74, bf16[2,64,128]{2,1,0:T(8,128)(2,1)} %bitcast.76, bf16[2,128,256]{2,1,0:T(8,128)(2,1)} %refs_2_.1, bf16[2,64,512]{2,1,0:T(8,128)(2,1)} %bitcast.73), custom_call_target="tpu_custom_call" | custom-call | tf_op jit(solution)/shard_map/pallas_call | solution.py:881
  3.1 6.5 %all-to-all-start = ((bf16[4,768,128]{2,1,0:T(8,128)(2,1)}), bf16[4,768,128]{2,1,0:T(8,128)(2,1)S(1)}, u32[]{:S(2)}, u32[]{:S(2)}) async-start(bf16[4,768,128]{2,1,0:T(8,128)(2,1)} %get-tuple-element.71), calls=%async_computation | async-start | bytes 1572864 | tf_op jit(solution)/shard_map/all_to_all | solution.py:841
  9.6 4.8 %collective-permute-start.1 = (bf16[2,16,512]{2,1,0:T(8,128)(2,1)S(1)}, bf16[2,16,512]{2,1,0:T(8,128)(2,1)S(1)}, u32[]{:S(2)}, u32[]{:S(2)}) collective-permute-start(bf16[2,16,512]{2,1,0:T(8,128)(2,1)S(1)} %slice.69), channel_id=1, source_target_pairs={{0,28},{4,0},{8,4},{12,8},{16,12},{20,16},{24,20},{28,24},{1,29},{... | collective-permute-start | bytes 98312 | tf_op jit(solution)/shard_map/ppermute | solution.py:808
  14.9 8.2 %collective-permute-done.1.refs_4_.refs_16_ = bf16[2,16,512]{2,1,0:T(8,128)(2,1)S(1)} collective-permute-done((bf16[2,16,512]{2,1,0:T(8,128)(2,1)S(1)}, bf16[2,16,512]{2,1,0:T(8,128)(2,1)S(1)}, u32[]{:S(2)}, u32[]{:S(2)}) %collective-permute-start.1) | collective-permute-done | bytes 32800 | tf_op jit(solution)/shard_map/ppermute | solution.py:808
  23.1 7.2 %collective-permute-done.refs_3_.refs_15_ = bf16[2,64,512]{2,1,0:T(8,128)(2,1)S(1)} collective-permute-done((bf16[2,64,512]{2,1,0:T(8,128)(2,1)S(1)}, bf16[2,64,512]{2,1,0:T(8,128)(2,1)S(1)}, u32[]{:S(2)}, u32[]{:S(2)}) %collective-permute-start) | collective-permute-done | bytes 131104 | tf_op jit(solution)/shard_map/ppermute | solution.py:808
  30.3 5.0 %all-to-all-start.1 = ((bf16[4,768,128]{2,1,0:T(8,128)(2,1)}), bf16[4,768,128]{2,1,0:T(8,128)(2,1)S(1)}, u32[]{:S(2)}, u32[]{:S(2)}) async-start(bf16[4,768,128]{2,1,0:T(8,128)(2,1)} %get-tuple-element.77), calls=%async_computation.1 | async-start | bytes 1572864 | tf_op jit(solution)/shard_map/all_to_all | solution.py:841
  35.3 1.5 collective-permute-start.2
  36.8 2.3 %collective-permute-start.3 = (bf16[4,768,128]{2,1,0:T(8,128)(2,1)S(1)}, bf16[4,768,128]{2,1,0:T(8,128)(2,1)}, u32[]{:S(2)}, u32[]{:S(2)}) collective-permute-start(bf16[4,768,128]{2,1,0:T(8,128)(2,1)S(1)} %all-to-all-done.refs_9_.refs_20_), channel_id=1, source_target_pairs={{0,4},{1,3},{2,6},{3,1},{4,0},{5,7},{6,2},{7,5},{8,12},{9,11},{10,... | collective-permute-start | bytes 2359304 | tf_op jit(solution)/shard_map/ppermute | solution.py:818
  39.1 16.5 %collective-permute-done.2.refs_10_.refs_21_ = bf16[4,768,128]{2,1,0:T(8,128)(2,1)S(1)} collective-permute-done((bf16[4,768,128]{2,1,0:T(8,128)(2,1)S(1)}, bf16[4,768,128]{2,1,0:T(8,128)(2,1)S(1)}, u32[]{:S(2)}, u32[]{:S(2)}) %collective-permute-start.2) | collective-permute-done | bytes 786464 | tf_op jit(solution)/shard_map/ppermute | solution.py:818
  55.6 1.5 collective-permute-start.4
  57.1 0.5 collective-permute-start.6
  57.6 10.0 %collective-permute-done.4.refs_12_.refs_23_ = bf16[4,768,128]{2,1,0:T(8,128)(2,1)S(1)} collective-permute-done((bf16[4,768,128]{2,1,0:T(8,128)(2,1)S(1)}, bf16[4,768,128]{2,1,0:T(8,128)(2,1)S(1)}, u32[]{:S(2)}, u32[]{:S(2)}) %collective-permute-start.4) | collective-permute-done | bytes 786464 | tf_op jit(solution)/shard_map/ppermute | solution.py:818
  67.6 1.5 collective-permute-start.12
  69.1 1.5 collective-permute-start.11
  70.6 9.8 %shard_map.170 = (bf16[416,512]{1,0:T(8,128)(2,1)S(1)}, bf16[416,1536]{1,0:T(8,128)(2,1)S(1)}, bf16[8,192,288]{2,1,0:T(8,128)(2,1)S(1)}, bf16[288,512]{1,0:T(8,1...) custom-call(s32[18]{0:T(128)S(1)} %stack.65.refs_0_, ...), custom_call_target="tpu_custom_call" | custom-call | flops 9663676416 | bytes 6291456 | tf_op jit(solution)/shard_map/pallas_call | solution.py:881
  80.4 0.8 collective-permute-start.9
  81.2 4.0 %collective-permute-start.10 = (bf16[2,16,512]{2,1,0:T(8,128)(2,1)S(1)}, bf16[2,16,512]{2,1,0:T(8,128)(2,1)S(1)}, u32[]{:S(2)}, u32[]{:S(2)}) collective-permute-start(bf16[2,16,512]{2,1,0:T(8,128)(2,1)S(1)} %get-tuple-element.81), channel_id=1, source_target_pairs={{0,28},{4,0},{8,4},{12,8},{16,12},{20,16},{24,20},{28,24},{1,29},{... | collective-permute-start | bytes 98312 | tf_op jit(solution)/shard_map/ppermute | solution.py:808
  85.2 4.2 %collective-permute-done.12.refs_14_ = bf16[4,768,128]{2,1,0:T(8,128)(2,1)S(1)} collective-permute-done((bf16[4,768,128]{2,1,0:T(8,128)(2,1)S(1)}, bf16[4,768,128]{2,1,0:T(8,128)(2,1)S(1)}, u32[]{:S(2)}, u32[]{:S(2)}) %collective-permute-start.12) | collective-permute-done | bytes 786464 | tf_op jit(solution)/shard_map/ppermute | solution.py:818
  89.4 0.7 collective-permute-done.10.refs_4_
  90.1 1.5 collective-permute-start.13
  92.3 9.8 %collective-permute-done.13.refs_15_ = bf16[4,768,128]{2,1,0:T(8,128)(2,1)S(1)} collective-permute-done((bf16[4,768,128]{2,1,0:T(8,128)(2,1)S(1)}, bf16[4,768,128]{2,1,0:T(8,128)(2,1)S(1)}, u32[]{:S(2)}, u32[]{:S(2)}) %collective-permute-start.13) | collective-permute-done | bytes 786464 | tf_op jit(solution)/shard_map/ppermute | solution.py:818
  102.1 2.3 %collective-permute-done.17.refs_19_ = bf16[4,768,128]{2,1,0:T(8,128)(2,1)S(1)} collective-permute-done((bf16[4,768,128]{2,1,0:T(8,128)(2,1)S(1)}, bf16[4,768,128]{2,1,0:T(8,128)(2,1)S(1)}, u32[]{:S(2)}, u32[]{:S(2)}) %collective-permute-start.17) | collective-permute-done | bytes 786464 | tf_op jit(solution)/shard_map/ppermute | solution.py:818
  104.4 17.2 %shard_map.171 = (f32[2,128,512]{2,1,0:T(8,128)}, f32[256,512]{1,0:T(8,128)S(1)}, f32[256,512]{1,0:T(8,128)S(1)}, f32[16,512]{1,0:T(8,128)S(1)}, bf16[2,48,512]{...) custom-call(s32[18]{0:T(128)S(1)} %stack.65.refs_0_, ...), custom_call_target="tpu_custom_call" | custom-call | flops 24159191040 | bytes 12582912 | tf_op jit(solution)/shard_map/pallas_call | solution.py:881
  122.2 1.5 collective-permute-start.21
  123.7 3.2 %collective-permute-start.20 = (bf16[2,48,512]{2,1,0:T(8,128)(2,1)S(1)}, bf16[2,48,512]{2,1,0:T(8,128)(2,1)S(1)}, u32[]{:S(2)}, u32[]{:S(2)}) collective-permute-start(bf16[2,48,512]{2,1,0:T(8,128)(2,1)S(1)} %get-tuple-element.94), channel_id=1, source_target_pairs={{0,28},{4,0},{8,4},{12,8},{16,12},{20,16},{24,20},{28,24},{1,29},{... | collective-permute-start | bytes 294920 | tf_op jit(solution)/shard_map/ppermute | solution.py:808
  126.9 0.4 add_convert_fusion.2
  127.4 1.4 collective-permute-done.21.refs_6_
  128.8 0.4 collective-permute-done.20.refs_5_
  129.3 15.1 %shard_map.172 = (f32[256,512]{1,0:T(8,128)S(1)}, f32[256,512]{1,0:T(8,128)S(1)}, f32[16,512]{1,0:T(8,128)S(1)}, bf16[2,48,512]{2,1,0:T(8,128)(2,1)S(1)}, bf16[2...) custom-call(s32[18]{0:T(128)S(1)} %stack.65.refs_0_, ...), custom_call_target="tpu_custom_call" | custom-call | flops 22548578304 | bytes 12582912 | tf_op jit(solution)/shard_map/pallas_call | solution.py:881
  144.4 3.4 %collective-permute-done.22 = bf16[4,1536,128]{2,1,0:T(8,128)(2,1)S(1)} collective-permute-done((bf16[4,1536,128]{2,1,0:T(8,128)(2,1)S(1)}, bf16[4,1536,128]{2,1,0:T(8,128)(2,1)S(1)}, u32[]{:S(2)}, u32[]{:S(2)}) %collective-permute-start.22) | collective-permute-done | bytes 1572896 | tf_op jit(solution)/shard_map/ppermute | solution.py:818
  148.1 4.4 %collective-permute-start.24 = (bf16[2,48,512]{2,1,0:T(8,128)(2,1)S(1)}, bf16[2,48,512]{2,1,0:T(8,128)(2,1)S(1)}, u32[]{:S(2)}, u32[]{:S(2)}) collective-permute-start(bf16[2,48,512]{2,1,0:T(8,128)(2,1)S(1)} %get-tuple-element.110), channel_id=1, source_target_pairs={{0,28},{4,0},{8,4},{12,8},{16,12},{20,16},{24,20},{28,24},{1,29},{... | collective-permute-start | bytes 294920 | tf_op jit(solution)/shard_map/ppermute | solution.py:808
  152.5 1.8 add_convert_fusion.1
  154.3 2.0 fusion
  156.6 5.4 %all-to-all-start.2 = ((bf16[4,1536,128]{2,1,0:T(8,128)(2,1)}), bf16[4,1536,128]{2,1,0:T(8,128)(2,1)S(1)}, u32[]{:S(2)}, u32[]{:S(2)}) async-start(bf16[4,1536,128]{2,1,0:T(8,128)(2,1)} %add_convert_fusion.1), calls=%async_computation.2 | async-start | bytes 3145728 | tf_op jit(solution)/shard_map/all_to_all | solution.py:841
  162.0 15.8 %collective-permute-done.26 = bf16[2,3168,128]{2,1,0:T(8,128)(2,1)} collective-permute-done((bf16[2,3168,128]{2,1,0:T(8,128)(2,1)}, bf16[2,3168,128]{2,1,0:T(8,128)(2,1)}, u32[]{:S(2)}, u32[]{:S(2)}) %collective-permute-start.26) | collective-permute-done | bytes 1622048 | tf_op jit(solution)/shard_map/ppermute | solution.py:818
  177.8 1.9 fusion.2
  179.8 2.1 collective-permute-start.27
  181.9 10.2 %collective-permute-done.27 = bf16[3168,128]{1,0:T(8,128)(2,1)S(1)} collective-permute-done((bf16[3168,128]{1,0:T(8,128)(2,1)S(1)}, bf16[3168,128]{1,0:T(8,128)(2,1)S(1)}, u32[]{:S(2)}, u32[]{:S(2)}) %collective-permute-start.27) | collective-permute-done | bytes 811040 | tf_op jit(solution)/shard_map/ppermute | solution.py:818
  192.1 2.1 add_convert_fusion.3
  194.3 1.0 pad_maximum_fusion
  195.3 3.9 %all-to-all-done.2.refs_0_ = bf16[4,1536,128]{2,1,0:T(8,128)(2,1)S(1)} async-done(((bf16[4,1536,128]{2,1,0:T(8,128)(2,1)}), bf16[4,1536,128]{2,1,0:T(8,128)(2,1)S(1)}, u32[]{:S(2)}, u32[]{:S(2)}) %all-to-all-start.2) | async-done | bytes 1572896 | tf_op jit(solution)/shard_map/all_to_all | solution.py:841
  199.2 3.5 %all-to-all-start.3 = ((bf16[4,864,128]{2,1,0:T(8,128)(2,1)}), bf16[4,864,128]{2,1,0:T(8,128)(2,1)S(1)}, u32[]{:S(2)}, u32[]{:S(2)}) async-start(bf16[4,864,128]{2,1,0:T(8,128)(2,1)} %pad_maximum_fusion), calls=%async_computation.3 | async-start | bytes 1769472 | tf_op jit(solution)/shard_map/all_to_all | solution.py:841
  203.2 1.0 copy-done.3
  204.2 1.2 shard_map.173
  205.4 3.2 %collective-permute-done.28.refs_1_ = bf16[1,768,128]{2,1,0:T(8,128)(2,1)S(1)} collective-permute-done((bf16[1,768,128]{2,1,0:T(8,128)(2,1)S(1)}, bf16[1,768,128]{2,1,0:T(8,128)(2,1)S(1)}, u32[]{:S(2)}, u32[]{:S(2)}) %collective-permute-start.28) | collective-permute-done | bytes 196640 | tf_op jit(solution)/shard_map/ppermute | solution.py:818
  208.5 0.9 shard_map.174
  209.5 14.9 %all-to-all-done.3.refs_0_ = bf16[4,864,128]{2,1,0:T(8,128)(2,1)S(1)} async-done(((bf16[4,864,128]{2,1,0:T(8,128)(2,1)}), bf16[4,864,128]{2,1,0:T(8,128)(2,1)S(1)}, u32[]{:S(2)}, u32[]{:S(2)}) %all-to-all-start.3) | async-done | bytes 884768 | tf_op jit(solution)/shard_map/all_to_all | solution.py:841
  224.4 1.5 shard_map.175
  (68 shorter events, 2.9 us)
Async XLA Ops:
  0.6 9.0 %copy-start.1 = (bf16[2,1,128,512]{3,2,1,0:T(8,128)(2,1)S(1)}, bf16[2,1,128,512]{3,2,1,0:T(8,128)(2,1)}, u32[]{:S(2)}) copy-start(bf16[2,1,128,512]{3,2,1,0:T(8,128)(2,1)} %param.10) | copy-start | bytes 786436
  0.7 13.8 %copy-start.4 = (f32[2,6,512]{2,0,1:T(2,128)S(1)}, f32[2,6,512]{2,0,1:T(2,128)}, u32[]{:S(2)}) copy-start(f32[2,6,512]{2,0,1:T(2,128)} %param.18) | copy-start | bytes 73732
  0.7 13.9 %copy-start.11 = (s32[2,1,4]{2,1,0:T(1,128)S(1)}, s32[2,1,4]{2,1,0:T(1,128)}, u32[]{:S(2)}) copy-start(s32[2,1,4]{2,1,0:T(1,128)} %param.11) | copy-start | bytes 100
  3.1 67.5 %copy-start.5 = (f32[2,2,512]{2,1,0:T(2,128)S(1)}, f32[2,2,512]{2,1,0:T(2,128)}, u32[]{:S(2)}) copy-start(f32[2,2,512]{2,1,0:T(2,128)} %refs_6_.1) | copy-start | bytes 24580
  3.1 67.5 %copy-start.9 = (f32[2,2048]{1,0:T(2,128)S(1)}, f32[2,2048]{1,0:T(2,128)}, u32[]{:S(2)}) copy-start(f32[2,2048]{1,0:T(2,128)} %refs_10_.1) | copy-start | bytes 49156
  3.1 27.2 %all-to-all-start = ((bf16[4,768,128]{2,1,0:T(8,128)(2,1)}), bf16[4,768,128]{2,1,0:T(8,128)(2,1)S(1)}, u32[]{:S(2)}, u32[]{:S(2)}) async-start(bf16[4,768,128]{2,1,0:T(8,128)(2,1)} %get-tuple-element.71), calls=%async_computation | async-start | bytes 1572864 | tf_op jit(solution)/shard_map/all_to_all | solution.py:841
  9.6 13.5 %collective-permute-start.1 = (bf16[2,16,512]{2,1,0:T(8,128)(2,1)S(1)}, bf16[2,16,512]{2,1,0:T(8,128)(2,1)S(1)}, u32[]{:S(2)}, u32[]{:S(2)}) collective-permute-start(bf16[2,16,512]{2,1,0:T(8,128)(2,1)S(1)} %slice.69), channel_id=1, source_target_pairs={{0,28},{4,0},{8,4},{12,8},{16,12},{20,16},{24,20},{28,24},{1,29},{... | collective-permute-start | bytes 98312 | tf_op jit(solution)/shard_map/ppermute | solution.py:808
  14.4 15.9 %collective-permute-start = (bf16[2,64,512]{2,1,0:T(8,128)(2,1)S(1)}, bf16[2,64,512]{2,1,0:T(8,128)(2,1)S(1)}, u32[]{:S(2)}, u32[]{:S(2)}) collective-permute-start(bf16[2,64,512]{2,1,0:T(8,128)(2,1)S(1)} %slice.68), channel_id=1, source_target_pairs={{0,4},{4,8},{8,12},{12,16},{16,20},{20,24},{24,28},{28,0},{1,5},{5... | collective-permute-start | bytes 393224 | tf_op jit(solution)/shard_map/ppermute | solution.py:808
  30.3 50.1 %copy-start.7 = (bf16[2,64,512]{2,1,0:T(8,128)(2,1)}, bf16[2,64,512]{2,1,0:T(8,128)(2,1)S(1)}, u32[]{:S(2)}) copy-start(bf16[2,64,512]{2,1,0:T(8,128)(2,1)S(1)} %collective-permute-done.refs_3_.refs_15_) | copy-start | bytes 393220
  30.3 25.3 %all-to-all-start.1 = ((bf16[4,768,128]{2,1,0:T(8,128)(2,1)}), bf16[4,768,128]{2,1,0:T(8,128)(2,1)S(1)}, u32[]{:S(2)}, u32[]{:S(2)}) async-start(bf16[4,768,128]{2,1,0:T(8,128)(2,1)} %get-tuple-element.77), calls=%async_computation.1 | async-start | bytes 1572864 | tf_op jit(solution)/shard_map/all_to_all | solution.py:841
  35.3 20.3 %collective-permute-start.2 = (bf16[4,768,128]{2,1,0:T(8,128)(2,1)S(1)}, bf16[4,768,128]{2,1,0:T(8,128)(2,1)S(1)}, u32[]{:S(2)}, u32[]{:S(2)}) collective-permute-start(bf16[4,768,128]{2,1,0:T(8,128)(2,1)S(1)} %all-to-all-done.refs_9_.refs_20_), channel_id=1, source_target_pairs={{0,2},{1,5},{2,0},{3,7},{4,6},{5,1},{6,4},{7,3},{8,10},{9,13},{10,... | collective-permute-start | bytes 2359304 | tf_op jit(solution)/shard_map/ppermute | solution.py:818
  36.8 20.8 %collective-permute-start.3 = (bf16[4,768,128]{2,1,0:T(8,128)(2,1)S(1)}, bf16[4,768,128]{2,1,0:T(8,128)(2,1)}, u32[]{:S(2)}, u32[]{:S(2)}) collective-permute-start(bf16[4,768,128]{2,1,0:T(8,128)(2,1)S(1)} %all-to-all-done.refs_9_.refs_20_), channel_id=1, source_target_pairs={{0,4},{1,3},{2,6},{3,1},{4,0},{5,7},{6,2},{7,5},{8,12},{9,11},{10,... | collective-permute-start | bytes 2359304 | tf_op jit(solution)/shard_map/ppermute | solution.py:818
  55.6 12.0 %collective-permute-start.4 = (bf16[4,768,128]{2,1,0:T(8,128)(2,1)S(1)}, bf16[4,768,128]{2,1,0:T(8,128)(2,1)S(1)}, u32[]{:S(2)}, u32[]{:S(2)}) collective-permute-start(bf16[4,768,128]{2,1,0:T(8,128)(2,1)S(1)} %collective-permute-done.2.refs_10_.refs_21_), channel_id=1, source_target_pairs={{0,4},{1,3},{2,6},{3,1},{4,0},{5,7},{6,2},{7,5},{8,12},{9,11},{10,... | collective-permute-start | bytes 2359304 | tf_op jit(solution)/shard_map/ppermute | solution.py:818
  57.1 12.0 %collective-permute-start.5 = (bf16[4,768,128]{2,1,0:T(8,128)(2,1)S(1)}, bf16[4,768,128]{2,1,0:T(8,128)(2,1)S(1)}, u32[]{:S(2)}, u32[]{:S(2)}) collective-permute-start(bf16[4,768,128]{2,1,0:T(8,128)(2,1)S(1)} %all-to-all-done.refs_9_.refs_20_), channel_id=1, source_target_pairs={{0,1},{1,0},{2,3},{3,2},{4,5},{5,4},{6,7},{7,6},{8,9},{9,8},{10,11... | collective-permute-start | bytes 2359304 | tf_op jit(solution)/shard_map/ppermute | solution.py:818
  57.1 13.5 %collective-permute-start.6 = (bf16[4,768,128]{2,1,0:T(8,128)(2,1)S(1)}, bf16[4,768,128]{2,1,0:T(8,128)(2,1)S(1)}, u32[]{:S(2)}, u32[]{:S(2)}) collective-permute-start(bf16[4,768,128]{2,1,0:T(8,128)(2,1)S(1)} %collective-permute-done.2.refs_10_.refs_21_), channel_id=1, source_target_pairs={{0,1},{1,0},{2,3},{3,2},{4,5},{5,4},{6,7},{7,6},{8,9},{9,8},{10,11... | collective-permute-start | bytes 2359304 | tf_op jit(solution)/shard_map/ppermute | solution.py:818
  57.6 13.0 %collective-permute-start.7 = (bf16[4,768,128]{2,1,0:T(8,128)(2,1)}, bf16[4,768,128]{2,1,0:T(8,128)(2,1)S(1)}, u32[]{:S(2)}, u32[]{:S(2)}) collective-permute-start(bf16[4,768,128]{2,1,0:T(8,128)(2,1)} %collective-permute-done.3.refs_11_.refs_22_), channel_id=1, source_target_pairs={{0,1},{1,0},{2,3},{3,2},{4,5},{5,4},{6,7},{7,6},{8,9},{9,8},{10,11... | collective-permute-start | bytes 2359304 | tf_op jit(solution)/shard_map/ppermute | solution.py:818
  67.6 3.0 %collective-permute-start.8 = (bf16[4,768,128]{2,1,0:T(8,128)(2,1)S(1)}, bf16[4,768,128]{2,1,0:T(8,128)(2,1)S(1)}, u32[]{:S(2)}, u32[]{:S(2)}) collective-permute-start(bf16[4,768,128]{2,1,0:T(8,128)(2,1)S(1)} %collective-permute-done.4.refs_12_.refs_23_), channel_id=1, source_target_pairs={{0,1},{1,0},{2,3},{3,2},{4,5},{5,4},{6,7},{7,6},{8,9},{9,8},{10,11... | collective-permute-start | bytes 2359304 | tf_op jit(solution)/shard_map/ppermute | solution.py:818
  67.6 21.8 %collective-permute-start.12 = (bf16[4,768,128]{2,1,0:T(8,128)(2,1)S(1)}, bf16[4,768,128]{2,1,0:T(8,128)(2,1)S(1)}, u32[]{:S(2)}, u32[]{:S(2)}) collective-permute-start(bf16[4,768,128]{2,1,0:T(8,128)(2,1)S(1)} %all-to-all-done.1.refs_12_), channel_id=1, source_target_pairs={{0,4},{1,3},{2,6},{3,1},{4,0},{5,7},{6,2},{7,5},{8,12},{9,11},{10,... | collective-permute-start | bytes 2359304 | tf_op jit(solution)/shard_map/ppermute | solution.py:818
  69.1 20.3 %collective-permute-start.11 = (bf16[4,768,128]{2,1,0:T(8,128)(2,1)S(1)}, bf16[4,768,128]{2,1,0:T(8,128)(2,1)S(1)}, u32[]{:S(2)}, u32[]{:S(2)}) collective-permute-start(bf16[4,768,128]{2,1,0:T(8,128)(2,1)S(1)} %all-to-all-done.1.refs_12_), channel_id=1, source_target_pairs={{0,2},{1,5},{2,0},{3,7},{4,6},{5,1},{6,4},{7,3},{8,10},{9,13},{10,... | collective-permute-start | bytes 2359304 | tf_op jit(solution)/shard_map/ppermute | solution.py:818
  70.6 33.8 %copy-start.6 = (bf16[2,1,128,512]{3,2,1,0:T(8,128)(2,1)S(1)}, bf16[2,1,128,512]{3,2,1,0:T(8,128)(2,1)}, u32[]{:S(2)}) copy-start(bf16[2,1,128,512]{3,2,1,0:T(8,128)(2,1)} %param.12) | copy-start | bytes 786436
  80.4 9.7 %collective-permute-start.9 = (bf16[2,48,512]{2,1,0:T(8,128)(2,1)S(1)}, bf16[2,48,512]{2,1,0:T(8,128)(2,1)S(1)}, u32[]{:S(2)}, u32[]{:S(2)}) collective-permute-start(bf16[2,48,512]{2,1,0:T(8,128)(2,1)S(1)} %get-tuple-element.80), channel_id=1, source_target_pairs={{0,4},{4,8},{8,12},{12,16},{16,20},{20,24},{24,28},{28,0},{1,5},{5... | collective-permute-start | bytes 294920 | tf_op jit(solution)/shard_map/ppermute | solution.py:808
  81.2 8.9 %collective-permute-start.10 = (bf16[2,16,512]{2,1,0:T(8,128)(2,1)S(1)}, bf16[2,16,512]{2,1,0:T(8,128)(2,1)S(1)}, u32[]{:S(2)}, u32[]{:S(2)}) collective-permute-start(bf16[2,16,512]{2,1,0:T(8,128)(2,1)S(1)} %get-tuple-element.81), channel_id=1, source_target_pairs={{0,28},{4,0},{8,4},{12,8},{16,12},{20,16},{24,20},{28,24},{1,29},{... | collective-permute-start | bytes 98312 | tf_op jit(solution)/shard_map/ppermute | solution.py:808
  90.1 12.0 %collective-permute-start.13 = (bf16[4,768,128]{2,1,0:T(8,128)(2,1)S(1)}, bf16[4,768,128]{2,1,0:T(8,128)(2,1)S(1)}, u32[]{:S(2)}, u32[]{:S(2)}) collective-permute-start(bf16[4,768,128]{2,1,0:T(8,128)(2,1)S(1)} %collective-permute-done.11.refs_13_), channel_id=1, source_target_pairs={{0,4},{1,3},{2,6},{3,1},{4,0},{5,7},{6,2},{7,5},{8,12},{9,11},{10,... | collective-permute-start | bytes 2359304 | tf_op jit(solution)/shard_map/ppermute | solution.py:818
  91.6 10.5 %collective-permute-start.14 = (bf16[4,768,128]{2,1,0:T(8,128)(2,1)S(1)}, bf16[4,768,128]{2,1,0:T(8,128)(2,1)S(1)}, u32[]{:S(2)}, u32[]{:S(2)}) collective-permute-start(bf16[4,768,128]{2,1,0:T(8,128)(2,1)S(1)} %all-to-all-done.1.refs_12_), channel_id=1, source_target_pairs={{0,1},{1,0},{2,3},{3,2},{4,5},{5,4},{6,7},{7,6},{8,9},{9,8},{10,11... | collective-permute-start | bytes 2359304 | tf_op jit(solution)/shard_map/ppermute | solution.py:818
  91.8 10.4 %collective-permute-start.16 = (bf16[4,768,128]{2,1,0:T(8,128)(2,1)S(1)}, bf16[4,768,128]{2,1,0:T(8,128)(2,1)S(1)}, u32[]{:S(2)}, u32[]{:S(2)}) collective-permute-start(bf16[4,768,128]{2,1,0:T(8,128)(2,1)S(1)} %collective-permute-done.12.refs_14_), channel_id=1, source_target_pairs={{0,1},{1,0},{2,3},{3,2},{4,5},{5,4},{6,7},{7,6},{8,9},{9,8},{10,11... | collective-permute-start | bytes 2359304 | tf_op jit(solution)/shard_map/ppermute | solution.py:818
  92.1 10.0 %collective-permute-start.15 = (bf16[4,768,128]{2,1,0:T(8,128)(2,1)S(1)}, bf16[4,768,128]{2,1,0:T(8,128)(2,1)S(1)}, u32[]{:S(2)}, u32[]{:S(2)}) collective-permute-start(bf16[4,768,128]{2,1,0:T(8,128)(2,1)S(1)} %collective-permute-done.11.refs_13_), channel_id=1, source_target_pairs={{0,1},{1,0},{2,3},{3,2},{4,5},{5,4},{6,7},{7,6},{8,9},{9,8},{10,11... | collective-permute-start | bytes 2359304 | tf_op jit(solution)/shard_map/ppermute | solution.py:818
  102.1 2.3 %collective-permute-start.17 = (bf16[4,768,128]{2,1,0:T(8,128)(2,1)S(1)}, bf16[4,768,128]{2,1,0:T(8,128)(2,1)S(1)}, u32[]{:S(2)}, u32[]{:S(2)}) collective-permute-start(bf16[4,768,128]{2,1,0:T(8,128)(2,1)S(1)} %collective-permute-done.13.refs_15_), channel_id=1, source_target_pairs={{0,1},{1,0},{2,3},{3,2},{4,5},{5,4},{6,7},{7,6},{8,9},{9,8},{10,11... | collective-permute-start | bytes 2359304 | tf_op jit(solution)/shard_map/ppermute | solution.py:818
  121.6 5.3 %collective-permute-start.18 = (bf16[4,1536,128]{2,1,0:T(8,128)(2,1)S(1)}, bf16[4,1536,128]{2,1,0:T(8,128)(2,1)S(1)}, u32[]{:S(2)}, u32[]{:S(2)}) collective-permute-start(bf16[4,1536,128]{2,1,0:T(8,128)(2,1)S(1)} %get-tuple-element.90), channel_id=1, source_target_pairs={{0,1},{1,0},{2,3},{3,2},{4,5},{5,4},{6,7},{7,6},{8,9},{9,8},{10,11... | collective-permute-start | bytes 4718600 | tf_op jit(solution)/shard_map/ppermute | solution.py:818
  121.8 5.6 %collective-permute-start.19 = (bf16[4,1536,128]{2,1,0:T(8,128)(2,1)S(1)}, bf16[4,1536,128]{2,1,0:T(8,128)(2,1)S(1)}, u32[]{:S(2)}, u32[]{:S(2)}) collective-permute-start(bf16[4,1536,128]{2,1,0:T(8,128)(2,1)S(1)} %get-tuple-element.91), channel_id=1, source_target_pairs={{0,1},{1,0},{2,3},{3,2},{4,5},{5,4},{6,7},{7,6},{8,9},{9,8},{10,11... | collective-permute-start | bytes 4718600 | tf_op jit(solution)/shard_map/ppermute | solution.py:818
  122.2 6.7 %collective-permute-start.21 = (bf16[2,16,512]{2,1,0:T(8,128)(2,1)S(1)}, bf16[2,16,512]{2,1,0:T(8,128)(2,1)S(1)}, u32[]{:S(2)}, u32[]{:S(2)}) collective-permute-start(bf16[2,16,512]{2,1,0:T(8,128)(2,1)S(1)} %get-tuple-element.95), channel_id=1, source_target_pairs={{0,4},{4,8},{8,12},{12,16},{16,20},{20,24},{24,28},{28,0},{1,5},{5... | collective-permute-start | bytes 98312 | tf_op jit(solution)/shard_map/ppermute | solution.py:808
  123.7 5.6 %collective-permute-start.20 = (bf16[2,48,512]{2,1,0:T(8,128)(2,1)S(1)}, bf16[2,48,512]{2,1,0:T(8,128)(2,1)S(1)}, u32[]{:S(2)}, u32[]{:S(2)}) collective-permute-start(bf16[2,48,512]{2,1,0:T(8,128)(2,1)S(1)} %get-tuple-element.94), channel_id=1, source_target_pairs={{0,28},{4,0},{8,4},{12,8},{16,12},{20,16},{24,20},{28,24},{1,29},{... | collective-permute-start | bytes 294920 | tf_op jit(solution)/shard_map/ppermute | solution.py:808
  126.9 2.4 %copy-start.8 = (bf16[2,64,512]{2,1,0:T(8,128)(2,1)S(1)}, bf16[2,64,512]{2,1,0:T(8,128)(2,1)}, u32[]{:S(2)}) copy-start(bf16[2,64,512]{2,1,0:T(8,128)(2,1)} %copy-done.7) | copy-start | bytes 393220
  127.3 20.5 %collective-permute-start.22 = (bf16[4,1536,128]{2,1,0:T(8,128)(2,1)S(1)}, bf16[4,1536,128]{2,1,0:T(8,128)(2,1)S(1)}, u32[]{:S(2)}, u32[]{:S(2)}) collective-permute-start(bf16[4,1536,128]{2,1,0:T(8,128)(2,1)S(1)} %add_convert_fusion.2), channel_id=1, source_target_pairs={{0,4},{1,3},{2,6},{3,1},{4,0},{5,7},{6,2},{7,5},{8,12},{9,11},{10,... | collective-permute-start | bytes 4718600 | tf_op jit(solution)/shard_map/ppermute | solution.py:818
  144.4 9.9 %copy-start.2 = (f32[256,512]{1,0:T(8,128)}, f32[256,512]{1,0:T(8,128)S(1)}, u32[]{:S(2)}) copy-start(f32[256,512]{1,0:T(8,128)S(1)} %get-tuple-element.116.refs_2_) | copy-start | bytes 1572868
  144.4 9.9 %copy-start = (bf16[2,2,3168,128]{3,2,1,0:T(8,128)(2,1)}, bf16[2,2,3168,128]{3,2,1,0:T(8,128)(2,1)S(1)}, u32[]{:S(2)}) copy-start(bf16[2,2,3168,128]{3,2,1,0:T(8,128)(2,1)S(1)} %get-tuple-element.105) | copy-start | bytes 9732100
  147.8 6.5 %collective-permute-start.23 = (bf16[2,2,3168,128]{3,2,1,0:T(8,128)(2,1)S(1)}, bf16[2,2,3168,128]{3,2,1,0:T(8,128)(2,1)S(1)}, u32[]{:S(2)}, u32[]{:S(2)}) collective-permute-start(bf16[2,2,3168,128]{3,2,1,0:T(8,128)(2,1)S(1)} %get-tuple-element.107), channel_id=1, source_target_pairs={{0,1},{1,0},{2,3},{3,2},{4,5},{5,4},{6,7},{7,6},{8,9},{9,8},{10,11... | collective-permute-start | bytes 9732104 | tf_op jit(solution)/shard_map/ppermute | solution.py:818
  147.8 8.5 %collective-permute-start.25 = (bf16[2,16,512]{2,1,0:T(8,128)(2,1)S(1)}, bf16[2,16,512]{2,1,0:T(8,128)(2,1)S(1)}, u32[]{:S(2)}, u32[]{:S(2)}) collective-permute-start(bf16[2,16,512]{2,1,0:T(8,128)(2,1)S(1)} %get-tuple-element.111), channel_id=1, source_target_pairs={{0,4},{4,8},{8,12},{12,16},{16,20},{20,24},{24,28},{28,0},{1,5},{5... | collective-permute-start | bytes 98312 | tf_op jit(solution)/shard_map/ppermute | solution.py:808
  148.1 8.2 %collective-permute-start.24 = (bf16[2,48,512]{2,1,0:T(8,128)(2,1)S(1)}, bf16[2,48,512]{2,1,0:T(8,128)(2,1)S(1)}, u32[]{:S(2)}, u32[]{:S(2)}) collective-permute-start(bf16[2,48,512]{2,1,0:T(8,128)(2,1)S(1)} %get-tuple-element.110), channel_id=1, source_target_pairs={{0,28},{4,0},{8,4},{12,8},{16,12},{20,16},{24,20},{28,24},{1,29},{... | collective-permute-start | bytes 294920 | tf_op jit(solution)/shard_map/ppermute | solution.py:808
  154.3 2.3 %copy-start.10 = (bf16[2,2,3168,128]{3,2,1,0:T(8,128)(2,1)}, bf16[2,2,3168,128]{3,2,1,0:T(8,128)(2,1)S(1)}, u32[]{:S(2)}) copy-start(bf16[2,2,3168,128]{3,2,1,0:T(8,128)(2,1)S(1)} %collective-permute-done.23) | copy-start | bytes 9732100
  156.6 21.3 %collective-permute-start.26 = (bf16[2,3168,128]{2,1,0:T(8,128)(2,1)}, bf16[2,3168,128]{2,1,0:T(8,128)(2,1)}, u32[]{:S(2)}, u32[]{:S(2)}) collective-permute-start(bf16[2,3168,128]{2,1,0:T(8,128)(2,1)} %fusion), channel_id=1, source_target_pairs={{0,4},{1,3},{2,6},{3,1},{4,0},{5,7},{6,2},{7,5},{8,12},{9,11},{10,... | collective-permute-start | bytes 4866056 | tf_op jit(solution)/shard_map/ppermute | solution.py:818
  156.6 42.6 %all-to-all-start.2 = ((bf16[4,1536,128]{2,1,0:T(8,128)(2,1)}), bf16[4,1536,128]{2,1,0:T(8,128)(2,1)S(1)}, u32[]{:S(2)}, u32[]{:S(2)}) async-start(bf16[4,1536,128]{2,1,0:T(8,128)(2,1)} %add_convert_fusion.1), calls=%async_computation.2 | async-start | bytes 3145728 | tf_op jit(solution)/shard_map/all_to_all | solution.py:841
  179.8 12.3 %collective-permute-start.27 = (bf16[3168,128]{1,0:T(8,128)(2,1)S(1)}, bf16[3168,128]{1,0:T(8,128)(2,1)S(1)}, u32[]{:S(2)}, u32[]{:S(2)}) collective-permute-start(bf16[3168,128]{1,0:T(8,128)(2,1)S(1)} %fusion.2), channel_id=1, source_target_pairs={{0,2},{1,5},{2,0},{3,7},{4,6},{5,1},{6,4},{7,3},{8,10},{9,13},{10,... | collective-permute-start | bytes 2433032 | tf_op jit(solution)/shard_map/ppermute | solution.py:818
  199.2 25.2 %all-to-all-start.3 = ((bf16[4,864,128]{2,1,0:T(8,128)(2,1)}), bf16[4,864,128]{2,1,0:T(8,128)(2,1)S(1)}, u32[]{:S(2)}, u32[]{:S(2)}) async-start(bf16[4,864,128]{2,1,0:T(8,128)(2,1)} %pad_maximum_fusion), calls=%async_computation.3 | async-start | bytes 1769472 | tf_op jit(solution)/shard_map/all_to_all | solution.py:841
  202.8 5.7 %collective-permute-start.28 = (bf16[1,768,128]{2,1,0:T(8,128)(2,1)S(1)}, bf16[1,768,128]{2,1,0:T(8,128)(2,1)S(1)}, u32[]{:S(2)}, u32[]{:S(2)}) collective-permute-start(bf16[1,768,128]{2,1,0:T(8,128)(2,1)S(1)} %bitcast.72), channel_id=1, source_target_pairs={{0,2},{1,5},{2,0},{3,7},{4,6},{5,1},{6,4},{7,3},{8,10},{9,13},{10,... | collective-permute-start | bytes 589832 | tf_op jit(solution)/shard_map/ppermute | solution.py:818
  203.2 1.0 copy-start.3

commit v4 on v3

--- a/solution.py
+++ b/solution.py
@@ -1126,7 +1126,6 @@
         both1 = summed(near1, near1_theirs, second1)
         lines1 = swap_z(both1)
         far0 = summed(mine0[1], after(theirs0, both1)[1])
-        far0 = after(far0, from_right0, from_left0)
         second0 = across_second(far0)
         mid0 = summed(mine0[0, 1], theirs0[0, 1], second0[1])
         first0 = across_first(mid0)
@@ -1140,7 +1139,7 @@
             ],
             axis=1,
         )
-        first_parts = swap_z(near0)
+        first_parts = swap_z(after(near0, from_right0, from_left0))
         gz0_last, lines1 = lax.optimization_barrier((after(gz0, near0), lines1))
         cross1 = jnp.sum(lines1[:, all_rows:].astype(F32), axis=0, keepdims=True).astype(BF16)
         first1 = across_first(cross1)

time: 227 us -> 228 us (level)
  transfers between devices with their start and end apart: 33 -> 33, of which waited for: 16 -> 17; matrix products, arithmetic and copies ran while one was open for 4% -> 3% of each run, Pallas kernels for 12% -> 12%
where the time goes in v4:
time: 228 us; the launch traced here: 227 us
  waiting for transfers between devices  113 us (50%)
  starting transfers between devices  53.8 us (24%)
  Pallas kernels  48.2 us (21%)
  other arithmetic  9.43 us (4%)
    ppermute x21, waiting for transfers between devices, permuted(): return lax.ppermute(value, ('seg', 'rep'), pairs)  75.2 us
    pallas_call x7, Pallas kernels, call(): pl.pallas_call(body, grid=grid, input_output_aliases=aliases, in_specs=in...  48.2 us
    all_to_all x4, starting transfers between devices, swap_z(): lax.all_to_all(blocks, 'seg', 0, 0, axis_index_groups=groups, tiled=True)  20.5 us
    all_to_all x4, waiting for transfers between devices, swap_z(): lax.all_to_all(blocks, 'seg', 0, 0, axis_index_groups=groups, tiled=True)  19.8 us
    ppermute x8, starting transfers between devices, shifted(): lax.ppermute(value, axis, [(i, (i + by) % size) for i in range(size)])  19.1 us
    ppermute x8, waiting for transfers between devices, shifted(): lax.ppermute(value, axis, [(i, (i + by) % size) for i in range(size)])  18 us
    ppermute x21, starting transfers between devices, permuted(): return lax.ppermute(value, ('seg', 'rep'), pairs)  14.3 us
    convert_element_type x5, other arithmetic, summed(): return total.astype(BF16)  8.12 us
  transfers between devices with their start and end apart: 33, of which 17 were waited for; matrix products, arithmetic and copies ran while one was open for 3% of the time, Pallas kernels for 12%

profile of v4, /device:TPU:0, one launch (start us, length us, event | category | flops | bytes accessed | tf_op | source)
XLA Modules:
  0.0 227.2 jit_solution(7963630993087918470)
XLA Ops:
  0.7 2.5 %shard_map.169 = (bf16[4,768,128]{2,1,0:T(8,128)(2,1)}, bf16[4,768,128]{2,1,0:T(8,128)(2,1)}) custom-call(bf16[2,192,128]{2,1,0:T(8,128)(2,1)} %bitcast.74, bf16[2,64,128]{2,1,0:T(8,128)(2,1)} %bitcast.76, bf16[2,128,256]{2,1,0:T(8,128)(2,1)} %refs_2_.1, bf16[2,64,512]{2,1,0:T(8,128)(2,1)} %bitcast.73), custom_call_target="tpu_custom_call" | custom-call | tf_op jit(solution)/shard_map/pallas_call | solution.py:881
  3.1 6.5 %all-to-all-start = ((bf16[4,768,128]{2,1,0:T(8,128)(2,1)}), bf16[4,768,128]{2,1,0:T(8,128)(2,1)S(1)}, u32[]{:S(2)}, u32[]{:S(2)}) async-start(bf16[4,768,128]{2,1,0:T(8,128)(2,1)} %get-tuple-element.71), calls=%async_computation | async-start | bytes 1572864 | tf_op jit(solution)/shard_map/all_to_all | solution.py:841
  9.6 4.8 %collective-permute-start.1 = (bf16[2,16,512]{2,1,0:T(8,128)(2,1)S(1)}, bf16[2,16,512]{2,1,0:T(8,128)(2,1)S(1)}, u32[]{:S(2)}, u32[]{:S(2)}) collective-permute-start(bf16[2,16,512]{2,1,0:T(8,128)(2,1)S(1)} %slice.69), channel_id=1, source_target_pairs={{0,28},{4,0},{8,4},{12,8},{16,12},{20,16},{24,20},{28,24},{1,29},{... | collective-permute-start | bytes 98312 | tf_op jit(solution)/shard_map/ppermute | solution.py:808
  14.9 8.2 %collective-permute-done.1.refs_4_.refs_16_ = bf16[2,16,512]{2,1,0:T(8,128)(2,1)S(1)} collective-permute-done((bf16[2,16,512]{2,1,0:T(8,128)(2,1)S(1)}, bf16[2,16,512]{2,1,0:T(8,128)(2,1)S(1)}, u32[]{:S(2)}, u32[]{:S(2)}) %collective-permute-start.1) | collective-permute-done | bytes 32800 | tf_op jit(solution)/shard_map/ppermute | solution.py:808
  23.1 7.2 %collective-permute-done.refs_3_.refs_15_ = bf16[2,64,512]{2,1,0:T(8,128)(2,1)S(1)} collective-permute-done((bf16[2,64,512]{2,1,0:T(8,128)(2,1)S(1)}, bf16[2,64,512]{2,1,0:T(8,128)(2,1)S(1)}, u32[]{:S(2)}, u32[]{:S(2)}) %collective-permute-start) | collective-permute-done | bytes 131104 | tf_op jit(solution)/shard_map/ppermute | solution.py:808
  30.3 5.0 %all-to-all-start.1 = ((bf16[4,768,128]{2,1,0:T(8,128)(2,1)}), bf16[4,768,128]{2,1,0:T(8,128)(2,1)S(1)}, u32[]{:S(2)}, u32[]{:S(2)}) async-start(bf16[4,768,128]{2,1,0:T(8,128)(2,1)} %get-tuple-element.77), calls=%async_computation.1 | async-start | bytes 1572864 | tf_op jit(solution)/shard_map/all_to_all | solution.py:841
  35.3 1.5 collective-permute-start.2
  36.8 2.3 %collective-permute-start.3 = (bf16[4,768,128]{2,1,0:T(8,128)(2,1)S(1)}, bf16[4,768,128]{2,1,0:T(8,128)(2,1)}, u32[]{:S(2)}, u32[]{:S(2)}) collective-permute-start(bf16[4,768,128]{2,1,0:T(8,128)(2,1)S(1)} %all-to-all-done.refs_9_.refs_20_), channel_id=1, source_target_pairs={{0,4},{1,3},{2,6},{3,1},{4,0},{5,7},{6,2},{7,5},{8,12},{9,11},{10,... | collective-permute-start | bytes 2359304 | tf_op jit(solution)/shard_map/ppermute | solution.py:818
  39.1 16.5 %collective-permute-done.2.refs_10_.refs_21_ = bf16[4,768,128]{2,1,0:T(8,128)(2,1)S(1)} collective-permute-done((bf16[4,768,128]{2,1,0:T(8,128)(2,1)S(1)}, bf16[4,768,128]{2,1,0:T(8,128)(2,1)S(1)}, u32[]{:S(2)}, u32[]{:S(2)}) %collective-permute-start.2) | collective-permute-done | bytes 786464 | tf_op jit(solution)/shard_map/ppermute | solution.py:818
  55.6 1.5 collective-permute-start.4
  57.1 0.5 collective-permute-start.6
  57.6 10.0 %collective-permute-done.4.refs_12_.refs_23_ = bf16[4,768,128]{2,1,0:T(8,128)(2,1)S(1)} collective-permute-done((bf16[4,768,128]{2,1,0:T(8,128)(2,1)S(1)}, bf16[4,768,128]{2,1,0:T(8,128)(2,1)S(1)}, u32[]{:S(2)}, u32[]{:S(2)}) %collective-permute-start.4) | collective-permute-done | bytes 786464 | tf_op jit(solution)/shard_map/ppermute | solution.py:818
  67.6 1.5 collective-permute-start.12
  69.1 1.5 collective-permute-start.11
  70.6 9.8 %shard_map.170 = (bf16[416,512]{1,0:T(8,128)(2,1)S(1)}, bf16[416,1536]{1,0:T(8,128)(2,1)S(1)}, bf16[8,192,288]{2,1,0:T(8,128)(2,1)S(1)}, bf16[288,512]{1,0:T(8,1...) custom-call(s32[18]{0:T(128)S(1)} %stack.65.refs_0_, ...), custom_call_target="tpu_custom_call" | custom-call | flops 9663676416 | bytes 6291456 | tf_op jit(solution)/shard_map/pallas_call | solution.py:881
  80.4 0.8 collective-permute-start.9
  81.2 4.0 %collective-permute-start.10 = (bf16[2,16,512]{2,1,0:T(8,128)(2,1)S(1)}, bf16[2,16,512]{2,1,0:T(8,128)(2,1)S(1)}, u32[]{:S(2)}, u32[]{:S(2)}) collective-permute-start(bf16[2,16,512]{2,1,0:T(8,128)(2,1)S(1)} %get-tuple-element.81), channel_id=1, source_target_pairs={{0,28},{4,0},{8,4},{12,8},{16,12},{20,16},{24,20},{28,24},{1,29},{... | collective-permute-start | bytes 98312 | tf_op jit(solution)/shard_map/ppermute | solution.py:808
  85.2 4.2 %collective-permute-done.12.refs_14_ = bf16[4,768,128]{2,1,0:T(8,128)(2,1)S(1)} collective-permute-done((bf16[4,768,128]{2,1,0:T(8,128)(2,1)S(1)}, bf16[4,768,128]{2,1,0:T(8,128)(2,1)S(1)}, u32[]{:S(2)}, u32[]{:S(2)}) %collective-permute-start.12) | collective-permute-done | bytes 786464 | tf_op jit(solution)/shard_map/ppermute | solution.py:818
  89.4 0.7 collective-permute-done.10.refs_4_
  90.1 1.5 collective-permute-start.13
  92.3 9.8 %collective-permute-done.13.refs_15_ = bf16[4,768,128]{2,1,0:T(8,128)(2,1)S(1)} collective-permute-done((bf16[4,768,128]{2,1,0:T(8,128)(2,1)S(1)}, bf16[4,768,128]{2,1,0:T(8,128)(2,1)S(1)}, u32[]{:S(2)}, u32[]{:S(2)}) %collective-permute-start.13) | collective-permute-done | bytes 786464 | tf_op jit(solution)/shard_map/ppermute | solution.py:818
  102.1 2.3 collective-permute-done.17.refs_19_
  104.4 17.2 %shard_map.171 = (f32[2,128,512]{2,1,0:T(8,128)}, f32[256,512]{1,0:T(8,128)S(1)}, f32[256,512]{1,0:T(8,128)S(1)}, f32[16,512]{1,0:T(8,128)S(1)}, bf16[2,48,512]{...) custom-call(s32[18]{0:T(128)S(1)} %stack.65.refs_0_, ...), custom_call_target="tpu_custom_call" | custom-call | flops 24159191040 | bytes 12582912 | tf_op jit(solution)/shard_map/pallas_call | solution.py:881
  122.2 1.5 collective-permute-start.21
  123.7 3.2 %collective-permute-start.20 = (bf16[2,48,512]{2,1,0:T(8,128)(2,1)S(1)}, bf16[2,48,512]{2,1,0:T(8,128)(2,1)S(1)}, u32[]{:S(2)}, u32[]{:S(2)}) collective-permute-start(bf16[2,48,512]{2,1,0:T(8,128)(2,1)S(1)} %get-tuple-element.94), channel_id=1, source_target_pairs={{0,28},{4,0},{8,4},{12,8},{16,12},{20,16},{24,20},{28,24},{1,29},{... | collective-permute-start | bytes 294920 | tf_op jit(solution)/shard_map/ppermute | solution.py:808
  127.4 1.4 collective-permute-done.21.refs_6_
  128.8 0.4 collective-permute-done.20.refs_5_
  129.3 15.1 %shard_map.172 = (f32[256,512]{1,0:T(8,128)S(1)}, f32[256,512]{1,0:T(8,128)S(1)}, f32[16,512]{1,0:T(8,128)S(1)}, bf16[2,48,512]{2,1,0:T(8,128)(2,1)S(1)}, bf16[2...) custom-call(s32[18]{0:T(128)S(1)} %stack.65.refs_0_, ...), custom_call_target="tpu_custom_call" | custom-call | flops 22548578304 | bytes 12582912 | tf_op jit(solution)/shard_map/pallas_call | solution.py:881
  144.4 3.4 %collective-permute-done.22 = bf16[4,1536,128]{2,1,0:T(8,128)(2,1)S(1)} collective-permute-done((bf16[4,1536,128]{2,1,0:T(8,128)(2,1)S(1)}, bf16[4,1536,128]{2,1,0:T(8,128)(2,1)S(1)}, u32[]{:S(2)}, u32[]{:S(2)}) %collective-permute-start.22) | collective-permute-done | bytes 1572896 | tf_op jit(solution)/shard_map/ppermute | solution.py:818
  147.8 1.8 add_convert_fusion.1
  149.6 4.0 %collective-permute-done.23 = bf16[2,2,3168,128]{3,2,1,0:T(8,128)(2,1)S(1)} collective-permute-done((bf16[2,2,3168,128]{3,2,1,0:T(8,128)(2,1)S(1)}, bf16[2,2,3168,128]{3,2,1,0:T(8,128)(2,1)S(1)}, u32[]{:S(2)}, u32[]{:S(2)}) %collective-permute-start.23) | collective-permute-done | bytes 3244064 | tf_op jit(solution)/shard_map/ppermute | solution.py:818
  153.6 2.0 fusion
  156.2 4.7 %all-to-all-start.2 = ((bf16[4,1536,128]{2,1,0:T(8,128)(2,1)}), bf16[4,1536,128]{2,1,0:T(8,128)(2,1)S(1)}, u32[]{:S(2)}, u32[]{:S(2)}) async-start(bf16[4,1536,128]{2,1,0:T(8,128)(2,1)} %add_convert_fusion.1), calls=%async_computation.2 | async-start | bytes 3145728 | tf_op jit(solution)/shard_map/all_to_all | solution.py:841
  160.9 16.2 %collective-permute-done.24 = bf16[2,3168,128]{2,1,0:T(8,128)(2,1)} collective-permute-done((bf16[2,3168,128]{2,1,0:T(8,128)(2,1)}, bf16[2,3168,128]{2,1,0:T(8,128)(2,1)}, u32[]{:S(2)}, u32[]{:S(2)}) %collective-permute-start.24) | collective-permute-done | bytes 1622048 | tf_op jit(solution)/shard_map/ppermute | solution.py:818
  177.1 1.9 fusion.2
  179.1 2.1 collective-permute-start.25
  181.5 4.4 %collective-permute-start.26 = (bf16[2,48,512]{2,1,0:T(8,128)(2,1)S(1)}, bf16[2,48,512]{2,1,0:T(8,128)(2,1)S(1)}, u32[]{:S(2)}, u32[]{:S(2)}) collective-permute-start(bf16[2,48,512]{2,1,0:T(8,128)(2,1)S(1)} %get-tuple-element.115), channel_id=1, source_target_pairs={{0,28},{4,0},{8,4},{12,8},{16,12},{20,16},{24,20},{28,24},{1,29},{... | collective-permute-start | bytes 294920 | tf_op jit(solution)/shard_map/ppermute | solution.py:808
  185.9 5.5 %collective-permute-done.25 = bf16[3168,128]{1,0:T(8,128)(2,1)S(1)} collective-permute-done((bf16[3168,128]{1,0:T(8,128)(2,1)S(1)}, bf16[3168,128]{1,0:T(8,128)(2,1)S(1)}, u32[]{:S(2)}, u32[]{:S(2)}) %collective-permute-start.25) | collective-permute-done | bytes 811040 | tf_op jit(solution)/shard_map/ppermute | solution.py:818
  191.4 2.1 add_convert_fusion.3
  193.6 1.0 pad_maximum_fusion
  194.6 4.7 %all-to-all-done.2.refs_0_ = bf16[4,1536,128]{2,1,0:T(8,128)(2,1)S(1)} async-done(((bf16[4,1536,128]{2,1,0:T(8,128)(2,1)}), bf16[4,1536,128]{2,1,0:T(8,128)(2,1)S(1)}, u32[]{:S(2)}, u32[]{:S(2)}) %all-to-all-start.2) | async-done | bytes 1572896 | tf_op jit(solution)/shard_map/all_to_all | solution.py:841
  199.2 4.3 %all-to-all-start.3 = ((bf16[4,864,128]{2,1,0:T(8,128)(2,1)}), bf16[4,864,128]{2,1,0:T(8,128)(2,1)S(1)}, u32[]{:S(2)}, u32[]{:S(2)}) async-start(bf16[4,864,128]{2,1,0:T(8,128)(2,1)} %pad_maximum_fusion), calls=%async_computation.3 | async-start | bytes 1769472 | tf_op jit(solution)/shard_map/all_to_all | solution.py:841
  204.0 1.0 copy-done.3
  205.0 1.2 shard_map.173
  206.2 3.2 %collective-permute-done.28.refs_1_ = bf16[1,768,128]{2,1,0:T(8,128)(2,1)S(1)} collective-permute-done((bf16[1,768,128]{2,1,0:T(8,128)(2,1)S(1)}, bf16[1,768,128]{2,1,0:T(8,128)(2,1)S(1)}, u32[]{:S(2)}, u32[]{:S(2)}) %collective-permute-start.28) | collective-permute-done | bytes 196640 | tf_op jit(solution)/shard_map/ppermute | solution.py:818
  209.4 0.9 shard_map.174
  210.3 15.1 %all-to-all-done.3.refs_0_ = bf16[4,864,128]{2,1,0:T(8,128)(2,1)S(1)} async-done(((bf16[4,864,128]{2,1,0:T(8,128)(2,1)}), bf16[4,864,128]{2,1,0:T(8,128)(2,1)S(1)}, u32[]{:S(2)}, u32[]{:S(2)}) %all-to-all-start.3) | async-done | bytes 884768 | tf_op jit(solution)/shard_map/all_to_all | solution.py:841
  225.5 1.5 shard_map.175
  (68 shorter events, 3.7 us)
Async XLA Ops:
  0.6 9.0 %copy-start.1 = (bf16[2,1,128,512]{3,2,1,0:T(8,128)(2,1)S(1)}, bf16[2,1,128,512]{3,2,1,0:T(8,128)(2,1)}, u32[]{:S(2)}) copy-start(bf16[2,1,128,512]{3,2,1,0:T(8,128)(2,1)} %param.10) | copy-start | bytes 786436
  0.7 13.8 %copy-start.4 = (f32[2,6,512]{2,0,1:T(2,128)S(1)}, f32[2,6,512]{2,0,1:T(2,128)}, u32[]{:S(2)}) copy-start(f32[2,6,512]{2,0,1:T(2,128)} %param.18) | copy-start | bytes 73732
  0.7 13.9 %copy-start.11 = (s32[2,1,4]{2,1,0:T(1,128)S(1)}, s32[2,1,4]{2,1,0:T(1,128)}, u32[]{:S(2)}) copy-start(s32[2,1,4]{2,1,0:T(1,128)} %param.11) | copy-start | bytes 100
  3.1 67.5 %copy-start.5 = (f32[2,2,512]{2,1,0:T(2,128)S(1)}, f32[2,2,512]{2,1,0:T(2,128)}, u32[]{:S(2)}) copy-start(f32[2,2,512]{2,1,0:T(2,128)} %refs_6_.1) | copy-start | bytes 24580
  3.1 67.5 %copy-start.9 = (f32[2,2048]{1,0:T(2,128)S(1)}, f32[2,2048]{1,0:T(2,128)}, u32[]{:S(2)}) copy-start(f32[2,2048]{1,0:T(2,128)} %refs_10_.1) | copy-start | bytes 49156
  3.1 27.2 %all-to-all-start = ((bf16[4,768,128]{2,1,0:T(8,128)(2,1)}), bf16[4,768,128]{2,1,0:T(8,128)(2,1)S(1)}, u32[]{:S(2)}, u32[]{:S(2)}) async-start(bf16[4,768,128]{2,1,0:T(8,128)(2,1)} %get-tuple-element.71), calls=%async_computation | async-start | bytes 1572864 | tf_op jit(solution)/shard_map/all_to_all | solution.py:841
  9.6 13.5 %collective-permute-start.1 = (bf16[2,16,512]{2,1,0:T(8,128)(2,1)S(1)}, bf16[2,16,512]{2,1,0:T(8,128)(2,1)S(1)}, u32[]{:S(2)}, u32[]{:S(2)}) collective-permute-start(bf16[2,16,512]{2,1,0:T(8,128)(2,1)S(1)} %slice.69), channel_id=1, source_target_pairs={{0,28},{4,0},{8,4},{12,8},{16,12},{20,16},{24,20},{28,24},{1,29},{... | collective-permute-start | bytes 98312 | tf_op jit(solution)/shard_map/ppermute | solution.py:808
  14.4 15.9 %collective-permute-start = (bf16[2,64,512]{2,1,0:T(8,128)(2,1)S(1)}, bf16[2,64,512]{2,1,0:T(8,128)(2,1)S(1)}, u32[]{:S(2)}, u32[]{:S(2)}) collective-permute-start(bf16[2,64,512]{2,1,0:T(8,128)(2,1)S(1)} %slice.68), channel_id=1, source_target_pairs={{0,4},{4,8},{8,12},{12,16},{16,20},{20,24},{24,28},{28,0},{1,5},{5... | collective-permute-start | bytes 393224 | tf_op jit(solution)/shard_map/ppermute | solution.py:808
  30.3 50.1 %copy-start.7 = (bf16[2,64,512]{2,1,0:T(8,128)(2,1)}, bf16[2,64,512]{2,1,0:T(8,128)(2,1)S(1)}, u32[]{:S(2)}) copy-start(bf16[2,64,512]{2,1,0:T(8,128)(2,1)S(1)} %collective-permute-done.refs_3_.refs_15_) | copy-start | bytes 393220
  30.3 25.3 %all-to-all-start.1 = ((bf16[4,768,128]{2,1,0:T(8,128)(2,1)}), bf16[4,768,128]{2,1,0:T(8,128)(2,1)S(1)}, u32[]{:S(2)}, u32[]{:S(2)}) async-start(bf16[4,768,128]{2,1,0:T(8,128)(2,1)} %get-tuple-element.77), calls=%async_computation.1 | async-start | bytes 1572864 | tf_op jit(solution)/shard_map/all_to_all | solution.py:841
  35.3 20.3 %collective-permute-start.2 = (bf16[4,768,128]{2,1,0:T(8,128)(2,1)S(1)}, bf16[4,768,128]{2,1,0:T(8,128)(2,1)S(1)}, u32[]{:S(2)}, u32[]{:S(2)}) collective-permute-start(bf16[4,768,128]{2,1,0:T(8,128)(2,1)S(1)} %all-to-all-done.refs_9_.refs_20_), channel_id=1, source_target_pairs={{0,2},{1,5},{2,0},{3,7},{4,6},{5,1},{6,4},{7,3},{8,10},{9,13},{10,... | collective-permute-start | bytes 2359304 | tf_op jit(solution)/shard_map/ppermute | solution.py:818
  36.8 20.8 %collective-permute-start.3 = (bf16[4,768,128]{2,1,0:T(8,128)(2,1)S(1)}, bf16[4,768,128]{2,1,0:T(8,128)(2,1)}, u32[]{:S(2)}, u32[]{:S(2)}) collective-permute-start(bf16[4,768,128]{2,1,0:T(8,128)(2,1)S(1)} %all-to-all-done.refs_9_.refs_20_), channel_id=1, source_target_pairs={{0,4},{1,3},{2,6},{3,1},{4,0},{5,7},{6,2},{7,5},{8,12},{9,11},{10,... | collective-permute-start | bytes 2359304 | tf_op jit(solution)/shard_map/ppermute | solution.py:818
  55.6 12.0 %collective-permute-start.4 = (bf16[4,768,128]{2,1,0:T(8,128)(2,1)S(1)}, bf16[4,768,128]{2,1,0:T(8,128)(2,1)S(1)}, u32[]{:S(2)}, u32[]{:S(2)}) collective-permute-start(bf16[4,768,128]{2,1,0:T(8,128)(2,1)S(1)} %collective-permute-done.2.refs_10_.refs_21_), channel_id=1, source_target_pairs={{0,4},{1,3},{2,6},{3,1},{4,0},{5,7},{6,2},{7,5},{8,12},{9,11},{10,... | collective-permute-start | bytes 2359304 | tf_op jit(solution)/shard_map/ppermute | solution.py:818
  57.1 12.0 %collective-permute-start.5 = (bf16[4,768,128]{2,1,0:T(8,128)(2,1)S(1)}, bf16[4,768,128]{2,1,0:T(8,128)(2,1)S(1)}, u32[]{:S(2)}, u32[]{:S(2)}) collective-permute-start(bf16[4,768,128]{2,1,0:T(8,128)(2,1)S(1)} %all-to-all-done.refs_9_.refs_20_), channel_id=1, source_target_pairs={{0,1},{1,0},{2,3},{3,2},{4,5},{5,4},{6,7},{7,6},{8,9},{9,8},{10,11... | collective-permute-start | bytes 2359304 | tf_op jit(solution)/shard_map/ppermute | solution.py:818
  57.1 13.5 %collective-permute-start.6 = (bf16[4,768,128]{2,1,0:T(8,128)(2,1)S(1)}, bf16[4,768,128]{2,1,0:T(8,128)(2,1)S(1)}, u32[]{:S(2)}, u32[]{:S(2)}) collective-permute-start(bf16[4,768,128]{2,1,0:T(8,128)(2,1)S(1)} %collective-permute-done.2.refs_10_.refs_21_), channel_id=1, source_target_pairs={{0,1},{1,0},{2,3},{3,2},{4,5},{5,4},{6,7},{7,6},{8,9},{9,8},{10,11... | collective-permute-start | bytes 2359304 | tf_op jit(solution)/shard_map/ppermute | solution.py:818
  57.6 13.0 %collective-permute-start.7 = (bf16[4,768,128]{2,1,0:T(8,128)(2,1)}, bf16[4,768,128]{2,1,0:T(8,128)(2,1)S(1)}, u32[]{:S(2)}, u32[]{:S(2)}) collective-permute-start(bf16[4,768,128]{2,1,0:T(8,128)(2,1)} %collective-permute-done.3.refs_11_.refs_22_), channel_id=1, source_target_pairs={{0,1},{1,0},{2,3},{3,2},{4,5},{5,4},{6,7},{7,6},{8,9},{9,8},{10,11... | collective-permute-start | bytes 2359304 | tf_op jit(solution)/shard_map/ppermute | solution.py:818
  67.6 3.0 %collective-permute-start.8 = (bf16[4,768,128]{2,1,0:T(8,128)(2,1)S(1)}, bf16[4,768,128]{2,1,0:T(8,128)(2,1)S(1)}, u32[]{:S(2)}, u32[]{:S(2)}) collective-permute-start(bf16[4,768,128]{2,1,0:T(8,128)(2,1)S(1)} %collective-permute-done.4.refs_12_.refs_23_), channel_id=1, source_target_pairs={{0,1},{1,0},{2,3},{3,2},{4,5},{5,4},{6,7},{7,6},{8,9},{9,8},{10,11... | collective-permute-start | bytes 2359304 | tf_op jit(solution)/shard_map/ppermute | solution.py:818
  67.6 21.8 %collective-permute-start.12 = (bf16[4,768,128]{2,1,0:T(8,128)(2,1)S(1)}, bf16[4,768,128]{2,1,0:T(8,128)(2,1)S(1)}, u32[]{:S(2)}, u32[]{:S(2)}) collective-permute-start(bf16[4,768,128]{2,1,0:T(8,128)(2,1)S(1)} %all-to-all-done.1.refs_12_), channel_id=1, source_target_pairs={{0,4},{1,3},{2,6},{3,1},{4,0},{5,7},{6,2},{7,5},{8,12},{9,11},{10,... | collective-permute-start | bytes 2359304 | tf_op jit(solution)/shard_map/ppermute | solution.py:818
  69.1 20.3 %collective-permute-start.11 = (bf16[4,768,128]{2,1,0:T(8,128)(2,1)S(1)}, bf16[4,768,128]{2,1,0:T(8,128)(2,1)S(1)}, u32[]{:S(2)}, u32[]{:S(2)}) collective-permute-start(bf16[4,768,128]{2,1,0:T(8,128)(2,1)S(1)} %all-to-all-done.1.refs_12_), channel_id=1, source_target_pairs={{0,2},{1,5},{2,0},{3,7},{4,6},{5,1},{6,4},{7,3},{8,10},{9,13},{10,... | collective-permute-start | bytes 2359304 | tf_op jit(solution)/shard_map/ppermute | solution.py:818
  70.6 33.8 %copy-start.6 = (bf16[2,1,128,512]{3,2,1,0:T(8,128)(2,1)S(1)}, bf16[2,1,128,512]{3,2,1,0:T(8,128)(2,1)}, u32[]{:S(2)}) copy-start(bf16[2,1,128,512]{3,2,1,0:T(8,128)(2,1)} %param.12) | copy-start | bytes 786436
  80.4 9.7 %collective-permute-start.9 = (bf16[2,48,512]{2,1,0:T(8,128)(2,1)S(1)}, bf16[2,48,512]{2,1,0:T(8,128)(2,1)S(1)}, u32[]{:S(2)}, u32[]{:S(2)}) collective-permute-start(bf16[2,48,512]{2,1,0:T(8,128)(2,1)S(1)} %get-tuple-element.80), channel_id=1, source_target_pairs={{0,4},{4,8},{8,12},{12,16},{16,20},{20,24},{24,28},{28,0},{1,5},{5... | collective-permute-start | bytes 294920 | tf_op jit(solution)/shard_map/ppermute | solution.py:808
  81.2 8.9 %collective-permute-start.10 = (bf16[2,16,512]{2,1,0:T(8,128)(2,1)S(1)}, bf16[2,16,512]{2,1,0:T(8,128)(2,1)S(1)}, u32[]{:S(2)}, u32[]{:S(2)}) collective-permute-start(bf16[2,16,512]{2,1,0:T(8,128)(2,1)S(1)} %get-tuple-element.81), channel_id=1, source_target_pairs={{0,28},{4,0},{8,4},{12,8},{16,12},{20,16},{24,20},{28,24},{1,29},{... | collective-permute-start | bytes 98312 | tf_op jit(solution)/shard_map/ppermute | solution.py:808
  90.1 12.0 %collective-permute-start.13 = (bf16[4,768,128]{2,1,0:T(8,128)(2,1)S(1)}, bf16[4,768,128]{2,1,0:T(8,128)(2,1)S(1)}, u32[]{:S(2)}, u32[]{:S(2)}) collective-permute-start(bf16[4,768,128]{2,1,0:T(8,128)(2,1)S(1)} %collective-permute-done.11.refs_13_), channel_id=1, source_target_pairs={{0,4},{1,3},{2,6},{3,1},{4,0},{5,7},{6,2},{7,5},{8,12},{9,11},{10,... | collective-permute-start | bytes 2359304 | tf_op jit(solution)/shard_map/ppermute | solution.py:818
  91.6 10.5 %collective-permute-start.14 = (bf16[4,768,128]{2,1,0:T(8,128)(2,1)S(1)}, bf16[4,768,128]{2,1,0:T(8,128)(2,1)S(1)}, u32[]{:S(2)}, u32[]{:S(2)}) collective-permute-start(bf16[4,768,128]{2,1,0:T(8,128)(2,1)S(1)} %all-to-all-done.1.refs_12_), channel_id=1, source_target_pairs={{0,1},{1,0},{2,3},{3,2},{4,5},{5,4},{6,7},{7,6},{8,9},{9,8},{10,11... | collective-permute-start | bytes 2359304 | tf_op jit(solution)/shard_map/ppermute | solution.py:818
  91.8 10.4 %collective-permute-start.16 = (bf16[4,768,128]{2,1,0:T(8,128)(2,1)S(1)}, bf16[4,768,128]{2,1,0:T(8,128)(2,1)S(1)}, u32[]{:S(2)}, u32[]{:S(2)}) collective-permute-start(bf16[4,768,128]{2,1,0:T(8,128)(2,1)S(1)} %collective-permute-done.12.refs_14_), channel_id=1, source_target_pairs={{0,1},{1,0},{2,3},{3,2},{4,5},{5,4},{6,7},{7,6},{8,9},{9,8},{10,11... | collective-permute-start | bytes 2359304 | tf_op jit(solution)/shard_map/ppermute | solution.py:818
  92.1 10.0 %collective-permute-start.15 = (bf16[4,768,128]{2,1,0:T(8,128)(2,1)S(1)}, bf16[4,768,128]{2,1,0:T(8,128)(2,1)S(1)}, u32[]{:S(2)}, u32[]{:S(2)}) collective-permute-start(bf16[4,768,128]{2,1,0:T(8,128)(2,1)S(1)} %collective-permute-done.11.refs_13_), channel_id=1, source_target_pairs={{0,1},{1,0},{2,3},{3,2},{4,5},{5,4},{6,7},{7,6},{8,9},{9,8},{10,11... | collective-permute-start | bytes 2359304 | tf_op jit(solution)/shard_map/ppermute | solution.py:818
  102.1 2.3 %collective-permute-start.17 = (bf16[4,768,128]{2,1,0:T(8,128)(2,1)S(1)}, bf16[4,768,128]{2,1,0:T(8,128)(2,1)S(1)}, u32[]{:S(2)}, u32[]{:S(2)}) collective-permute-start(bf16[4,768,128]{2,1,0:T(8,128)(2,1)S(1)} %collective-permute-done.13.refs_15_), channel_id=1, source_target_pairs={{0,1},{1,0},{2,3},{3,2},{4,5},{5,4},{6,7},{7,6},{8,9},{9,8},{10,11... | collective-permute-start | bytes 2359304 | tf_op jit(solution)/shard_map/ppermute | solution.py:818
  121.6 5.3 %collective-permute-start.18 = (bf16[4,1536,128]{2,1,0:T(8,128)(2,1)S(1)}, bf16[4,1536,128]{2,1,0:T(8,128)(2,1)S(1)}, u32[]{:S(2)}, u32[]{:S(2)}) collective-permute-start(bf16[4,1536,128]{2,1,0:T(8,128)(2,1)S(1)} %get-tuple-element.90), channel_id=1, source_target_pairs={{0,1},{1,0},{2,3},{3,2},{4,5},{5,4},{6,7},{7,6},{8,9},{9,8},{10,11... | collective-permute-start | bytes 4718600 | tf_op jit(solution)/shard_map/ppermute | solution.py:818
  121.8 5.6 %collective-permute-start.19 = (bf16[4,1536,128]{2,1,0:T(8,128)(2,1)S(1)}, bf16[4,1536,128]{2,1,0:T(8,128)(2,1)S(1)}, u32[]{:S(2)}, u32[]{:S(2)}) collective-permute-start(bf16[4,1536,128]{2,1,0:T(8,128)(2,1)S(1)} %get-tuple-element.91), channel_id=1, source_target_pairs={{0,1},{1,0},{2,3},{3,2},{4,5},{5,4},{6,7},{7,6},{8,9},{9,8},{10,11... | collective-permute-start | bytes 4718600 | tf_op jit(solution)/shard_map/ppermute | solution.py:818
  122.2 6.7 %collective-permute-start.21 = (bf16[2,16,512]{2,1,0:T(8,128)(2,1)S(1)}, bf16[2,16,512]{2,1,0:T(8,128)(2,1)S(1)}, u32[]{:S(2)}, u32[]{:S(2)}) collective-permute-start(bf16[2,16,512]{2,1,0:T(8,128)(2,1)S(1)} %get-tuple-element.95), channel_id=1, source_target_pairs={{0,4},{4,8},{8,12},{12,16},{16,20},{20,24},{24,28},{28,0},{1,5},{5... | collective-permute-start | bytes 98312 | tf_op jit(solution)/shard_map/ppermute | solution.py:808
  123.7 5.6 %collective-permute-start.20 = (bf16[2,48,512]{2,1,0:T(8,128)(2,1)S(1)}, bf16[2,48,512]{2,1,0:T(8,128)(2,1)S(1)}, u32[]{:S(2)}, u32[]{:S(2)}) collective-permute-start(bf16[2,48,512]{2,1,0:T(8,128)(2,1)S(1)} %get-tuple-element.94), channel_id=1, source_target_pairs={{0,28},{4,0},{8,4},{12,8},{16,12},{20,16},{24,20},{28,24},{1,29},{... | collective-permute-start | bytes 294920 | tf_op jit(solution)/shard_map/ppermute | solution.py:808
  126.9 2.4 %copy-start.8 = (bf16[2,64,512]{2,1,0:T(8,128)(2,1)S(1)}, bf16[2,64,512]{2,1,0:T(8,128)(2,1)}, u32[]{:S(2)}) copy-start(bf16[2,64,512]{2,1,0:T(8,128)(2,1)} %copy-done.7) | copy-start | bytes 393220
  127.3 20.5 %collective-permute-start.22 = (bf16[4,1536,128]{2,1,0:T(8,128)(2,1)S(1)}, bf16[4,1536,128]{2,1,0:T(8,128)(2,1)S(1)}, u32[]{:S(2)}, u32[]{:S(2)}) collective-permute-start(bf16[4,1536,128]{2,1,0:T(8,128)(2,1)S(1)} %add_convert_fusion.2), channel_id=1, source_target_pairs={{0,4},{1,3},{2,6},{3,1},{4,0},{5,7},{6,2},{7,5},{8,12},{9,11},{10,... | collective-permute-start | bytes 4718600 | tf_op jit(solution)/shard_map/ppermute | solution.py:818
  144.4 5.2 %copy-start.2 = (f32[256,512]{1,0:T(8,128)}, f32[256,512]{1,0:T(8,128)S(1)}, u32[]{:S(2)}) copy-start(f32[256,512]{1,0:T(8,128)S(1)} %get-tuple-element.113.refs_2_) | copy-start | bytes 1572868
  144.4 9.2 %copy-start = (bf16[2,2,3168,128]{3,2,1,0:T(8,128)(2,1)}, bf16[2,2,3168,128]{3,2,1,0:T(8,128)(2,1)S(1)}, u32[]{:S(2)}) copy-start(bf16[2,2,3168,128]{3,2,1,0:T(8,128)(2,1)S(1)} %get-tuple-element.105) | copy-start | bytes 9732100
  147.8 5.8 %collective-permute-start.23 = (bf16[2,2,3168,128]{3,2,1,0:T(8,128)(2,1)S(1)}, bf16[2,2,3168,128]{3,2,1,0:T(8,128)(2,1)S(1)}, u32[]{:S(2)}, u32[]{:S(2)}) collective-permute-start(bf16[2,2,3168,128]{3,2,1,0:T(8,128)(2,1)S(1)} %get-tuple-element.107), channel_id=1, source_target_pairs={{0,1},{1,0},{2,3},{3,2},{4,5},{5,4},{6,7},{7,6},{8,9},{9,8},{10,11... | collective-permute-start | bytes 9732104 | tf_op jit(solution)/shard_map/ppermute | solution.py:818
  153.6 2.3 %copy-start.10 = (bf16[2,2,3168,128]{3,2,1,0:T(8,128)(2,1)}, bf16[2,2,3168,128]{3,2,1,0:T(8,128)(2,1)S(1)}, u32[]{:S(2)}) copy-start(bf16[2,2,3168,128]{3,2,1,0:T(8,128)(2,1)S(1)} %collective-permute-done.23) | copy-start | bytes 9732100
  155.9 21.3 %collective-permute-start.24 = (bf16[2,3168,128]{2,1,0:T(8,128)(2,1)}, bf16[2,3168,128]{2,1,0:T(8,128)(2,1)}, u32[]{:S(2)}, u32[]{:S(2)}) collective-permute-start(bf16[2,3168,128]{2,1,0:T(8,128)(2,1)} %fusion), channel_id=1, source_target_pairs={{0,4},{1,3},{2,6},{3,1},{4,0},{5,7},{6,2},{7,5},{8,12},{9,11},{10,... | collective-permute-start | bytes 4866056 | tf_op jit(solution)/shard_map/ppermute | solution.py:818
  156.2 43.1 %all-to-all-start.2 = ((bf16[4,1536,128]{2,1,0:T(8,128)(2,1)}), bf16[4,1536,128]{2,1,0:T(8,128)(2,1)S(1)}, u32[]{:S(2)}, u32[]{:S(2)}) async-start(bf16[4,1536,128]{2,1,0:T(8,128)(2,1)} %add_convert_fusion.1), calls=%async_computation.2 | async-start | bytes 3145728 | tf_op jit(solution)/shard_map/all_to_all | solution.py:841
  179.1 12.3 %collective-permute-start.25 = (bf16[3168,128]{1,0:T(8,128)(2,1)S(1)}, bf16[3168,128]{1,0:T(8,128)(2,1)S(1)}, u32[]{:S(2)}, u32[]{:S(2)}) collective-permute-start(bf16[3168,128]{1,0:T(8,128)(2,1)S(1)} %fusion.2), channel_id=1, source_target_pairs={{0,2},{1,5},{2,0},{3,7},{4,6},{5,1},{6,4},{7,3},{8,10},{9,13},{10,... | collective-permute-start | bytes 2433032 | tf_op jit(solution)/shard_map/ppermute | solution.py:818
  181.2 13.4 %collective-permute-start.27 = (bf16[2,16,512]{2,1,0:T(8,128)(2,1)S(1)}, bf16[2,16,512]{2,1,0:T(8,128)(2,1)S(1)}, u32[]{:S(2)}, u32[]{:S(2)}) collective-permute-start(bf16[2,16,512]{2,1,0:T(8,128)(2,1)S(1)} %get-tuple-element.116), channel_id=1, source_target_pairs={{0,4},{4,8},{8,12},{12,16},{16,20},{20,24},{24,28},{28,0},{1,5},{5... | collective-permute-start | bytes 98312 | tf_op jit(solution)/shard_map/ppermute | solution.py:808
  181.5 13.0 %collective-permute-start.26 = (bf16[2,48,512]{2,1,0:T(8,128)(2,1)S(1)}, bf16[2,48,512]{2,1,0:T(8,128)(2,1)S(1)}, u32[]{:S(2)}, u32[]{:S(2)}) collective-permute-start(bf16[2,48,512]{2,1,0:T(8,128)(2,1)S(1)} %get-tuple-element.115), channel_id=1, source_target_pairs={{0,28},{4,0},{8,4},{12,8},{16,12},{20,16},{24,20},{28,24},{1,29},{... | collective-permute-start | bytes 294920 | tf_op jit(solution)/shard_map/ppermute | solution.py:808
  199.2 26.2 %all-to-all-start.3 = ((bf16[4,864,128]{2,1,0:T(8,128)(2,1)}), bf16[4,864,128]{2,1,0:T(8,128)(2,1)S(1)}, u32[]{:S(2)}, u32[]{:S(2)}) async-start(bf16[4,864,128]{2,1,0:T(8,128)(2,1)} %pad_maximum_fusion), calls=%async_computation.3 | async-start | bytes 1769472 | tf_op jit(solution)/shard_map/all_to_all | solution.py:841
  203.6 5.7 %collective-permute-start.28 = (bf16[1,768,128]{2,1,0:T(8,128)(2,1)S(1)}, bf16[1,768,128]{2,1,0:T(8,128)(2,1)S(1)}, u32[]{:S(2)}, u32[]{:S(2)}) collective-permute-start(bf16[1,768,128]{2,1,0:T(8,128)(2,1)S(1)} %bitcast.72), channel_id=1, source_target_pairs={{0,2},{1,5},{2,0},{3,7},{4,6},{5,1},{6,4},{7,3},{8,10},{9,13},{10,... | collective-permute-start | bytes 589832 | tf_op jit(solution)/shard_map/ppermute | solution.py:818
  204.0 1.0 copy-start.3
